TPU v7x, 32 devices: a whole 2x2x4 slice. The times are simulated.
32 devices in a mesh: mesh: 4 (over y, x), mode: 8 (over z, core).
Axes of the slice: x: 2, y: 2, z: 4, core: 2. Of those that a mesh axis runs over, the one named last changes fastest.
Arguments:
- magnetic: float32 [2, 6, 64, 8192], P(None, None, 'mode', 'mesh'), may hold values from -6 to 6
- velocity: float32 [3, 128, 8192], P(None, None, ('mesh', 'mode')), may hold values from -3 to 3
- stiffness: float32 [6, 6, 4096], P(None, None, 'mesh')
- mass_r: float32 [6, 6, 4096], P(None, None, 'mesh')
- coupling: float32 [6, 6, 4096], P(None, None, 'mesh'), may hold values from -3 to 3
- inv_mass: float32 [8192], P('mesh'), may hold values from 0.5 to 2
- connect: int32 [6, 4096], P(None, 'mesh'), may hold values from 0 to 2559, as said below
- interface: int32 [4, 512], P('mesh'), may hold values from 0 to 2047, as said below
- counts: int32 [4, 2], P('mesh'), may hold values from 0 to 256, as said below
- elem_live: int32 [4], P('mesh'), may hold values from 128 to 1024
Outputs:
- advanced: float32 [2, 6, 64, 8192], P(None, None, 'mode', 'mesh')
Inputs may be any that keep to these rules, and one draw needn't show every extreme that they name: `connect`: entries below 2048 are the partition's own nodes; 2048 + s appears only for s < counts[q - 1, 1] and 2304 + s only for s < counts[q + 1, 0]. `interface`: each row holds distinct node indices of its partition; the first counts[q, 0] are shared with partition q - 1, the next counts[q, 1] with partition q + 1. counts[0, 0] = 0 and counts[3, 1] = 0.
All inputs are finite; a program needn't handle non-finite values.
Results may differ from a plain program's by a relative error of at most 0.00005.
Values sent between devices are 32-bit elements; how exact they have to be, the bound alone decides.
No kernel may reach another device: no remote copies, remote signals or barrier semaphores. Data moves between devices by JAX's collectives and lax.ppermute only.
A program may use at most 320 MiB of HBM per device.

v0:
```python
import math

import jax
import jax.numpy as jnp
from jax import lax
from jax.sharding import PartitionSpec as P

diffusivity = 1.0
time_step = 0.1
highest = lax.Precision.HIGHEST


def extended_2(cells, sides, width):
    for axis, dim in sides:
        count = lax.axis_size(axis)
        ends = count - 1
        head = lax.slice_in_dim(cells, 0, width, axis=dim)
        tail = lax.slice_in_dim(cells, cells.shape[dim] - width, cells.shape[dim], axis=dim)
        cells = jnp.concatenate(
            [
                lax.ppermute(tail, axis, [(i, (i + 1) % count) for i in range(ends)]),
                cells,
                lax.ppermute(head, axis, [((i + 1) % count, i) for i in range(ends)]),
            ],
            axis=dim,
        )
    return cells


def transform_tables(spectral_modes):
    samples = 2 * spectral_modes
    sample_ids = jnp.arange(samples)[:, None]
    mode_ids = jnp.arange(spectral_modes)[None, :]
    phases = 2.0 * math.pi / samples * (sample_ids * mode_ids % samples).astype(jnp.float32)
    cosines = jnp.cos(phases)
    sines = jnp.sin(phases)
    inverse_fourier = jnp.concatenate([cosines, sines], 1)
    weights = jnp.where(mode_ids == 0, 1.0, 2.0).astype(jnp.float32) / samples
    forward_fourier = jnp.concatenate([(cosines * weights).T, (sines * (2.0 / samples)).T], 0)
    return (inverse_fourier, forward_fourier)


def electric_spectral(split_into_slabs, velocity, inverse_fourier, forward_fourier):
    group_members, vector_parts, spectral_modes, slab_width = split_into_slabs.shape
    mode_coefficient_values = split_into_slabs.reshape(
        group_members, 3, 2 * spectral_modes, slab_width
    )
    points = jnp.einsum(
        "pc,ficn->fipn", inverse_fourier, mode_coefficient_values, precision=highest
    )
    vel_r, vel_t, vel_z = (velocity[0], velocity[1], velocity[2])
    mag_r, mag_t, mag_z = (points[:, 0], points[:, 1], points[:, 2])
    cross = jnp.stack(
        [
            vel_t * mag_z - vel_z * mag_t,
            vel_z * mag_r - vel_r * mag_z,
            vel_r * mag_t - vel_t * mag_r,
        ],
        1,
    )
    back = jnp.einsum("cp,fipn->ficn", forward_fourier, cross, precision=highest)
    return back.reshape(group_members, vector_parts, spectral_modes, slab_width)


def element_terms(mag_ext, ele_ext, connect, stiffness, mass_r, coupling, mode_ids, live):
    squares = (mode_ids.astype(jnp.float32) ** 2)[:, None, None, None]
    operator = stiffness[None] + squares * mass_r[None]
    terms = jnp.zeros(mag_ext.shape[:3] + connect.shape, jnp.float32)
    for corner in range(6):
        mag_col = jnp.take(mag_ext, connect[corner], axis=3)[:, :, :, None, :]
        ele_col = jnp.take(ele_ext, connect[corner], axis=3)[:, :, :, None, :]
        terms = terms + coupling[:, corner, :][None, None, None] * ele_col
        terms = terms - diffusivity * (operator[:, :, corner, :][None, None] * mag_col)
    return jnp.where(live, terms, 0.0)


def on_device(
    magnetic, velocity, stiffness, mass_r, coupling, inv_mass, connect, interface, counts, elem_live
):
    group_members, vector_parts, mode_dev, node_dev = magnetic.shape
    ghost_cap = interface.shape[1] // 2
    slot_ids = jnp.arange(ghost_cap)
    left_count = counts[0, 0]
    right_count = counts[0, 1]
    left_nodes = interface[0, :ghost_cap]
    right_nodes = lax.dynamic_slice_in_dim(interface[0], left_count, ghost_cap)
    left_keep = slot_ids < left_count
    right_keep = slot_ids < right_count
    inverse_fourier, forward_fourier = transform_tables(mode_dev * lax.axis_size("mode"))
    pieces = []
    for member in range(group_members):
        split_into_slabs = lax.all_to_all(
            magnetic[member : member + 1], "mode", split_axis=3, concat_axis=2, tiled=True
        )
        pieces.append(
            lax.all_to_all(
                electric_spectral(split_into_slabs, velocity, inverse_fourier, forward_fourier),
                "mode",
                split_axis=2,
                concat_axis=3,
                tiled=True,
            )
        )
    electric = jnp.concatenate(pieces, 0)
    values = jnp.concatenate([magnetic, electric], 1)
    to_left = jnp.where(left_keep, jnp.take(values, left_nodes, axis=3), 0.0)
    to_right = jnp.where(right_keep, jnp.take(values, right_nodes, axis=3), 0.0)
    extended = extended_2(jnp.concatenate([to_left, to_right], 3), (("mesh", 3),), ghost_cap)
    joined = jnp.concatenate([extended[..., :ghost_cap], extended[..., 3 * ghost_cap :]], 3)
    mag_ghosts = joined[:, :vector_parts]
    ele_ghosts = joined[:, vector_parts:]
    mag_ext = jnp.concatenate([magnetic, mag_ghosts], 3)
    ele_ext = jnp.concatenate([electric, ele_ghosts], 3)
    mode_ids = lax.axis_index("mode") * mode_dev + jnp.arange(mode_dev)
    live = jnp.arange(connect.shape[1]) < elem_live[0]
    terms = element_terms(mag_ext, ele_ext, connect, stiffness, mass_r, coupling, mode_ids, live)
    partial_sums = jnp.zeros(mag_ext.shape, jnp.float32).at[:, :, :, connect].add(terms)
    returned = extended_2(partial_sums[..., node_dev:], (("mesh", 3),), ghost_cap)
    own_sums = partial_sums[..., :node_dev]
    own_sums = own_sums.at[..., left_nodes].add(
        jnp.where(left_keep, returned[..., :ghost_cap], 0.0)
    )
    own_sums = own_sums.at[..., right_nodes].add(
        jnp.where(right_keep, returned[..., 3 * ghost_cap :], 0.0)
    )
    return magnetic + time_step * inv_mass * own_sums


def solution(mesh):
    return jax.shard_map(
        on_device,
        mesh=mesh,
        in_specs=(
            P(None, None, "mode", "mesh"),
            P(None, None, ("mesh", "mode")),
            P(None, None, "mesh"),
            P(None, None, "mesh"),
            P(None, None, "mesh"),
            P("mesh"),
            P(None, "mesh"),
            P("mesh", None),
            P("mesh", None),
            P("mesh"),
        ),
        out_specs=P(None, None, "mode", "mesh"),
        check_vma=False,
    )
```

profile of v0, /device:TPU:0, one launch (start us, length us, event | category | flops | bytes accessed | tf_op | source)
XLA Modules:
  0.0 1577.2 jit_solution(10423552469041543884)
XLA Ops:
  39.9 12.6 multiply_add_fusion
  61.0 7.0 reshape.328
  102.2 13.5 slice_bitcast_fusion.5
  115.9 9.1 copy.171
  125.0 7.9 gather_fusion
  141.1 8.0 gather_fusion.1
  164.1 13.5 copy.175
  177.7 13.6 copy.178
  191.2 22.3 %gather_fusion.2 = f32[1024,2,6,8]{3,1,2,0:T(2,128)} fusion(f32[2,6,8,2560]{2,0,3,1:T(2,128)} %copy.175, s32[1024]{0:T(1024)S(1)} %get-tuple-element.60), kind=kCustom, calls=%fused_computation.1.clone | custom fusion | bytes 790528 | tf_op jit(solution)/shard_map/jit(_take)/gather | solution.py:71
  213.5 22.1 %gather_fusion.3 = f32[1024,2,6,8]{3,1,2,0:T(2,128)} fusion(f32[2,6,8,2560]{2,0,3,1:T(2,128)} %copy.178, s32[1024]{0:T(1024)S(1)} %get-tuple-element.60), kind=kCustom, calls=%fused_computation.3.clone | custom fusion | bytes 790528 | tf_op jit(solution)/shard_map/jit(_take)/gather | solution.py:70
  235.7 22.3 %gather_fusion.4 = f32[1024,2,6,8]{3,1,2,0:T(2,128)} fusion(f32[2,6,8,2560]{2,0,3,1:T(2,128)} %copy.175, s32[1024]{0:T(1024)S(1)} %get-tuple-element.61), kind=kCustom, calls=%fused_computation.4.clone | custom fusion | bytes 790528 | tf_op jit(solution)/shard_map/jit(_take)/gather | solution.py:71
  258.0 22.3 %gather_fusion.5 = f32[1024,2,6,8]{3,1,2,0:T(2,128)} fusion(f32[2,6,8,2560]{2,0,3,1:T(2,128)} %copy.178, s32[1024]{0:T(1024)S(1)} %get-tuple-element.61), kind=kCustom, calls=%fused_computation.5.clone | custom fusion | bytes 790528 | tf_op jit(solution)/shard_map/jit(_take)/gather | solution.py:70
  280.3 22.2 %gather_fusion.6 = f32[1024,2,6,8]{3,1,2,0:T(2,128)} fusion(f32[2,6,8,2560]{2,0,3,1:T(2,128)} %copy.175, s32[1024]{0:T(1024)S(1)} %get-tuple-element.62), kind=kCustom, calls=%fused_computation.6.clone | custom fusion | bytes 790528 | tf_op jit(solution)/shard_map/jit(_take)/gather | solution.py:71
  302.5 22.2 %gather_fusion.7 = f32[1024,2,6,8]{3,1,2,0:T(2,128)} fusion(f32[2,6,8,2560]{2,0,3,1:T(2,128)} %copy.178, s32[1024]{0:T(1024)S(1)} %get-tuple-element.62), kind=kCustom, calls=%fused_computation.7.clone | custom fusion | bytes 790528 | tf_op jit(solution)/shard_map/jit(_take)/gather | solution.py:70
  324.8 22.2 %gather_fusion.8 = f32[1024,2,6,8]{3,1,2,0:T(2,128)} fusion(f32[2,6,8,2560]{2,0,3,1:T(2,128)} %copy.175, s32[1024]{0:T(1024)S(1)} %get-tuple-element.63), kind=kCustom, calls=%fused_computation.8.clone | custom fusion | bytes 790528 | tf_op jit(solution)/shard_map/jit(_take)/gather | solution.py:71
  346.9 22.3 %gather_fusion.9 = f32[1024,2,6,8]{3,1,2,0:T(2,128)} fusion(f32[2,6,8,2560]{2,0,3,1:T(2,128)} %copy.178, s32[1024]{0:T(1024)S(1)} %get-tuple-element.63), kind=kCustom, calls=%fused_computation.9.clone | custom fusion | bytes 790528 | tf_op jit(solution)/shard_map/jit(_take)/gather | solution.py:70
  369.2 22.2 %gather_fusion.10 = f32[1024,2,6,8]{3,1,2,0:T(2,128)} fusion(f32[2,6,8,2560]{2,0,3,1:T(2,128)} %copy.175, s32[1024]{0:T(1024)S(1)} %get-tuple-element.64), kind=kCustom, calls=%fused_computation.10.clone | custom fusion | bytes 790528 | tf_op jit(solution)/shard_map/jit(_take)/gather | solution.py:71
  391.4 22.4 %gather_fusion.11 = f32[1024,2,6,8]{3,1,2,0:T(2,128)} fusion(f32[2,6,8,2560]{2,0,3,1:T(2,128)} %copy.178, s32[1024]{0:T(1024)S(1)} %get-tuple-element.64), kind=kCustom, calls=%fused_computation.11.clone | custom fusion | bytes 790528 | tf_op jit(solution)/shard_map/jit(_take)/gather | solution.py:70
  413.8 22.2 %gather_fusion.12 = f32[1024,2,6,8]{3,1,2,0:T(2,128)} fusion(f32[2,6,8,2560]{2,0,3,1:T(2,128)} %copy.175, s32[1024]{0:T(1024)S(1)} %get-tuple-element.65), kind=kCustom, calls=%fused_computation.12.clone | custom fusion | bytes 790528 | tf_op jit(solution)/shard_map/jit(_take)/gather | solution.py:71
  436.0 22.2 %gather_fusion.13 = f32[1024,2,6,8]{3,1,2,0:T(2,128)} fusion(f32[2,6,8,2560]{2,0,3,1:T(2,128)} %copy.178, s32[1024]{0:T(1024)S(1)} %get-tuple-element.65), kind=kCustom, calls=%fused_computation.13.clone | custom fusion | bytes 790528 | tf_op jit(solution)/shard_map/jit(_take)/gather | solution.py:70
  458.2 14.4 select_bitcast_fusion.11
  472.7 14.4 select_bitcast_fusion.9
  487.2 9.1 select_bitcast_fusion.7
  496.4 9.2 select_bitcast_fusion.5
  505.7 9.2 select_bitcast_fusion.3
  515.0 9.4 select_bitcast_fusion.1
  524.4 151.0 %subtract_select_fusion = f32[2,6,8,6,1024]{2,0,1,4,3:T(2,128)} fusion(pred[1024]{0:T(1024)(128)(4,1)S(1)} %iota_compare_fusion, f32[2,6,8,1024]{2,0,1,3:T(2,128)} %get-tuple-element.51, f32[8,6,1024]{0,2,1:T(8,128)} %get-tuple-element.10, f32[2,6,8,1024]{2,0,1,3:T(2,128)} %get-tuple-element.50, f32[6,1024]{1,0:T(8,128)S(1)} %get-tuple-element.70, ...), kind=kLoop, calls=%fused_computation.17 | loop fusion | flops 14155776 | bytes 8406016 | tf_op jit(solution)/shard_map/jit(_where)/select_n | solution.py:74
  681.3 785.2 %scatter_fusion = f32[2,6,8,2560]{2,0,3,1:T(2,128)} fusion(f32[2,6,8,2560]{2,0,3,1:T(2,128)} %broadcast_in_dim.84, s32[6144]{0:T(1024)S(1)} %reshape.257, f32[6144,2,6,8]{3,1,2,0:T(2,128)} %bitcast.185), kind=kCustom, calls=%fused_computation.14 | custom fusion | flops 589824 | bytes 7102464 | tf_op jit(solution)/shard_map/scatter-add | solution.py:117
  1475.9 10.2 slice.202
  1495.3 31.0 %scatter_fusion.1 = f32[2,6,8,2048]{2,0,3,1:T(2,128)} fusion(f32[2,6,8,2048]{2,0,3,1:T(2,128)} %slice.202, s32[256]{0:T(256)S(1)} %bitcast.231, f32[256,2,6,8]{3,1,2,0:T(2,128)S(1)} %copy.195), kind=kCustom, calls=%fused_computation.15 | custom fusion | flops 24576 | bytes 295936 | tf_op jit(solution)/shard_map/scatter-add | solution.py:120
  1526.4 34.3 %scatter_fusion.2 = f32[2,6,8,2048]{2,0,3,1:T(2,128)} fusion(f32[2,6,8,2048]{2,0,3,1:T(2,128)} %scatter_fusion.1, s32[256]{0:T(256)S(1)} %bitcast.230, f32[256,2,6,8]{3,1,2,0:T(2,128)} %copy.197), kind=kCustom, calls=%fused_computation.16 | custom fusion | flops 24576 | bytes 295936 | tf_op jit(solution)/shard_map/scatter-add | solution.py:123
  1560.7 15.1 copy.198
  (180 shorter events, 128.5 us)
Async XLA Ops:
  5.8 12.7 copy-start.11
  11.9 40.6 %all-to-all-start = ((f32[8,1,12288]{2,1,0:T(1,128)}), f32[8,1,12288]{2,1,0:T(1,128)S(1)}, u32[]{:S(2)}, u32[]{:S(2)}) async-start(f32[8,1,12288]{2,1,0:T(1,128)} %reshape.327), calls=%async_computation | async-start | bytes 786432 | tf_op jit(solution)/shard_map/all_to_all | solution.py:92
  26.8 9.6 copy-start.10
  26.8 9.7 copy-start.3
  26.9 9.8 copy-start.4
  52.5 22.7 %all-to-all-start.2 = ((f32[8,1,12288]{2,1,0:T(1,128)}), f32[8,1,12288]{2,1,0:T(1,128)S(1)}, u32[]{:S(2)}, u32[]{:S(2)}) async-start(f32[8,1,12288]{2,1,0:T(1,128)} %reshape.325), calls=%async_computation.2 | async-start | bytes 786432 | tf_op jit(solution)/shard_map/all_to_all | solution.py:92
  75.2 21.9 %all-to-all-start.1 = ((f32[1,6,64,256]{3,0,1,2:T(1,128)}), f32[1,6,64,256]{3,0,1,2:T(1,128)S(1)}, u32[]{:S(2)}, u32[]{:S(2)}) async-start(f32[1,6,64,256]{3,0,1,2:T(1,128)} %copy.165), calls=%async_computation.1 | async-start | bytes 786432 | tf_op jit(solution)/shard_map/all_to_all | solution.py:96
  81.4 51.5 %copy-start.14 = (pred[256]{0:T(512)(128)(4,1)}, pred[256]{0:T(512)(128)(4,1)S(1)}, u32[]{:S(2)}) copy-start(pred[256]{0:T(512)(128)(4,1)S(1)} %get-tuple-element.67) | copy-start | bytes 772
  97.1 18.6 %all-to-all-start.3 = ((f32[1,6,64,256]{3,0,1,2:T(1,128)}), f32[1,6,64,256]{3,0,1,2:T(1,128)S(1)}, u32[]{:S(2)}, u32[]{:S(2)}) async-start(f32[1,6,64,256]{3,0,1,2:T(1,128)} %copy.169), calls=%async_computation.3 | async-start | bytes 786432 | tf_op jit(solution)/shard_map/all_to_all | solution.py:96
  102.2 13.6 copy-start
  137.1 18.3 %collective-permute-start = (f32[2,12,8,256]{3,2,1,0:T(8,128)S(1)}, f32[2,12,8,256]{3,2,1,0:T(8,128)}, u32[]{:S(2)}, u32[]{:S(2)}) collective-permute-start(f32[2,12,8,256]{3,2,1,0:T(8,128)S(1)} %copy.172), channel_id=1, source_target_pairs={{0,8},{8,16},{16,24},{1,9},{9,17},{17,25},{2,10},{10,18},{18,26},{... | collective-permute-start | bytes 589832 | tf_op jit(solution)/shard_map/ppermute | solution.py:21
  153.9 9.1 collective-permute-start.1
  191.2 267.0 %copy-start.22 = (pred[1024]{0:T(1024)(128)(4,1)S(1)}, pred[1024]{0:T(1024)(128)(4,1)}, u32[]{:S(2)}) copy-start(pred[1024]{0:T(1024)(128)(4,1)} %compare_and_fusion.5) | copy-start | bytes 3076
  458.2 14.4 copy-start.21
  458.2 28.9 %slice-start.12 = ((s8[6291456]{0:T(1024)(128)(4,1)}), s8[4194304]{0:T(1024)(128)(4,1)S(1)}, s32[]{:S(2)}) async-start(s8[6291456]{0:T(1024)(128)(4,1)} %bitcast.202), calls=%async_computation.16 | async-start | bytes 8388608
  458.2 28.9 %slice-start.14 = ((s8[6291456]{0:T(1024)(128)(4,1)}), s8[4194304]{0:T(1024)(128)(4,1)S(1)}, s32[]{:S(2)}) async-start(s8[6291456]{0:T(1024)(128)(4,1)} %bitcast.204), calls=%async_computation.18 | async-start | bytes 8388608
  472.6 14.5 slice-start.13
  472.6 14.5 slice-start.15
  472.7 14.5 copy-start.20
  472.7 23.7 %slice-start.8 = ((s8[6291456]{0:T(1024)(128)(4,1)}), s8[4194304]{0:T(1024)(128)(4,1)S(1)}, s32[]{:S(2)}) async-start(s8[6291456]{0:T(1024)(128)(4,1)} %bitcast.198), calls=%async_computation.12 | async-start | bytes 8388608
  472.7 23.7 %slice-start.10 = ((s8[6291456]{0:T(1024)(128)(4,1)}), s8[4194304]{0:T(1024)(128)(4,1)S(1)}, s32[]{:S(2)}) async-start(s8[6291456]{0:T(1024)(128)(4,1)} %bitcast.200), calls=%async_computation.14 | async-start | bytes 8388608
  487.2 18.4 %slice-start.4 = ((s8[6291456]{0:T(1024)(128)(4,1)}), s8[4194304]{0:T(1024)(128)(4,1)S(1)}, s32[]{:S(2)}) async-start(s8[6291456]{0:T(1024)(128)(4,1)} %bitcast.194), calls=%async_computation.8 | async-start | bytes 8388608
  487.2 18.4 %slice-start.6 = ((s8[6291456]{0:T(1024)(128)(4,1)}), s8[4194304]{0:T(1024)(128)(4,1)S(1)}, s32[]{:S(2)}) async-start(s8[6291456]{0:T(1024)(128)(4,1)} %bitcast.196), calls=%async_computation.10 | async-start | bytes 8388608
  496.4 18.5 %slice-start = ((s8[6291456]{0:T(1024)(128)(4,1)}), s8[4194304]{0:T(1024)(128)(4,1)S(1)}, s32[]{:S(2)}) async-start(s8[6291456]{0:T(1024)(128)(4,1)} %bitcast.190), calls=%async_computation.4 | async-start | bytes 8388608
  496.4 18.5 %slice-start.2 = ((s8[6291456]{0:T(1024)(128)(4,1)}), s8[4194304]{0:T(1024)(128)(4,1)S(1)}, s32[]{:S(2)}) async-start(s8[6291456]{0:T(1024)(128)(4,1)} %bitcast.192), calls=%async_computation.6 | async-start | bytes 8388608
  514.9 9.4 copy-start.5
  1472.1 15.8 %collective-permute-start.2 = (f32[2,6,8,256]{3,2,1,0:T(8,128)S(1)}, f32[2,6,8,256]{3,2,1,0:T(8,128)S(1)}, u32[]{:S(2)}, u32[]{:S(2)}) collective-permute-start(f32[2,6,8,256]{3,2,1,0:T(8,128)S(1)} %copy.194), channel_id=1, source_target_pairs={{0,8},{8,16},{16,24},{1,9},{9,17},{17,25},{2,10},{10,18},{18,26},{... | collective-permute-start | bytes 294920 | tf_op jit(solution)/shard_map/ppermute | solution.py:21
  1475.8 12.2 copy-start.13
  1475.8 17.4 %copy-start.15 = (pred[256]{0:T(512)(128)(4,1)S(1)}, pred[256]{0:T(512)(128)(4,1)}, u32[]{:S(2)}) copy-start(pred[256]{0:T(512)(128)(4,1)} %copy-done.14) | copy-start | bytes 772
  1475.9 19.5 %copy-start.24 = (s32[256,1]{0,1:T(1,128)S(1)}, s32[256,1]{0,1:T(1,128)}, u32[]{:S(2)}) copy-start(s32[256,1]{0,1:T(1,128)} %get-tuple-element.39) | copy-start | bytes 3076
  1475.9 50.5 %copy-start.23 = (s32[256,1]{0,1:T(1,128)S(1)}, s32[256,1]{0,1:T(1,128)}, u32[]{:S(2)}) copy-start(s32[256,1]{0,1:T(1,128)} %get-tuple-element.6) | copy-start | bytes 3076
  1486.7 6.5 collective-permute-start.3
  (18 other events, 159.0 us)
where the time goes:
time: 1600 us; the launch traced here: 1580 us
  other arithmetic  1100 us (69%)
  local copies, waits for them, and re-layouts  429 us (27%)
  starting transfers between devices  32.6 us (2%)
    scatter-add x1, other arithmetic, on_device(): jnp.zeros(mag_ext.shape, jnp.float32).at[:, :, :, connect].add(terms)  785 us
    select_n x1, other arithmetic, element_terms(): return jnp.where(live, terms, 0.0)  151 us
    gather x6, local copies, waits for them, and re-layouts, element_terms(): mag_col = jnp.take(mag_ext, connect[corner], axis=3)[:, :, :, None, :]  134 us
    gather x6, local copies, waits for them, and re-layouts, element_terms(): ele_col = jnp.take(ele_ext, connect[corner], axis=3)[:, :, :, None, :]  133 us
    select_n x6, other arithmetic, element_terms(): ele_col = jnp.take(ele_ext, connect[corner], axis=3)[:, :, :, None, :]  65.7 us
    scatter-add x1, other arithmetic, on_device(): own_sums.at[..., right_nodes]  34.3 us
  transfers between devices with their start and end apart: 8, of which 2 were waited for; matrix products, arithmetic and copies ran while one was open for 7% of the time, Pallas kernels for 0%

commit v1 on v0

v1 whole, which is shorter than its diff:
```python
import functools
import math

import jax
import jax.numpy as jnp
from jax import lax
from jax.experimental import pallas as pl
from jax.experimental.pallas import tpu as pltpu
from jax.sharding import PartitionSpec as P

diffusivity = 1.0
time_step = 0.1
f32 = jnp.float32
bf16 = jnp.bfloat16
KERNEL_VMEM = 30 << 20
ELEM_TILE = 256


def whole_block(shape):
    return pl.BlockSpec(shape, lambda *ids: (0,) * len(shape))


def params():
    return pltpu.CompilerParams(vmem_limit_bytes=KERNEL_VMEM)


def cost(us):
    return pl.CostEstimate(flops=0, bytes_accessed=int(us * 3.0e6), transcendentals=0)


def split_rows(value):
    high = value.astype(bf16)
    low = (value - high.astype(f32)).astype(bf16)
    return jnp.concatenate([high, low], 0)


def halves_sum(value):
    rows = value.shape[0] // 2
    return value[:rows] + value[rows:]


def one_hot(iota, ids):
    return jnp.where(iota == ids, 1.0, 0.0).astype(bf16)


def transform_tables(mode_dev, members, me):
    spectral_modes = mode_dev * members
    samples = 2 * spectral_modes
    row = jnp.arange(samples)
    step = row // (2 * mode_dev)
    parity = (row // mode_dev) % 2
    mode = (me ^ step) * mode_dev + row % mode_dev
    sample_ids = jnp.arange(samples)
    phases = (2.0 * math.pi / samples) * ((sample_ids[:, None] * mode[None, :]) % samples).astype(f32)
    inverse = jnp.where(parity[None, :] == 0, jnp.cos(phases), jnp.sin(phases))
    weights = jnp.where((mode == 0) & (parity == 0), 1.0, 2.0).astype(f32) / samples
    forward = (inverse * weights[None, :]).T
    return inverse, forward


def spread_table(table):
    high = table.astype(bf16)
    low = (table - high.astype(f32)).astype(bf16)
    return jnp.concatenate([high, high, low], 1)


def spread_value(value):
    high = value.astype(bf16)
    low = (value - high.astype(f32)).astype(bf16)
    return jnp.concatenate([high, low, high], 0)


def transform_kernel(members, mode_dev, fields, *refs):
    inverse, forward, velocity = refs[:3]
    blocks = refs[3 : 3 + members]
    outs = refs[3 + members :]
    pair = 2 * mode_dev
    to_points, to_modes = spread_table(inverse[...]), spread_table(forward[...])
    for field in range(fields):
        points = []
        for part in range(3):
            low = (field * 3 + part) * pair
            stacked = jnp.concatenate([block[low : low + pair, :] for block in blocks], 0)
            points.append(
                jnp.dot(to_points, spread_value(stacked), preferred_element_type=f32)
            )
        for part in range(3):
            after, last = (part + 1) % 3, (part + 2) % 3
            cross = velocity[after] * points[last] - velocity[last] * points[after]
            back = jnp.dot(to_modes, spread_value(cross), preferred_element_type=f32)
            low = (field * 3 + part) * pair
            for step in range(members):
                outs[step][low : low + pair, :] = back[step * pair : (step + 1) * pair]


def transform(blocks, velocity, inverse, forward, mode_dev, fields):
    members = len(blocks)
    return pl.pallas_call(
        functools.partial(transform_kernel, members, mode_dev, fields),
        out_shape=[jax.ShapeDtypeStruct(block.shape, f32) for block in blocks],
        compiler_params=params(),
        cost_estimate=cost(3),
        name="transform",
    )(inverse, forward, velocity, *blocks)


def interface_kernel(count, bases, ids, *refs):
    blocks = refs[:count]
    left, right, hot = refs[count:]
    width = ids.shape[1]
    row = 0
    stacked = []
    for at, block in enumerate(blocks):
        size = block.shape[1]
        iota = lax.broadcasted_iota(jnp.int32, (size, width), 0)
        hot[row : row + size, :] = one_hot(iota, ids[...] - bases[at])
        stacked.append(split_rows(block[...]))
        row += size
    values = jnp.concatenate(stacked, 1)
    got = halves_sum(jnp.dot(values, hot[...], preferred_element_type=f32))
    left[...] = got[:, : width // 2]
    right[...] = got[:, width // 2 :]


def interface_values(blocks, bases, ids, us):
    rows = blocks[0].shape[0]
    total = sum(block.shape[1] for block in blocks)
    cap = ids.shape[1] // 2
    vmem = pl.BlockSpec(memory_space=pltpu.VMEM)
    return pl.pallas_call(
        functools.partial(interface_kernel, len(blocks)),
        in_specs=[pl.BlockSpec(memory_space=pltpu.SMEM), vmem] + [vmem] * len(blocks),
        out_shape=[jax.ShapeDtypeStruct((rows, cap), f32)] * 2,
        scratch_shapes=[pltpu.VMEM((total, 2 * cap), bf16)],
        compiler_params=params(),
        cost_estimate=cost(us),
        name="interface_values",
    )(bases, ids, *blocks)


def fill_gather(hot, conn, blocks, bases, tile):
    row = 0
    for at, block in enumerate(blocks):
        size = block.shape[1]
        iota = lax.broadcasted_iota(jnp.int32, (size, tile), 0)
        for corner in range(6):
            hot[row : row + size, corner * tile : (corner + 1) * tile] = one_hot(
                iota, conn[corner : corner + 1, :] - bases[at]
            )
        row += size


def fill_values(values, blocks):
    column = 0
    for block in blocks:
        size = block.shape[1]
        values[:, column : column + size] = split_rows(block[...])
        column += size


def magnetic_terms_kernel(count, bases, conn, stiffness, mass_r, squares, *refs):
    blocks = refs[:count]
    out, values, hot, operator = refs[count:]
    tile = conn.shape[1]

    @pl.when(pl.program_id(0) == 0)
    def _():
        fill_values(values, blocks)

    fill_gather(hot, conn, blocks, bases, tile)
    got = halves_sum(jnp.dot(values[...], hot[...], preferred_element_type=f32))
    for a in range(6):
        for b in range(6):
            operator[a * 6 + b] = diffusivity * (
                stiffness[a, b : b + 1, :] + squares[...] * mass_r[a, b : b + 1, :]
            )
    for low in range(0, out.shape[0], 8):
        for a in range(6):
            total = None
            for b in range(6):
                term = operator[a * 6 + b] * got[low : low + 8, b * tile : (b + 1) * tile]
                total = term if total is None else total + term
            out[low : low + 8, a * tile : (a + 1) * tile] = total


def magnetic_terms(blocks, bases, conn, stiffness, mass_r, squares):
    rows = blocks[0].shape[0]
    elems = conn.shape[1]
    tile = ELEM_TILE
    total = sum(block.shape[1] for block in blocks)
    elem_block = pl.BlockSpec((6, 6, tile), lambda j: (0, 0, j))
    return pl.pallas_call(
        functools.partial(magnetic_terms_kernel, len(blocks)),
        grid=(elems // tile,),
        in_specs=[
            pl.BlockSpec(memory_space=pltpu.SMEM),
            pl.BlockSpec((6, tile), lambda j: (0, j)),
            elem_block,
            elem_block,
            whole_block((8, 1)),
        ]
        + [whole_block(block.shape) for block in blocks],
        out_specs=pl.BlockSpec((rows, 6 * tile), lambda j: (0, j)),
        out_shape=jax.ShapeDtypeStruct((rows, 6 * elems), f32),
        scratch_shapes=[
            pltpu.VMEM((2 * rows, total), bf16),
            pltpu.VMEM((total, 6 * tile), bf16),
            pltpu.VMEM((36, 8, tile), f32),
        ],
        compiler_params=params(),
        cost_estimate=cost(14),
        name="magnetic_terms",
    )(bases, conn, stiffness, mass_r, squares, *blocks)


def gather_kernel(count, adds, bases, conn, *refs):
    blocks = refs[:count]
    refs = refs[count:]
    if adds:
        earlier, refs = refs[0], refs[1:]
    out, values, hot = refs
    tile = conn.shape[1]

    @pl.when(pl.program_id(0) == 0)
    def _():
        fill_values(values, blocks)

    fill_gather(hot, conn, blocks, bases, tile)
    got = halves_sum(jnp.dot(values[...], hot[...], preferred_element_type=f32))
    out[...] = got + earlier[...] if adds else got


def gathered(blocks, bases, conn, earlier, us):
    rows = blocks[0].shape[0]
    elems = conn.shape[1]
    tile = ELEM_TILE
    total = sum(block.shape[1] for block in blocks)
    wide = pl.BlockSpec((rows, 6 * tile), lambda j: (0, j))
    adds = earlier is not None
    return pl.pallas_call(
        functools.partial(gather_kernel, len(blocks), adds),
        grid=(elems // tile,),
        in_specs=[
            pl.BlockSpec(memory_space=pltpu.SMEM),
            pl.BlockSpec((6, tile), lambda j: (0, j)),
        ]
        + [whole_block(block.shape) for block in blocks]
        + [wide] * adds,
        out_specs=wide,
        out_shape=jax.ShapeDtypeStruct((rows, 6 * elems), f32),
        scratch_shapes=[
            pltpu.VMEM((2 * rows, total), bf16),
            pltpu.VMEM((total, 6 * tile), bf16),
        ],
        compiler_params=params(),
        cost_estimate=cost(us),
        name="gathered",
    )(bases, conn, *blocks, *([earlier] * adds))


def fill_scatter(hot, conn_columns, first, tile):
    iota = lax.broadcasted_iota(jnp.int32, (tile, hot.shape[1]), 1)
    for corner in range(6):
        hot[corner * tile : (corner + 1) * tile, :] = one_hot(
            iota, conn_columns[:, corner : corner + 1] - first
        )


def ghost_terms_kernel(
    first, conn, conn_columns, coupling, magnetic_part, electric_part, left, right,
    terms, sums, values, hot, hot_columns, total_sums
):
    step = pl.program_id(0)
    tile = conn.shape[1]
    cap = left.shape[1]

    @pl.when(step == 0)
    def _():
        fill_values(values, (left, right))
        total_sums[...] = jnp.zeros_like(total_sums)

    fill_gather(hot, conn, (left, right), (first, first + cap), tile)
    got = electric_part[...] + halves_sum(
        jnp.dot(values[...], hot[...], preferred_element_type=f32)
    )
    rows = got.shape[0]
    for low in range(0, rows, 16):
        for a in range(6):
            at = slice(a * tile, (a + 1) * tile)
            total = -magnetic_part[low : low + 16, at]
            for b in range(6):
                total = total + coupling[a, b : b + 1, :] * got[low : low + 16, b * tile : (b + 1) * tile]
            high = total.astype(bf16)
            terms[low : low + 16, at] = high
            terms[rows + low : rows + low + 16, at] = (total - high.astype(f32)).astype(bf16)
    fill_scatter(hot_columns, conn_columns, first, tile)
    total_sums[...] += halves_sum(
        jnp.dot(terms[...], hot_columns[...], preferred_element_type=f32)
    )

    @pl.when(step == pl.num_programs(0) - 1)
    def _():
        sums[0] = total_sums[:, :cap]
        sums[1] = total_sums[:, cap:]


def ghost_terms(first, conn, conn_columns, coupling, magnetic_part, electric_part, left, right):
    rows, cap = left.shape
    elems = conn.shape[1]
    tile = ELEM_TILE
    wide = pl.BlockSpec((rows, 6 * tile), lambda j: (0, j))
    return pl.pallas_call(
        functools.partial(ghost_terms_kernel, first),
        grid=(elems // tile,),
        in_specs=[
            pl.BlockSpec((6, tile), lambda j: (0, j)),
            pl.BlockSpec((tile, 6), lambda j: (j, 0)),
            pl.BlockSpec((6, 6, tile), lambda j: (0, 0, j)),
            wide,
            wide,
            whole_block((rows, cap)),
            whole_block((rows, cap)),
        ],
        out_specs=[
            pl.BlockSpec((2 * rows, 6 * tile), lambda j: (0, j)),
            whole_block((2, rows, cap)),
        ],
        out_shape=[
            jax.ShapeDtypeStruct((2 * rows, 6 * elems), bf16),
            jax.ShapeDtypeStruct((2, rows, cap), f32),
        ],
        scratch_shapes=[
            pltpu.VMEM((2 * rows, 2 * cap), bf16),
            pltpu.VMEM((2 * cap, 6 * tile), bf16),
            pltpu.VMEM((6 * tile, 2 * cap), bf16),
            pltpu.VMEM((rows, 2 * cap), f32),
        ],
        compiler_params=params(),
        cost_estimate=cost(8),
        name="ghost_terms",
    )(conn, conn_columns, coupling, magnetic_part, electric_part, left, right)


def own_sums_kernel(conn_columns, terms, out, hot):
    @pl.when(pl.program_id(0) == 0)
    def _():
        out[...] = jnp.zeros_like(out)

    fill_scatter(hot, conn_columns, 0, conn_columns.shape[0])
    out[...] += halves_sum(jnp.dot(terms[...], hot[...], preferred_element_type=f32))


def own_sums(conn_columns, terms, nodes):
    rows = terms.shape[0] // 2
    tile = ELEM_TILE
    elems = conn_columns.shape[0]
    return pl.pallas_call(
        own_sums_kernel,
        grid=(elems // tile,),
        in_specs=[
            pl.BlockSpec((tile, 6), lambda j: (j, 0)),
            pl.BlockSpec((2 * rows, 6 * tile), lambda j: (0, j)),
        ],
        out_specs=whole_block((rows, nodes)),
        out_shape=jax.ShapeDtypeStruct((rows, nodes), f32),
        scratch_shapes=[pltpu.VMEM((6 * tile, nodes), bf16)],
        compiler_params=params(),
        cost_estimate=cost(9),
        name="own_sums",
    )(conn_columns, terms)


def finish_kernel(columns, magnetic, sums, left, right, inv_mass, out):
    width = columns.shape[0]
    nodes = out.shape[1]
    iota = lax.broadcasted_iota(jnp.int32, (width, nodes), 1)
    hot = one_hot(iota, columns[...])
    values = jnp.concatenate([split_rows(left[...]), split_rows(right[...])], 1)
    extra = halves_sum(jnp.dot(values, hot, preferred_element_type=f32))
    out[...] = magnetic[...] + time_step * inv_mass[...] * (sums[...] + extra)


def finish(columns, magnetic, sums, left, right, inv_mass):
    return pl.pallas_call(
        finish_kernel,
        out_shape=jax.ShapeDtypeStruct(magnetic.shape, f32),
        compiler_params=params(),
        cost_estimate=cost(3),
        name="finish",
    )(columns, magnetic, sums, left, right, inv_mass)


def exchange(blocks):
    members = len(blocks)
    return [blocks[0]] + [
        lax.ppermute(blocks[s], "mode", [(k, k ^ s) for k in range(members)])
        for s in range(1, members)
    ]


def neighbours(to_left, to_right):
    count = lax.axis_size("mesh")
    from_left = lax.ppermute(to_right, "mesh", [(i, i + 1) for i in range(count - 1)])
    from_right = lax.ppermute(to_left, "mesh", [(i + 1, i) for i in range(count - 1)])
    return from_left, from_right


def on_device(
    magnetic, velocity, stiffness, mass_r, coupling, inv_mass, connect, interface, counts, elem_live
):
    fields, vector_parts, mode_dev, node_dev = magnetic.shape
    rows = fields * vector_parts * mode_dev
    cap = interface.shape[1] // 2
    elems = connect.shape[1]
    members = lax.axis_size("mode")
    me = lax.axis_index("mode")
    slab = node_dev // members
    values = magnetic.reshape(rows, node_dev)

    slabs = [
        lax.dynamic_slice_in_dim(values, (me ^ s) * slab, slab, axis=1) for s in range(members)
    ]
    arrived = exchange(slabs)

    right_nodes = lax.dynamic_slice_in_dim(interface[0], counts[0, 0], cap)
    nodes = jnp.concatenate([interface[0, :cap], right_nodes])
    node_row = nodes[None, :]
    node_column = nodes[:, None]
    live = jnp.arange(elems) < elem_live[0]
    conn = jnp.where(live, connect, -1)
    conn_columns = conn.T
    mode_ids = me * mode_dev + jnp.arange(8) % mode_dev
    squares = (mode_ids.astype(f32) ** 2)[:, None]

    zero = jnp.zeros((1,), jnp.int32)
    mag_left, mag_right = neighbours(*interface_values([values], zero, node_row, 3))
    ghost_bases = jnp.array([0, node_dev, node_dev + cap], jnp.int32)
    magnetic_part = magnetic_terms(
        [values, mag_left, mag_right], ghost_bases, conn, stiffness, mass_r, squares
    )

    inverse, forward = transform_tables(mode_dev, members, me)
    electric = exchange(transform(arrived, velocity, inverse, forward, mode_dev, fields))
    bases = (me ^ jnp.arange(members, dtype=jnp.int32)) * slab
    near = members // 2
    electric_part = gathered(electric[:near], bases[:near], conn, None, 6)
    ele_left, ele_right = neighbours(*interface_values(electric, bases, node_row, 3))
    electric_part = gathered(electric[near:], bases[near:], conn, electric_part, 6)
    terms, ghost_sums = ghost_terms(
        node_dev, conn, conn_columns, coupling, magnetic_part, electric_part, ele_left, ele_right
    )
    sum_left, sum_right = neighbours(ghost_sums[0], ghost_sums[1])
    sums = own_sums(conn_columns, terms, node_dev)
    out = finish(node_column, values, sums, sum_left, sum_right, inv_mass[None, :])
    return out.reshape(magnetic.shape)


def solution(mesh):
    return jax.shard_map(
        on_device,
        mesh=mesh,
        in_specs=(
            P(None, None, "mode", "mesh"),
            P(None, None, ("mesh", "mode")),
            P(None, None, "mesh"),
            P(None, None, "mesh"),
            P(None, None, "mesh"),
            P("mesh"),
            P(None, "mesh"),
            P("mesh", None),
            P("mesh", None),
            P("mesh"),
        ),
        out_specs=P(None, None, "mode", "mesh"),
        check_vma=False,
    )
```

time: 1600 us -> 96.2 us (0.06)
  the two profiles are of different devices: /device:TPU:0 before, /device:TPU:12 now
where the time goes in v1:
time: 96.2 us; the launch traced here: 95.8 us
  starting transfers between devices  38 us (40%)
  Pallas kernels  32.9 us (34%)
  waiting for transfers between devices  14.1 us (15%)
  local copies, waits for them, and re-layouts  7.79 us (8%)
  other arithmetic  1.85 us (2%)
  between operations  1.17 us (1%)
    ppermute x14, starting transfers between devices, exchange(): lax.ppermute(blocks[s], 'mode', [(k, k ^ s) for k in range(members)])  17.8 us
    ppermute x14, waiting for transfers between devices, exchange(): lax.ppermute(blocks[s], 'mode', [(k, k ^ s) for k in range(members)])  14.1 us
    ppermute x3, starting transfers between devices, neighbours(): lax.ppermute(to_left, 'mesh', [(i + 1, i) for i in range(count - 1)])  12.4 us
    pallas_call x1, Pallas kernels, magnetic_terms(): pl.pallas_call(functools.partial(magnetic_terms_kernel, len(blocks)), gri...  8.58 us
    pallas_call x2, Pallas kernels, gathered(): pl.pallas_call(functools.partial(gather_kernel, len(blocks), adds), grid=...  8.24 us
    ppermute x3, starting transfers between devices, neighbours(): lax.ppermute(to_right, 'mesh', [(i, i + 1) for i in range(count - 1)])  7.79 us
    pallas_call x1, Pallas kernels, own_sums(): pl.pallas_call(own_sums_kernel, grid=(elems // tile,), in_specs=[pl.Block...  6.17 us
    pallas_call x1, Pallas kernels, ghost_terms(): pl.pallas_call(functools.partial(ghost_terms_kernel, first), grid=(elems...  5.58 us
  transfers between devices with their start and end apart: 20, of which 6 were waited for; matrix products, arithmetic and copies ran while one was open for 5% of the time, Pallas kernels for 26%

profile of v1, /device:TPU:12, one launch (start us, length us, event | category | flops | bytes accessed | tf_op | source)
XLA Modules:
  0.0 95.8 jit_solution(16625119829545415574)
XLA Ops:
  0.1 2.1 %constant_dynamic-slice_fusion = (f32[96,256]{1,0:T(8,128)S(1)}, f32[96,256]{1,0:T(8,128)S(1)}, f32[96,256]{1,0:T(8,128)S(1)}, f32[96,256]{1,0:T(8,128)}, f32[96...) fusion(f32[96,2048]{1,0:T(8,128)} %bitcast.17, s32[]{:T(128)S(6)} %select_n.141, ...), kind=kLoop, calls=%fused_computation.32 | loop fusion | bytes 1572896 | tf_op jit(solution)/shard_map/dynamic_slice | solution.py:421
  2.6 1.4 %collective-permute-start.4 = (f32[96,256]{1,0:T(8,128)}, f32[96,256]{1,0:T(8,128)S(1)}, u32[]{:S(2)}, u32[]{:S(2)}) collective-permute-start(f32[96,256]{1,0:T(8,128)} %get-tuple-element.37), channel_id=1, source_target_pairs={{0,3},{1,2},{2,1},{3,0},{4,7},{5,6},{6,5},{7,4},{8,11},{9,10},{10,... | collective-permute-start | bytes 294920 | tf_op jit(solution)/shard_map/ppermute | solution.py:396
  4.0 2.6 %collective-permute-start.5 = (f32[96,256]{1,0:T(8,128)}, f32[96,256]{1,0:T(8,128)S(1)}, u32[]{:S(2)}, u32[]{:S(2)}) collective-permute-start(f32[96,256]{1,0:T(8,128)} %get-tuple-element.36), channel_id=1, source_target_pairs={{0,4},{1,5},{2,6},{3,7},{4,0},{5,1},{6,2},{7,3},{8,12},{9,13},{10,... | collective-permute-start | bytes 294920 | tf_op jit(solution)/shard_map/ppermute | solution.py:396
  6.7 1.0 %copy.17 = s32[6,1024]{0,1:T(8,128)S(1)} copy(s32[6,1024]{1,0:T(8,128)} %param.17) | data formatting | bytes 49152 | tf_op args[6]
  8.4 1.0 %broadcast_select_fusion = s32[6,1024]{0,1:T(8,128)} fusion(s32[6,1024]{0,1:T(8,128)S(1)} %copy.17, pred[1024]{0:T(1024)(128)(4,1)S(1)} %iota_compare_fusion), kind=kLoop, calls=%fused_computation | loop fusion | flops 6144 | bytes 50176 | tf_op jit(solution)/shard_map/jit(_where)/select_n | solution.py:430
  10.4 1.6 %collective-permute-start.7 = (f32[96,256]{1,0:T(8,128)S(1)}, f32[96,256]{1,0:T(8,128)S(1)}, u32[]{:S(2)}, u32[]{:S(2)}) collective-permute-start(f32[96,256]{1,0:T(8,128)S(1)} %get-tuple-element.34), channel_id=1, source_target_pairs={{0,6},{1,7},{2,4},{3,5},{4,2},{5,3},{6,0},{7,1},{8,14},{9,15},{10,... | collective-permute-start | bytes 294920 | tf_op jit(solution)/shard_map/ppermute | solution.py:396
  12.2 2.1 %collective-permute-done.5.refs_7_ = f32[96,256]{1,0:T(8,128)S(1)} collective-permute-done((f32[96,256]{1,0:T(8,128)}, f32[96,256]{1,0:T(8,128)S(1)}, u32[]{:S(2)}, u32[]{:S(2)}) %collective-permute-start.5) | collective-permute-done | bytes 98336 | tf_op jit(solution)/shard_map/ppermute | solution.py:396
  14.3 6.2 %collective-permute-done.6.refs_8_ = f32[96,256]{1,0:T(8,128)S(1)} collective-permute-done((f32[96,256]{1,0:T(8,128)S(1)}, f32[96,256]{1,0:T(8,128)S(1)}, u32[]{:S(2)}, u32[]{:S(2)}) %collective-permute-start.6) | collective-permute-done | bytes 98336 | tf_op jit(solution)/shard_map/ppermute | solution.py:396
  20.5 2.1 %collective-permute-done.7.refs_9_ = f32[96,256]{1,0:T(8,128)S(1)} collective-permute-done((f32[96,256]{1,0:T(8,128)S(1)}, f32[96,256]{1,0:T(8,128)S(1)}, u32[]{:S(2)}, u32[]{:S(2)}) %collective-permute-start.7) | collective-permute-done | bytes 98336 | tf_op jit(solution)/shard_map/ppermute | solution.py:396
  22.6 1.5 %collective-permute-done.8.refs_10_ = f32[96,256]{1,0:T(8,128)S(1)} collective-permute-done((f32[96,256]{1,0:T(8,128)S(1)}, f32[96,256]{1,0:T(8,128)S(1)}, u32[]{:S(2)}, u32[]{:S(2)}) %collective-permute-start.8) | collective-permute-done | bytes 98336 | tf_op jit(solution)/shard_map/ppermute | solution.py:396
  24.1 1.0 %transform.1 = (f32[96,256]{1,0:T(8,128)S(1)}, f32[96,256]{1,0:T(8,128)S(1)}, f32[96,256]{1,0:T(8,128)S(1)}, f32[96,256]{1,0:T(8,128)S(1)}, f32[96,256]{1,0:T(8,...) custom-call(f32[128,128]{1,0:T(8,128)S(1)} %get-tuple-element.46.refs_0_, ...), custom_call_target="tpu_custom_call" | custom-call | bytes 9000000 | tf_op jit(solution)/shard_map/transform/pallas_call | solution.py:98
  25.2 1.9 %collective-permute-start.11 = (f32[96,256]{1,0:T(8,128)S(1)}, f32[96,256]{1,0:T(8,128)S(1)}, u32[]{:S(2)}, u32[]{:S(2)}) collective-permute-start(f32[96,256]{1,0:T(8,128)S(1)} %get-tuple-element.23), channel_id=1, source_target_pairs={{0,6},{1,7},{2,4},{3,5},{4,2},{5,3},{6,0},{7,1},{8,14},{9,15},{10,... | collective-permute-start | bytes 294920 | tf_op jit(solution)/shard_map/ppermute | solution.py:396
  27.2 1.2 %copy.21.conn = s32[6,1024]{1,0:T(8,128)S(1)} copy(s32[6,1024]{0,1:T(8,128)} %broadcast_select_fusion) | data formatting | bytes 49152 | tf_op jit(solution)/shard_map/jit(_where)/select_n | solution.py:430
  28.7 5.1 %collective-permute-start.14 = (f32[96,256]{1,0:T(8,128)S(1)}, f32[96,256]{1,0:T(8,128)S(1)}, u32[]{:S(2)}, u32[]{:S(2)}) collective-permute-start(f32[96,256]{1,0:T(8,128)S(1)} %get-tuple-element.27), channel_id=1, source_target_pairs={{0,2},{1,3},{2,0},{3,1},{4,6},{5,7},{6,4},{7,5},{8,10},{9,11},{10,... | collective-permute-start | bytes 294920 | tf_op jit(solution)/shard_map/ppermute | solution.py:396
  33.8 4.1 %collective-permute-start.15 = (f32[96,256]{1,0:T(8,128)S(1)}, f32[96,256]{1,0:T(8,128)S(1)}, u32[]{:S(2)}, u32[]{:S(2)}) collective-permute-start(f32[96,256]{1,0:T(8,128)S(1)} %get-tuple-element.28), channel_id=1, source_target_pairs={{0,3},{1,2},{2,1},{3,0},{4,7},{5,6},{6,5},{7,4},{8,11},{9,10},{10,... | collective-permute-start | bytes 294920 | tf_op jit(solution)/shard_map/ppermute | solution.py:396
  37.9 1.2 %collective-permute-done.11.refs_2_.refs_6_ = f32[96,256]{1,0:T(8,128)S(1)} collective-permute-done((f32[96,256]{1,0:T(8,128)S(1)}, f32[96,256]{1,0:T(8,128)S(1)}, u32[]{:S(2)}, u32[]{:S(2)}) %collective-permute-start.11) | collective-permute-done | bytes 98336 | tf_op jit(solution)/shard_map/ppermute | solution.py:396
  39.7 1.0 %collective-permute-done.12.refs_3_.refs_7_ = f32[96,256]{1,0:T(8,128)S(1)} collective-permute-done((f32[96,256]{1,0:T(8,128)S(1)}, f32[96,256]{1,0:T(8,128)S(1)}, u32[]{:S(2)}, u32[]{:S(2)}) %collective-permute-start.12) | collective-permute-done | bytes 98336 | tf_op jit(solution)/shard_map/ppermute | solution.py:396
  40.7 3.4 %collective-permute-start = (f32[96,256]{1,0:T(8,128)S(1)}, f32[96,256]{1,0:T(8,128)S(1)}, u32[]{:S(2)}, u32[]{:S(2)}) collective-permute-start(f32[96,256]{1,0:T(8,128)S(1)} %get-tuple-element.19), channel_id=1, source_target_pairs={{0,8},{8,16},{16,24},{1,9},{9,17},{17,25},{2,10},{10,18},{18,26},{... | collective-permute-start | bytes 294920 | tf_op jit(solution)/shard_map/ppermute | solution.py:403
  44.1 3.4 %collective-permute-start.1 = (f32[96,256]{1,0:T(8,128)S(1)}, f32[96,256]{1,0:T(8,128)S(1)}, u32[]{:S(2)}, u32[]{:S(2)}) collective-permute-start(f32[96,256]{1,0:T(8,128)S(1)} %get-tuple-element.20), channel_id=1, source_target_pairs={{8,0},{16,8},{24,16},{9,1},{17,9},{25,17},{10,2},{18,10},{26,18},{... | collective-permute-start | bytes 294920 | tf_op jit(solution)/shard_map/ppermute | solution.py:404
  47.5 1.1 %interface_values.3 = (f32[96,256]{1,0:T(8,128)S(1)}, f32[96,256]{1,0:T(8,128)S(1)}) custom-call(s32[8]{0:T(128)S(1)} %xor_multiply_fusion.bases, s32[1,512]{1,0:T(1,128)S(1)} %bitcast.22, f32[96,256]{1,0:T(8,128)S(1)} %get-tuple-element.25.refs_0_, f32[96,256]{1,0:T(8,128)S(1)} %collective-permute-done.13.refs_1_, ...), custom_call_target="tpu_custom_call" | custom-call | bytes 9000000 | tf_op jit(solution)/shard_map/interface_values/pallas_call | solution.py:130
  48.7 2.5 %collective-permute-start.16 = (f32[96,256]{1,0:T(8,128)S(1)}, f32[96,256]{1,0:T(8,128)S(1)}, u32[]{:S(2)}, u32[]{:S(2)}) collective-permute-start(f32[96,256]{1,0:T(8,128)S(1)} %get-tuple-element.29), channel_id=1, source_target_pairs={{0,8},{8,16},{16,24},{1,9},{9,17},{17,25},{2,10},{10,18},{18,26},{... | collective-permute-start | bytes 294920 | tf_op jit(solution)/shard_map/ppermute | solution.py:403
  51.2 4.3 %collective-permute-start.17 = (f32[96,256]{1,0:T(8,128)S(1)}, f32[96,256]{1,0:T(8,128)S(1)}, u32[]{:S(2)}, u32[]{:S(2)}) collective-permute-start(f32[96,256]{1,0:T(8,128)S(1)} %get-tuple-element.30), channel_id=1, source_target_pairs={{8,0},{16,8},{24,16},{9,1},{17,9},{25,17},{10,2},{18,10},{26,18},{... | collective-permute-start | bytes 294920 | tf_op jit(solution)/shard_map/ppermute | solution.py:404
  55.5 8.6 %magnetic_terms.1.magnetic_part = f32[96,6144]{1,0:T(8,128)S(1)} custom-call(s32[3]{0:T(128)S(1)} %copy-done.8, s32[6,1024]{1,0:T(8,128)S(1)} %copy.21.conn, f32[6,6,1024]{2,1,0:T(8,128)S(1)} %copy-done.4, f32[6,6,1024]{2,1,0:T(8,128)S(1)} %copy-done.5, f32[8,1]{1,0:T(8,128)S(1)} %fusion.14.squares, f32[96,2048]{1,0:T(8,128)S(1)} %bitcast.19, ...), custom_call_target="tpu_custom_call" | custom-call | bytes 42000000 | tf_op jit(solution)/shard_map/magnetic_terms/pallas_call | solution.py:192
  64.1 4.0 %gathered.2.refs_4_ = f32[96,6144]{1,0:T(8,128)S(1)} custom-call(s32[4]{0:T(128)S(1)} %get-tuple-element.47.bases, s32[6,1024]{1,0:T(8,128)S(1)} %copy.21.conn, f32[96,256]{1,0:T(8,128)S(1)} %get-tuple-element.25.refs_0_, f32[96,256]{1,0:T(8,128)S(1)} %collective-permute-done.13.refs_1_, f32[96,256]{1,0:T(8,128)S(1)} %collective-permute-done.14.refs_2_, ...), custom_call_target="tpu_custom_call" | custom-call | bytes 18000000 | tf_op jit(solution)/shard_map/gathered/pallas_call | solution.py:240
  68.1 4.2 %gathered.3.electric_part = f32[96,6144]{1,0:T(8,128)S(1)} custom-call(s32[4]{0:T(128)S(1)} %get-tuple-element.48.bases, s32[6,1024]{1,0:T(8,128)S(1)} %copy.21.conn, f32[96,256]{1,0:T(8,128)S(1)} %collective-permute-done.9.refs_0_.refs_4_, f32[96,256]{1,0:T(8,128)S(1)} %collective-permute-done.10.refs_1_.refs_5_, ...), custom_call_target="tpu_custom_call" | custom-call | bytes 18000000 | tf_op jit(solution)/shard_map/gathered/pallas_call | solution.py:240
  72.4 5.6 %ghost_terms.1 = (bf16[192,6144]{1,0:T(8,128)(2,1)S(1)}, f32[2,96,256]{2,1,0:T(8,128)S(1)}) custom-call(s32[6,1024]{1,0:T(8,128)S(1)} %copy.21.conn, s32[1024,6]{1,0:T(8,128)S(1)} %fusion.26.conn_columns, f32[6,6,1024]{2,1,0:T(8,128)S(1)} %copy-done.6, f32[96,6144]{1,0:T(8,128)S(1)} %magnetic_terms.1.magnetic_part, f32[96,6144]{1,0:T(8,128)S(1)} %gathered.3.electric_part, ...), custom_call_target="tpu_custom_call" | custom-call | bytes 24000000 | tf_op jit(solution)/shard_map/ghost_terms/pallas_call | solution.py:312
  78.0 1.4 %copy-done.1 = bf16[192,6144]{1,0:T(8,128)(2,1)} copy-done((bf16[192,6144]{1,0:T(8,128)(2,1)}, bf16[192,6144]{1,0:T(8,128)(2,1)S(1)}, u32[]{:S(2)}) %copy-start.1) | copy-done | bytes 2359320
  79.4 1.9 %collective-permute-start.18 = (f32[96,256]{1,0:T(8,128)S(1)}, f32[96,256]{1,0:T(8,128)S(1)}, u32[]{:S(2)}, u32[]{:S(2)}) collective-permute-start(f32[96,256]{1,0:T(8,128)S(1)} %get-tuple-element.42), channel_id=1, source_target_pairs={{0,8},{8,16},{16,24},{1,9},{9,17},{17,25},{2,10},{10,18},{18,26},{... | collective-permute-start | bytes 294920 | tf_op jit(solution)/shard_map/ppermute | solution.py:403
  81.4 4.8 %collective-permute-start.19 = (f32[96,256]{1,0:T(8,128)S(1)}, f32[96,256]{1,0:T(8,128)S(1)}, u32[]{:S(2)}, u32[]{:S(2)}) collective-permute-start(f32[96,256]{1,0:T(8,128)S(1)} %get-tuple-element.41), channel_id=1, source_target_pairs={{8,0},{16,8},{24,16},{9,1},{17,9},{25,17},{10,2},{18,10},{26,18},{... | collective-permute-start | bytes 294920 | tf_op jit(solution)/shard_map/ppermute | solution.py:404
  86.3 1.7 %copy-done.2 = bf16[192,6144]{1,0:T(8,128)(2,1)S(1)} copy-done((bf16[192,6144]{1,0:T(8,128)(2,1)S(1)}, bf16[192,6144]{1,0:T(8,128)(2,1)}, u32[]{:S(2)}) %copy-start.2) | copy-done | bytes 2359320
  88.0 6.2 %own_sums.1.sums = f32[96,2048]{1,0:T(8,128)S(1)} custom-call(s32[1024,6]{1,0:T(8,128)S(1)} %fusion.26.conn_columns, bf16[192,6144]{1,0:T(8,128)(2,1)S(1)} %copy-done.2), custom_call_target="tpu_custom_call" | custom-call | bytes 27000000 | tf_op jit(solution)/shard_map/own_sums/pallas_call | solution.py:357
  94.2 1.6 %finish.1 = f32[96,2048]{1,0:T(8,128)} custom-call(s32[512,1]{1,0:T(8,128)S(1)} %copy.22.columns, f32[96,2048]{1,0:T(8,128)S(1)} %bitcast.20, f32[96,2048]{1,0:T(8,128)S(1)} %own_sums.1.sums, f32[96,256]{1,0:T(8,128)S(1)} %collective-permute-done.18.left, f32[96,256]{1,0:T(8,128)S(1)} %collective-permute-done.19.right, f32[1,2048]{1,0:T(1,128)S(1)} %bitcast.24), custom_call_target="tpu_custom_call" | custom-call | bytes 9000000 | tf_op jit(solution)/shard_map/finish/pallas_call | solution.py:384
  (56 shorter events, 3.0 us)
Async XLA Ops:
  0.0 9.6 %copy-start.10 = (s32[1,2]{1,0:T(1,128)S(1)}, s32[1,2]{1,0:T(1,128)}, u32[]{:S(2)}) copy-start(s32[1,2]{1,0:T(1,128)} %param.19) | copy-start | bytes 28
  0.0 10.3 %copy-start.9 = (s32[1,512]{1,0:T(1,128)S(1)}, s32[1,512]{1,0:T(1,128)}, u32[]{:S(2)}) copy-start(s32[1,512]{1,0:T(1,128)} %param.18) | copy-start | bytes 6148
  0.0 24.1 %copy-start.3 = (f32[3,128,256]{2,1,0:T(8,128)S(1)}, f32[3,128,256]{2,1,0:T(8,128)}, u32[]{:S(2)}) copy-start(f32[3,128,256]{2,1,0:T(8,128)} %refs_2_.1) | copy-start | bytes 1179652
  2.2 8.3 %collective-permute-start.2 = (f32[96,256]{1,0:T(8,128)}, f32[96,256]{1,0:T(8,128)S(1)}, u32[]{:S(2)}, u32[]{:S(2)}) collective-permute-start(f32[96,256]{1,0:T(8,128)} %get-tuple-element.39), channel_id=1, source_target_pairs={{0,1},{1,0},{2,3},{3,2},{4,5},{5,4},{6,7},{7,6},{8,9},{9,8},{10,11... | collective-permute-start | bytes 294920 | tf_op jit(solution)/shard_map/ppermute | solution.py:396
  2.2 9.8 %collective-permute-start.3 = (f32[96,256]{1,0:T(8,128)}, f32[96,256]{1,0:T(8,128)S(1)}, u32[]{:S(2)}, u32[]{:S(2)}) collective-permute-start(f32[96,256]{1,0:T(8,128)} %get-tuple-element.38), channel_id=1, source_target_pairs={{0,2},{1,3},{2,0},{3,1},{4,6},{5,7},{6,4},{7,5},{8,10},{9,11},{10,... | collective-permute-start | bytes 294920 | tf_op jit(solution)/shard_map/ppermute | solution.py:396
  2.6 9.6 %collective-permute-start.4 = (f32[96,256]{1,0:T(8,128)}, f32[96,256]{1,0:T(8,128)S(1)}, u32[]{:S(2)}, u32[]{:S(2)}) collective-permute-start(f32[96,256]{1,0:T(8,128)} %get-tuple-element.37), channel_id=1, source_target_pairs={{0,3},{1,2},{2,1},{3,0},{4,7},{5,6},{6,5},{7,4},{8,11},{9,10},{10,... | collective-permute-start | bytes 294920 | tf_op jit(solution)/shard_map/ppermute | solution.py:396
  4.0 10.3 %collective-permute-start.5 = (f32[96,256]{1,0:T(8,128)}, f32[96,256]{1,0:T(8,128)S(1)}, u32[]{:S(2)}, u32[]{:S(2)}) collective-permute-start(f32[96,256]{1,0:T(8,128)} %get-tuple-element.36), channel_id=1, source_target_pairs={{0,4},{1,5},{2,6},{3,7},{4,0},{5,1},{6,2},{7,3},{8,12},{9,13},{10,... | collective-permute-start | bytes 294920 | tf_op jit(solution)/shard_map/ppermute | solution.py:396
  6.6 13.9 %collective-permute-start.6 = (f32[96,256]{1,0:T(8,128)S(1)}, f32[96,256]{1,0:T(8,128)S(1)}, u32[]{:S(2)}, u32[]{:S(2)}) collective-permute-start(f32[96,256]{1,0:T(8,128)S(1)} %get-tuple-element.35), channel_id=1, source_target_pairs={{0,5},{1,4},{2,7},{3,6},{4,1},{5,0},{6,3},{7,2},{8,13},{9,12},{10,... | collective-permute-start | bytes 294920 | tf_op jit(solution)/shard_map/ppermute | solution.py:396
  6.6 32.5 %copy-start = (f32[2,6,8,2048]{3,2,1,0:T(8,128)S(1)}, f32[2,6,8,2048]{3,2,1,0:T(8,128)}, u32[]{:S(2)}) copy-start(f32[2,6,8,2048]{3,2,1,0:T(8,128)} %param.11) | copy-start | bytes 2359300
  9.4 46.1 %copy-start.4 = (f32[6,6,1024]{2,1,0:T(8,128)S(1)}, f32[6,6,1024]{2,1,0:T(8,128)}, u32[]{:S(2)}) copy-start(f32[6,6,1024]{2,1,0:T(8,128)} %stiffness.1) | copy-start | bytes 442372
  9.4 46.1 %copy-start.5 = (f32[6,6,1024]{2,1,0:T(8,128)S(1)}, f32[6,6,1024]{2,1,0:T(8,128)}, u32[]{:S(2)}) copy-start(f32[6,6,1024]{2,1,0:T(8,128)} %mass_r.1) | copy-start | bytes 442372
  9.4 46.1 %copy-start.8 = (s32[3]{0:T(128)S(1)}, s32[3]{0:T(128)}, u32[]{:S(2)}) copy-start(s32[3]{0:T(128)} %constant.121.clone.bases) | copy-start | bytes 40
  10.4 12.2 %collective-permute-start.7 = (f32[96,256]{1,0:T(8,128)S(1)}, f32[96,256]{1,0:T(8,128)S(1)}, u32[]{:S(2)}, u32[]{:S(2)}) collective-permute-start(f32[96,256]{1,0:T(8,128)S(1)} %get-tuple-element.34), channel_id=1, source_target_pairs={{0,6},{1,7},{2,4},{3,5},{4,2},{5,3},{6,0},{7,1},{8,14},{9,15},{10,... | collective-permute-start | bytes 294920 | tf_op jit(solution)/shard_map/ppermute | solution.py:396
  12.0 12.2 %collective-permute-start.8 = (f32[96,256]{1,0:T(8,128)S(1)}, f32[96,256]{1,0:T(8,128)S(1)}, u32[]{:S(2)}, u32[]{:S(2)}) collective-permute-start(f32[96,256]{1,0:T(8,128)S(1)} %get-tuple-element.33), channel_id=1, source_target_pairs={{0,7},{1,6},{2,5},{3,4},{4,3},{5,2},{6,1},{7,0},{8,15},{9,14},{10,... | collective-permute-start | bytes 294920 | tf_op jit(solution)/shard_map/ppermute | solution.py:396
  25.1 8.7 %collective-permute-start.10 = (f32[96,256]{1,0:T(8,128)S(1)}, f32[96,256]{1,0:T(8,128)S(1)}, u32[]{:S(2)}, u32[]{:S(2)}) collective-permute-start(f32[96,256]{1,0:T(8,128)S(1)} %get-tuple-element.22), channel_id=1, source_target_pairs={{0,5},{1,4},{2,7},{3,6},{4,1},{5,0},{6,3},{7,2},{8,13},{9,12},{10,... | collective-permute-start | bytes 294920 | tf_op jit(solution)/shard_map/ppermute | solution.py:396
  25.2 13.9 %collective-permute-start.11 = (f32[96,256]{1,0:T(8,128)S(1)}, f32[96,256]{1,0:T(8,128)S(1)}, u32[]{:S(2)}, u32[]{:S(2)}) collective-permute-start(f32[96,256]{1,0:T(8,128)S(1)} %get-tuple-element.23), channel_id=1, source_target_pairs={{0,6},{1,7},{2,4},{3,5},{4,2},{5,3},{6,0},{7,1},{8,14},{9,15},{10,... | collective-permute-start | bytes 294920 | tf_op jit(solution)/shard_map/ppermute | solution.py:396
  28.4 12.3 %collective-permute-start.12 = (f32[96,256]{1,0:T(8,128)S(1)}, f32[96,256]{1,0:T(8,128)S(1)}, u32[]{:S(2)}, u32[]{:S(2)}) collective-permute-start(f32[96,256]{1,0:T(8,128)S(1)} %get-tuple-element.24), channel_id=1, source_target_pairs={{0,7},{1,6},{2,5},{3,4},{4,3},{5,2},{6,1},{7,0},{8,15},{9,14},{10,... | collective-permute-start | bytes 294920 | tf_op jit(solution)/shard_map/ppermute | solution.py:396
  28.5 15.6 %collective-permute-start.13 = (f32[96,256]{1,0:T(8,128)S(1)}, f32[96,256]{1,0:T(8,128)S(1)}, u32[]{:S(2)}, u32[]{:S(2)}) collective-permute-start(f32[96,256]{1,0:T(8,128)S(1)} %get-tuple-element.26), channel_id=1, source_target_pairs={{0,1},{1,0},{2,3},{3,2},{4,5},{5,4},{6,7},{7,6},{8,9},{9,8},{10,11... | collective-permute-start | bytes 294920 | tf_op jit(solution)/shard_map/ppermute | solution.py:396
  28.7 18.8 %collective-permute-start.14 = (f32[96,256]{1,0:T(8,128)S(1)}, f32[96,256]{1,0:T(8,128)S(1)}, u32[]{:S(2)}, u32[]{:S(2)}) collective-permute-start(f32[96,256]{1,0:T(8,128)S(1)} %get-tuple-element.27), channel_id=1, source_target_pairs={{0,2},{1,3},{2,0},{3,1},{4,6},{5,7},{6,4},{7,5},{8,10},{9,11},{10,... | collective-permute-start | bytes 294920 | tf_op jit(solution)/shard_map/ppermute | solution.py:396
  33.8 13.7 %collective-permute-start.15 = (f32[96,256]{1,0:T(8,128)S(1)}, f32[96,256]{1,0:T(8,128)S(1)}, u32[]{:S(2)}, u32[]{:S(2)}) collective-permute-start(f32[96,256]{1,0:T(8,128)S(1)} %get-tuple-element.28), channel_id=1, source_target_pairs={{0,3},{1,2},{2,1},{3,0},{4,7},{5,6},{6,5},{7,4},{8,11},{9,10},{10,... | collective-permute-start | bytes 294920 | tf_op jit(solution)/shard_map/ppermute | solution.py:396
  39.1 8.4 %collective-permute-start.9 = (f32[96,256]{1,0:T(8,128)S(1)}, f32[96,256]{1,0:T(8,128)S(1)}, u32[]{:S(2)}, u32[]{:S(2)}) collective-permute-start(f32[96,256]{1,0:T(8,128)S(1)} %get-tuple-element.21), channel_id=1, source_target_pairs={{0,4},{1,5},{2,6},{3,7},{4,0},{5,1},{6,2},{7,3},{8,12},{9,13},{10,... | collective-permute-start | bytes 294920 | tf_op jit(solution)/shard_map/ppermute | solution.py:396
  40.7 14.7 %collective-permute-start = (f32[96,256]{1,0:T(8,128)S(1)}, f32[96,256]{1,0:T(8,128)S(1)}, u32[]{:S(2)}, u32[]{:S(2)}) collective-permute-start(f32[96,256]{1,0:T(8,128)S(1)} %get-tuple-element.19), channel_id=1, source_target_pairs={{0,8},{8,16},{16,24},{1,9},{9,17},{17,25},{2,10},{10,18},{18,26},{... | collective-permute-start | bytes 294920 | tf_op jit(solution)/shard_map/ppermute | solution.py:403
  44.1 11.3 %collective-permute-start.1 = (f32[96,256]{1,0:T(8,128)S(1)}, f32[96,256]{1,0:T(8,128)S(1)}, u32[]{:S(2)}, u32[]{:S(2)}) collective-permute-start(f32[96,256]{1,0:T(8,128)S(1)} %get-tuple-element.20), channel_id=1, source_target_pairs={{8,0},{16,8},{24,16},{9,1},{17,9},{25,17},{10,2},{18,10},{26,18},{... | collective-permute-start | bytes 294920 | tf_op jit(solution)/shard_map/ppermute | solution.py:404
  48.7 23.7 %collective-permute-start.16 = (f32[96,256]{1,0:T(8,128)S(1)}, f32[96,256]{1,0:T(8,128)S(1)}, u32[]{:S(2)}, u32[]{:S(2)}) collective-permute-start(f32[96,256]{1,0:T(8,128)S(1)} %get-tuple-element.29), channel_id=1, source_target_pairs={{0,8},{8,16},{16,24},{1,9},{9,17},{17,25},{2,10},{10,18},{18,26},{... | collective-permute-start | bytes 294920 | tf_op jit(solution)/shard_map/ppermute | solution.py:403
  51.2 21.2 %collective-permute-start.17 = (f32[96,256]{1,0:T(8,128)S(1)}, f32[96,256]{1,0:T(8,128)S(1)}, u32[]{:S(2)}, u32[]{:S(2)}) collective-permute-start(f32[96,256]{1,0:T(8,128)S(1)} %get-tuple-element.30), channel_id=1, source_target_pairs={{8,0},{16,8},{24,16},{9,1},{17,9},{25,17},{10,2},{18,10},{26,18},{... | collective-permute-start | bytes 294920 | tf_op jit(solution)/shard_map/ppermute | solution.py:404
  68.1 4.3 %copy-start.6 = (f32[6,6,1024]{2,1,0:T(8,128)S(1)}, f32[6,6,1024]{2,1,0:T(8,128)}, u32[]{:S(2)}) copy-start(f32[6,6,1024]{2,1,0:T(8,128)} %coupling.1) | copy-start | bytes 442372
  78.0 1.4 %copy-start.1 = (bf16[192,6144]{1,0:T(8,128)(2,1)}, bf16[192,6144]{1,0:T(8,128)(2,1)S(1)}, u32[]{:S(2)}) copy-start(bf16[192,6144]{1,0:T(8,128)(2,1)S(1)} %get-tuple-element.31.terms) | copy-start | bytes 7077892
  79.4 14.8 %copy-start.7 = (f32[2048]{0:T(1024)S(1)}, f32[2048]{0:T(1024)}, u32[]{:S(2)}) copy-start(f32[2048]{0:T(1024)} %param.16) | copy-start | bytes 24580
  79.4 14.8 %collective-permute-start.18 = (f32[96,256]{1,0:T(8,128)S(1)}, f32[96,256]{1,0:T(8,128)S(1)}, u32[]{:S(2)}, u32[]{:S(2)}) collective-permute-start(f32[96,256]{1,0:T(8,128)S(1)} %get-tuple-element.42), channel_id=1, source_target_pairs={{0,8},{8,16},{16,24},{1,9},{9,17},{17,25},{2,10},{10,18},{18,26},{... | collective-permute-start | bytes 294920 | tf_op jit(solution)/shard_map/ppermute | solution.py:403
  81.4 12.8 %collective-permute-start.19 = (f32[96,256]{1,0:T(8,128)S(1)}, f32[96,256]{1,0:T(8,128)S(1)}, u32[]{:S(2)}, u32[]{:S(2)}) collective-permute-start(f32[96,256]{1,0:T(8,128)S(1)} %get-tuple-element.41), channel_id=1, source_target_pairs={{8,0},{16,8},{24,16},{9,1},{17,9},{25,17},{10,2},{18,10},{26,18},{... | collective-permute-start | bytes 294920 | tf_op jit(solution)/shard_map/ppermute | solution.py:404
  86.3 1.7 %copy-start.2 = (bf16[192,6144]{1,0:T(8,128)(2,1)S(1)}, bf16[192,6144]{1,0:T(8,128)(2,1)}, u32[]{:S(2)}) copy-start(bf16[192,6144]{1,0:T(8,128)(2,1)} %copy-done.1) | copy-start | bytes 7077892

commit v2 on v1

v2 whole, which is shorter than its diff:
```python
import functools
import math

import jax
import jax.numpy as jnp
import numpy as np
from jax import lax
from jax.experimental import pallas as pl
from jax.experimental.pallas import tpu as pltpu
from jax.sharding import PartitionSpec as P

diffusivity = 1.0
time_step = 0.1
f32 = jnp.float32
bf16 = jnp.bfloat16
KERNEL_VMEM = 20 << 20
ELEM_TILE = 256


def whole_block(shape):
    return pl.BlockSpec(shape, lambda *ids: (0,) * len(shape))


class Block:
    def __init__(self, array, rows, at=0):
        self.array, self.rows, self.at = array, rows, at
        self.shape = (rows, array.shape[1])

    def spec(self):
        at = self.at
        return pl.BlockSpec(self.shape, lambda *ids: (at, 0))


def specs(blocks):
    return [block.spec() for block in blocks]


def arrays(blocks):
    return [block.array for block in blocks]


def params():
    return pltpu.CompilerParams(vmem_limit_bytes=KERNEL_VMEM)


def cost(us):
    return pl.CostEstimate(flops=0, bytes_accessed=int(us * 3.0e6), transcendentals=0)


def split_rows(value):
    high = value.astype(bf16)
    low = (value - high.astype(f32)).astype(bf16)
    return jnp.concatenate([high, low], 0)


def halves_sum(value):
    rows = value.shape[0] // 2
    return value[:rows] + value[rows:]


def own_member():
    return lax.axis_index("mode")


def base_of(step, slab):
    return (own_member() ^ step) * slab


def columns_of(ids):
    rows = ids.shape[0]
    filled = jnp.concatenate([ids, jnp.broadcast_to(ids[:1], (8 - rows, ids.shape[1]))], 0)
    return filled.T


def one_hot(iota, ids):
    return jnp.where(iota == ids, 1.0, 0.0).astype(bf16)


def transform_tables(mode_dev, members):
    spectral_modes = mode_dev * members
    samples = 2 * spectral_modes
    row = np.arange(samples)
    parity = (row // mode_dev) % 2
    mode = row // (2 * mode_dev) * mode_dev + row % mode_dev
    phases = 2.0 * np.pi / samples * (np.arange(samples)[None, :] * mode[:, None] % samples)
    inverse = np.where(parity[:, None] == 0, np.cos(phases), np.sin(phases))
    weights = np.where((mode == 0) & (parity == 0), 1.0, 2.0) / samples
    return jnp.asarray(inverse, f32), jnp.asarray(inverse * weights[:, None], f32)


def spread_table(table):
    high = table.astype(bf16)
    low = (table - high.astype(f32)).astype(bf16)
    return jnp.concatenate([high, high, low], 1)


def spread_value(value):
    high = value.astype(bf16)
    low = (value - high.astype(f32)).astype(bf16)
    return jnp.concatenate([high, low, high], 0)


def transform_kernel(members, mode_dev, fields, *refs):
    inverse, forward, velocity = refs[:3]
    blocks = refs[3 : 3 + members]
    outs = refs[-(members // 2) :]
    pair = 2 * mode_dev
    rows = blocks[0].shape[0]
    ordered = []
    for table in (inverse, forward):
        starts = [pl.multiple_of(base_of(step, pair), 8) for step in range(members)]
        ordered.append(jnp.concatenate([table[pl.ds(start, pair), :] for start in starts], 0))
    to_points, to_modes = spread_table(ordered[0].T), spread_table(ordered[1])
    for field in range(fields):
        points = []
        for part in range(3):
            low = (field * 3 + part) * pair
            stacked = jnp.concatenate([block[low : low + pair, :] for block in blocks], 0)
            points.append(
                jnp.dot(to_points, spread_value(stacked), preferred_element_type=f32)
            )
        for part in range(3):
            after, last = (part + 1) % 3, (part + 2) % 3
            cross = velocity[after] * points[last] - velocity[last] * points[after]
            back = jnp.dot(to_modes, spread_value(cross), preferred_element_type=f32)
            low = (field * 3 + part) * pair
            for step in range(members):
                at = (step % 2) * rows + low
                outs[step // 2][at : at + pair, :] = back[step * pair : (step + 1) * pair]


def transform(blocks, velocity, inverse, forward, mode_dev, fields):
    members = len(blocks)
    rows, slab = blocks[0].shape
    return pl.pallas_call(
        functools.partial(transform_kernel, members, mode_dev, fields),
        grid=(1,),
        in_specs=[whole_block(x.shape) for x in (inverse, forward, velocity)]
        + specs(blocks),
        out_specs=[whole_block((2 * rows, slab))] * (members // 2),
        out_shape=[jax.ShapeDtypeStruct((2 * rows, slab), f32)] * (members // 2),
        compiler_params=params(),
        cost_estimate=cost(1),
        name="transform",
    )(inverse, forward, velocity, *arrays(blocks))


def pack_kernel(rows, slab, values, *refs):
    outs, sems = refs[:-1], refs[-1]
    copies = []
    for at in range(2 * len(outs)):
        start = pl.multiple_of(base_of(at, slab), 128)
        half = at % 2
        copies.append(
            pltpu.make_async_copy(
                values.at[:, pl.ds(start, slab)],
                outs[at // 2].at[half * rows : (half + 1) * rows, :],
                sems.at[at],
            )
        )
    for copy in copies:
        copy.start()
    for copy in copies:
        copy.wait()


def pack(values, members, slab):
    rows = values.shape[0]
    anywhere = pl.BlockSpec(memory_space=pl.ANY)
    return pl.pallas_call(
        functools.partial(pack_kernel, rows, slab),
        in_specs=[anywhere],
        out_specs=[anywhere] * (members // 2),
        out_shape=[jax.ShapeDtypeStruct((2 * rows, slab), f32)] * (members // 2),
        scratch_shapes=[pltpu.SemaphoreType.DMA((members,))],
        compiler_params=params(),
        cost_estimate=cost(1),
        name="pack",
    )(values)


def lower_halves_kernel(count, *refs):
    blocks, out, sems = refs[:count], refs[-2], refs[-1]
    rows = blocks[0].shape[0] // 2
    copies = [
        pltpu.make_async_copy(
            block.at[rows:, :], out.at[at * rows : (at + 1) * rows, :], sems.at[at]
        )
        for at, block in enumerate(blocks)
    ]
    for copy in copies:
        copy.start()
    for copy in copies:
        copy.wait()


def lower_halves(blocks, after):
    rows, width = blocks[0].shape[0] // 2, blocks[0].shape[1]
    anywhere = pl.BlockSpec(memory_space=pl.ANY)
    return pl.pallas_call(
        functools.partial(lower_halves_kernel, len(blocks)),
        in_specs=[anywhere] * (len(blocks) + len(after)),
        out_specs=anywhere,
        out_shape=jax.ShapeDtypeStruct((len(blocks) * rows, width), f32),
        scratch_shapes=[pltpu.SemaphoreType.DMA((len(blocks),))],
        compiler_params=params(),
        cost_estimate=cost(0.5),
        name="lower_halves",
    )(*blocks, *after)


def interface_ids(interface, counts):
    width = interface.shape[1]
    cap = width // 2
    lists = jnp.broadcast_to(interface[...], (8, width))
    shifted = pltpu.roll(lists, lax.rem(width - counts[0, 0], width), 1)
    return jnp.concatenate([lists[:1, :cap], shifted[:1, :cap]], 1)


def interface_kernel(count, steps, counts, interface, *refs):
    blocks = refs[:count]
    left, right, hot = refs[-3:]
    width = interface.shape[1]
    ids = interface_ids(interface, counts)
    row = 0
    stacked = []
    for at, block in enumerate(blocks):
        size = block.shape[1]
        iota = lax.broadcasted_iota(jnp.int32, (size, width), 0)
        base = 0 if steps is None else base_of(steps[at], size)
        hot[row : row + size, :] = one_hot(iota, ids - base)
        stacked.append(split_rows(block[...]))
        row += size
    values = jnp.concatenate(stacked, 1)
    got = halves_sum(jnp.dot(values, hot[...], preferred_element_type=f32))
    left[...] = got[:, : width // 2]
    right[...] = got[:, width // 2 :]


def interface_values(blocks, steps, counts, interface, us, after=()):
    rows = blocks[0].shape[0]
    total = sum(block.shape[1] for block in blocks)
    cap = interface.shape[1] // 2
    return pl.pallas_call(
        functools.partial(interface_kernel, len(blocks), steps),
        grid=(1,),
        in_specs=[pl.BlockSpec(memory_space=pltpu.SMEM), whole_block(interface.shape)]
        + specs(blocks)
        + [pl.BlockSpec(memory_space=pl.ANY)] * len(after),
        out_specs=[whole_block((rows, cap))] * 2,
        out_shape=[jax.ShapeDtypeStruct((rows, cap), f32)] * 2,
        scratch_shapes=[pltpu.VMEM((total, 2 * cap), bf16)],
        compiler_params=params(),
        cost_estimate=cost(us),
        name="interface_values",
    )(counts, interface, *arrays(blocks), *after)


def live_rows(conn, live, tile_at):
    tile = conn.shape[1]
    element = tile_at * tile + lax.broadcasted_iota(jnp.int32, conn.shape, 1)
    return jnp.where(element < live[0], conn[...], -1)


def fill_gather(hot, conn, blocks, bases, tile):
    row = 0
    for at, block in enumerate(blocks):
        size = block.shape[1]
        iota = lax.broadcasted_iota(jnp.int32, (size, tile), 0)
        for corner in range(6):
            hot[row : row + size, corner * tile : (corner + 1) * tile] = one_hot(
                iota, conn[corner : corner + 1, :] - bases[at]
            )
        row += size


def fill_values(values, blocks):
    column = 0
    for block in blocks:
        size = block.shape[1]
        values[:, column : column + size] = split_rows(block[...])
        column += size


def magnetic_terms_kernel(count, mode_dev, live, conn, stiffness, mass_r, *refs):
    blocks = refs[:count]
    out, done, values, hot, operator = refs[-5:]
    tile = conn.shape[1]
    done[...] = jnp.zeros_like(done)

    @pl.when(pl.program_id(0) == 0)
    def _():
        fill_values(values, blocks)

    bases = [0]
    for block in blocks[:-1]:
        bases.append(bases[-1] + block.shape[1])
    fill_gather(hot, live_rows(conn, live, pl.program_id(0)), blocks, bases, tile)
    lane = lax.broadcasted_iota(jnp.int32, (8, tile), 0)
    squares = (own_member() * mode_dev + lax.rem(lane, mode_dev)).astype(f32) ** 2
    got = halves_sum(jnp.dot(values[...], hot[...], preferred_element_type=f32))
    for a in range(6):
        for b in range(6):
            operator[a * 6 + b] = diffusivity * (
                stiffness[a, b : b + 1, :] + squares * mass_r[a, b : b + 1, :]
            )
    for low in range(0, out.shape[0], 8):
        for a in range(6):
            total = None
            for b in range(6):
                term = operator[a * 6 + b] * got[low : low + 8, b * tile : (b + 1) * tile]
                total = term if total is None else total + term
            out[low : low + 8, a * tile : (a + 1) * tile] = total


def magnetic_terms(blocks, mode_dev, live, conn, stiffness, mass_r, after):
    rows = blocks[0].shape[0]
    elems = conn.shape[1]
    tile = ELEM_TILE
    total = sum(block.shape[1] for block in blocks)
    elem_block = pl.BlockSpec((6, 6, tile), lambda j: (0, 0, j))
    return pl.pallas_call(
        functools.partial(magnetic_terms_kernel, len(blocks), mode_dev),
        grid=(elems // tile,),
        in_specs=[
            pl.BlockSpec(memory_space=pltpu.SMEM),
            pl.BlockSpec((6, tile), lambda j: (0, j)),
            elem_block,
            elem_block,
        ]
        + specs(blocks)
        + [pl.BlockSpec(memory_space=pl.ANY)] * len(after),
        out_specs=[pl.BlockSpec((rows, 6 * tile), lambda j: (0, j)), whole_block((8, 128))],
        out_shape=[
            jax.ShapeDtypeStruct((rows, 6 * elems), f32),
            jax.ShapeDtypeStruct((8, 128), f32),
        ],
        scratch_shapes=[
            pltpu.VMEM((2 * rows, total), bf16),
            pltpu.VMEM((total, 6 * tile), bf16),
            pltpu.VMEM((36, 8, tile), f32),
        ],
        compiler_params=params(),
        cost_estimate=cost(8),
        name="magnetic_terms",
    )(live, conn, stiffness, mass_r, *arrays(blocks), *after)


def gather_kernel(count, steps, adds, live, conn, *refs):
    blocks = refs[:count]
    refs = refs[count:]
    if adds:
        earlier, refs = refs[0], refs[1:]
    out, done, values, hot = refs
    done[...] = jnp.zeros_like(done)
    tile = conn.shape[1]

    @pl.when(pl.program_id(0) == 0)
    def _():
        fill_values(values, blocks)

    bases = [base_of(step, block.shape[1]) for step, block in zip(steps, blocks)]
    fill_gather(hot, live_rows(conn, live, pl.program_id(0)), blocks, bases, tile)
    got = halves_sum(jnp.dot(values[...], hot[...], preferred_element_type=f32))
    out[...] = got + earlier[...] if adds else got


def gathered(blocks, steps, live, conn, earlier, us):
    rows = blocks[0].shape[0]
    elems = conn.shape[1]
    tile = ELEM_TILE
    total = sum(block.shape[1] for block in blocks)
    wide = pl.BlockSpec((rows, 6 * tile), lambda j: (0, j))
    adds = earlier is not None
    return pl.pallas_call(
        functools.partial(gather_kernel, len(blocks), steps, adds),
        grid=(elems // tile,),
        in_specs=[
            pl.BlockSpec(memory_space=pltpu.SMEM),
            pl.BlockSpec((6, tile), lambda j: (0, j)),
        ]
        + specs(blocks)
        + [wide] * adds,
        out_specs=[wide, whole_block((8, 128))],
        out_shape=[
            jax.ShapeDtypeStruct((rows, 6 * elems), f32),
            jax.ShapeDtypeStruct((8, 128), f32),
        ],
        scratch_shapes=[
            pltpu.VMEM((2 * rows, total), bf16),
            pltpu.VMEM((total, 6 * tile), bf16),
        ],
        compiler_params=params(),
        cost_estimate=cost(us),
        name="gathered",
    )(live, conn, *arrays(blocks), *([earlier] * adds))


def fill_scatter(hot, conn_columns, first, tile):
    iota = lax.broadcasted_iota(jnp.int32, (tile, hot.shape[1]), 1)
    for corner in range(6):
        hot[corner * tile : (corner + 1) * tile, :] = one_hot(
            iota, conn_columns[:, corner : corner + 1] - first
        )


def ghost_terms_kernel(
    first, live, conn, coupling, magnetic_part, electric_part, left, right,
    terms, left_sums, right_sums, values, hot, hot_columns, total_sums
):
    step = pl.program_id(0)
    tile = conn.shape[1]
    cap = left.shape[1]

    @pl.when(step == 0)
    def _():
        fill_values(values, (left, right))
        total_sums[...] = jnp.zeros_like(total_sums)

    ids = live_rows(conn, live, step)
    fill_gather(hot, ids, (left, right), (first, first + cap), tile)
    got = electric_part[...] + halves_sum(
        jnp.dot(values[...], hot[...], preferred_element_type=f32)
    )
    rows = got.shape[0]
    for low in range(0, rows, 16):
        for a in range(6):
            at = slice(a * tile, (a + 1) * tile)
            total = -magnetic_part[low : low + 16, at]
            for b in range(6):
                total = total + coupling[a, b : b + 1, :] * got[low : low + 16, b * tile : (b + 1) * tile]
            high = total.astype(bf16)
            terms[low : low + 16, at] = high
            terms[rows + low : rows + low + 16, at] = (total - high.astype(f32)).astype(bf16)
    fill_scatter(hot_columns, columns_of(ids), first, tile)
    total_sums[...] += halves_sum(
        jnp.dot(terms[...], hot_columns[...], preferred_element_type=f32)
    )

    @pl.when(step == pl.num_programs(0) - 1)
    def _():
        left_sums[...] = total_sums[:, :cap]
        right_sums[...] = total_sums[:, cap:]


def ghost_terms(first, live, conn, coupling, magnetic_part, electric_part, left, right):
    rows, cap = left.shape
    elems = conn.shape[1]
    tile = ELEM_TILE
    wide = pl.BlockSpec((rows, 6 * tile), lambda j: (0, j))
    return pl.pallas_call(
        functools.partial(ghost_terms_kernel, first),
        grid=(elems // tile,),
        in_specs=[
            pl.BlockSpec(memory_space=pltpu.SMEM),
            pl.BlockSpec((6, tile), lambda j: (0, j)),
            pl.BlockSpec((6, 6, tile), lambda j: (0, 0, j)),
            wide,
            wide,
            whole_block((rows, cap)),
            whole_block((rows, cap)),
        ],
        out_specs=[
            pl.BlockSpec((2 * rows, 6 * tile), lambda j: (0, j)),
            whole_block((rows, cap)),
            whole_block((rows, cap)),
        ],
        out_shape=[
            jax.ShapeDtypeStruct((2 * rows, 6 * elems), bf16),
            jax.ShapeDtypeStruct((rows, cap), f32),
            jax.ShapeDtypeStruct((rows, cap), f32),
        ],
        scratch_shapes=[
            pltpu.VMEM((2 * rows, 2 * cap), bf16),
            pltpu.VMEM((2 * cap, 6 * tile), bf16),
            pltpu.VMEM((6 * tile, 2 * cap), bf16),
            pltpu.VMEM((rows, 2 * cap), f32),
        ],
        compiler_params=params(),
        cost_estimate=cost(8),
        name="ghost_terms",
    )(live, conn, coupling, magnetic_part, electric_part, left, right)


def own_sums_kernel(live, conn, terms, out, hot):
    @pl.when(pl.program_id(0) == 0)
    def _():
        out[...] = jnp.zeros_like(out)

    columns = columns_of(live_rows(conn, live, pl.program_id(0)))
    fill_scatter(hot, columns, 0, conn.shape[1])
    out[...] += halves_sum(jnp.dot(terms[...], hot[...], preferred_element_type=f32))


def own_sums(live, conn, terms, nodes):
    rows = terms.shape[0] // 2
    tile = ELEM_TILE
    elems = conn.shape[1]
    return pl.pallas_call(
        own_sums_kernel,
        grid=(elems // tile,),
        in_specs=[
            pl.BlockSpec(memory_space=pltpu.SMEM),
            pl.BlockSpec((6, tile), lambda j: (0, j)),
            pl.BlockSpec((2 * rows, 6 * tile), lambda j: (0, j)),
        ],
        out_specs=whole_block((rows, nodes)),
        out_shape=jax.ShapeDtypeStruct((rows, nodes), f32),
        scratch_shapes=[pltpu.VMEM((6 * tile, nodes), bf16)],
        compiler_params=params(),
        cost_estimate=cost(9),
        name="own_sums",
    )(live, conn, terms)


def finish_kernel(counts, interface, magnetic, sums, left, right, inv_mass, out):
    width = interface.shape[1]
    nodes = out.shape[1]
    iota = lax.broadcasted_iota(jnp.int32, (width, nodes), 1)
    hot = one_hot(iota, columns_of(interface_ids(interface, counts))[:, :1])
    values = jnp.concatenate([split_rows(left[...]), split_rows(right[...])], 1)
    extra = halves_sum(jnp.dot(values, hot, preferred_element_type=f32))
    out[...] = magnetic[...] + time_step * inv_mass[...] * (sums[...] + extra)


def finish(counts, interface, magnetic, sums, left, right, inv_mass):
    return pl.pallas_call(
        finish_kernel,
        in_specs=[pl.BlockSpec(memory_space=pltpu.SMEM)]
        + [pl.BlockSpec(memory_space=pltpu.VMEM)] * 6,
        out_shape=jax.ShapeDtypeStruct(magnetic.shape, f32),
        compiler_params=params(),
        cost_estimate=cost(3),
        name="finish",
    )(counts, interface, magnetic, sums, left, right, inv_mass)


def between_chips(blocks):
    members = lax.axis_size("mode")
    order = sorted(range(1, members // 2), key=lambda t: -t)
    got = {
        t: lax.ppermute(blocks[t], "mode", [(k, k ^ (2 * t)) for k in range(members)])
        for t in order
    }
    return [blocks[0]] + [got[t] for t in range(1, members // 2)]


def between_cores(blocks, after):
    members = lax.axis_size("mode")
    return lax.ppermute(lower_halves(blocks, after), "mode", [(k, k ^ 1) for k in range(members)])


def neighbours(to_left, to_right):
    count = lax.axis_size("mesh")
    from_left = lax.ppermute(to_right, "mesh", [(i, i + 1) for i in range(count - 1)])
    from_right = lax.ppermute(to_left, "mesh", [(i + 1, i) for i in range(count - 1)])
    return from_left, from_right


def on_device(
    magnetic, velocity, stiffness, mass_r, coupling, inv_mass, connect, interface, counts, elem_live
):
    fields, vector_parts, mode_dev, node_dev = magnetic.shape
    rows = fields * vector_parts * mode_dev
    cap = interface.shape[1] // 2
    members = lax.axis_size("mode")
    slab = node_dev // members
    values = magnetic.reshape(rows, node_dev)

    packed = pack(values, members, slab)
    kept = between_chips(packed)
    own = Block(values, rows)
    mag_left, mag_right = neighbours(
        *interface_values([own], None, counts, interface, 1, (packed[0],))
    )
    extended = [own, Block(mag_left, rows), Block(mag_right, rows)]
    swapped = between_cores(kept, (mag_left, mag_right))
    arrived = []
    for t, block in enumerate(kept):
        arrived += [Block(block, rows), Block(swapped, rows, t)]
    inverse, forward = transform_tables(mode_dev, members)
    sent = transform(arrived, velocity, inverse, forward, mode_dev, fields)
    kept = between_chips(sent)
    magnetic_part, done = magnetic_terms(
        extended, mode_dev, elem_live, connect, stiffness, mass_r, (sent[0],)
    )
    swapped = between_cores(kept, (done,))
    electric = []
    for t, block in enumerate(kept):
        electric += [Block(block, rows), Block(swapped, rows, t)]
    steps = tuple(range(members))
    ele_left, ele_right = neighbours(*interface_values(electric, steps, counts, interface, 1))
    electric_part, _ = gathered(electric, steps, elem_live, connect, None, 4)
    terms, left_sums, right_sums = ghost_terms(
        node_dev, elem_live, connect, coupling, magnetic_part, electric_part, ele_left, ele_right
    )
    sum_left, sum_right = neighbours(left_sums, right_sums)
    sums = own_sums(elem_live, connect, terms, node_dev)
    out = finish(counts, interface, values, sums, sum_left, sum_right, inv_mass[None, :])
    return out.reshape(magnetic.shape)


def solution(mesh):
    return jax.shard_map(
        on_device,
        mesh=mesh,
        in_specs=(
            P(None, None, "mode", "mesh"),
            P(None, None, ("mesh", "mode")),
            P(None, None, "mesh"),
            P(None, None, "mesh"),
            P(None, None, "mesh"),
            P("mesh"),
            P(None, "mesh"),
            P("mesh", None),
            P("mesh", None),
            P("mesh"),
        ),
        out_specs=P(None, None, "mode", "mesh"),
        check_vma=False,
    )
```

time: 96.2 us -> 85 us (0.88)
  the two profiles are of different devices: /device:TPU:12 before, /device:TPU:20 now
where the time goes in v2:
time: 85 us; the launch traced here: 84.7 us
  Pallas kernels  34.1 us (40%)
  starting transfers between devices  27.6 us (32%)
  waiting for transfers between devices  19.5 us (23%)
  local copies, waits for them, and re-layouts  2.53 us (3%)
  between operations  0.94 us (1%)
    ppermute x6, waiting for transfers between devices, between_chips(): lax.ppermute(blocks[t], 'mode', [(k, k ^ 2 * t) for k in range(members)])  12.9 us
    ppermute x3, starting transfers between devices, neighbours(): lax.ppermute(to_left, 'mesh', [(i + 1, i) for i in range(count - 1)])  10.9 us
    ppermute x3, starting transfers between devices, neighbours(): lax.ppermute(to_right, 'mesh', [(i, i + 1) for i in range(count - 1)])  9.41 us
    pallas_call x1, Pallas kernels, magnetic_terms(): pl.pallas_call(functools.partial(magnetic_terms_kernel, len(blocks), mode...  8.04 us
    ppermute x6, starting transfers between devices, between_chips(): lax.ppermute(blocks[t], 'mode', [(k, k ^ 2 * t) for k in range(members)])  7.1 us
    pallas_call x1, Pallas kernels, own_sums(): pl.pallas_call(own_sums_kernel, grid=(elems // tile,), in_specs=[pl.Block...  6.81 us
    pallas_call x1, Pallas kernels, gathered(): pl.pallas_call(functools.partial(gather_kernel, len(blocks), steps, adds)...  6.61 us
    pallas_call x1, Pallas kernels, ghost_terms(): pl.pallas_call(functools.partial(ghost_terms_kernel, first), grid=(elems...  5.68 us
  transfers between devices with their start and end apart: 14, of which 7 were waited for; matrix products, arithmetic and copies ran while one was open for 0% of the time, Pallas kernels for 27%

profile of v2, /device:TPU:20, one launch (start us, length us, event | category | flops | bytes accessed | tf_op | source)
XLA Modules:
  0.0 84.7 jit_solution(5790575355774716743)
XLA Ops:
  0.0 1.1 %copy-done = f32[2,6,8,2048]{3,2,1,0:T(8,128)S(1)} copy-done((f32[2,6,8,2048]{3,2,1,0:T(8,128)S(1)}, f32[2,6,8,2048]{3,2,1,0:T(8,128)}, u32[]{:S(2)}) %copy-start) | copy-done | bytes 786456
  1.1 0.2 pack.1
  1.4 1.6 %collective-permute-start.2 = (f32[192,256]{1,0:T(8,128)S(1)}, f32[192,256]{1,0:T(8,128)S(1)}, u32[]{:S(2)}, u32[]{:S(2)}) collective-permute-start(f32[192,256]{1,0:T(8,128)S(1)} %get-tuple-element.26), channel_id=1, source_target_pairs={{0,2},{1,3},{2,0},{3,1},{4,6},{5,7},{6,4},{7,5},{8,10},{9,11},{10,... | collective-permute-start | bytes 589832 | tf_op jit(solution)/shard_map/ppermute | solution.py:542
  3.0 0.3 collective-permute-start.3
  3.3 1.6 %collective-permute-start.4 = (f32[192,256]{1,0:T(8,128)S(1)}, f32[192,256]{1,0:T(8,128)S(1)}, u32[]{:S(2)}, u32[]{:S(2)}) collective-permute-start(f32[192,256]{1,0:T(8,128)S(1)} %get-tuple-element.28), channel_id=1, source_target_pairs={{0,6},{1,7},{2,4},{3,5},{4,2},{5,3},{6,0},{7,1},{8,14},{9,15},{10,... | collective-permute-start | bytes 589832 | tf_op jit(solution)/shard_map/ppermute | solution.py:542
  4.9 0.7 copy-done.9
  5.6 0.7 copy-done.12
  6.2 1.3 %interface_values.2 = (f32[96,256]{1,0:T(8,128)S(1)}, f32[96,256]{1,0:T(8,128)S(1)}) custom-call(s32[1,2]{1,0:T(1,128)S(1)} %copy-done.12, s32[1,512]{1,0:T(1,128)S(1)} %copy-done.9, f32[96,2048]{1,0:T(8,128)S(1)} %bitcast.4, f32[192,256]{1,0:T(8,128)S(1)} %get-tuple-element.23.refs_1_.refs_0_.refs_3_), custom_call_target="tpu_custom_call" | custom-call | bytes 3000000 | tf_op jit(solution)/shard_map/interface_values/pallas_call | solution.py:244
  7.6 3.5 %collective-permute-start = (f32[96,256]{1,0:T(8,128)S(1)}, f32[96,256]{1,0:T(8,128)S(1)}, u32[]{:S(2)}, u32[]{:S(2)}) collective-permute-start(f32[96,256]{1,0:T(8,128)S(1)} %get-tuple-element.24), channel_id=1, source_target_pairs={{0,8},{8,16},{16,24},{1,9},{9,17},{17,25},{2,10},{10,18},{18,26},{... | collective-permute-start | bytes 294920 | tf_op jit(solution)/shard_map/ppermute | solution.py:555
  11.1 3.3 %collective-permute-start.1 = (f32[96,256]{1,0:T(8,128)S(1)}, f32[96,256]{1,0:T(8,128)S(1)}, u32[]{:S(2)}, u32[]{:S(2)}) collective-permute-start(f32[96,256]{1,0:T(8,128)S(1)} %get-tuple-element.25), channel_id=1, source_target_pairs={{8,0},{16,8},{24,16},{9,1},{17,9},{25,17},{10,2},{18,10},{26,18},{... | collective-permute-start | bytes 294920 | tf_op jit(solution)/shard_map/ppermute | solution.py:556
  14.5 1.5 %collective-permute-done.refs_4_.refs_1_ = f32[96,256]{1,0:T(8,128)S(1)} collective-permute-done((f32[96,256]{1,0:T(8,128)S(1)}, f32[96,256]{1,0:T(8,128)S(1)}, u32[]{:S(2)}, u32[]{:S(2)}) %collective-permute-start) | collective-permute-done | bytes 98336 | tf_op jit(solution)/shard_map/ppermute | solution.py:555
  16.0 1.7 %collective-permute-done.1.refs_5_.refs_2_ = f32[96,256]{1,0:T(8,128)S(1)} collective-permute-done((f32[96,256]{1,0:T(8,128)S(1)}, f32[96,256]{1,0:T(8,128)S(1)}, u32[]{:S(2)}, u32[]{:S(2)}) %collective-permute-start.1) | collective-permute-done | bytes 98336 | tf_op jit(solution)/shard_map/ppermute | solution.py:556
  17.6 4.3 %collective-permute-done.4.refs_3_.refs_9_ = f32[192,256]{1,0:T(8,128)S(1)} collective-permute-done((f32[192,256]{1,0:T(8,128)S(1)}, f32[192,256]{1,0:T(8,128)S(1)}, u32[]{:S(2)}, u32[]{:S(2)}) %collective-permute-start.4) | collective-permute-done | bytes 196640 | tf_op jit(solution)/shard_map/ppermute | solution.py:542
  21.9 0.5 lower_halves.2
  22.5 1.7 %collective-permute-done.5.refs_4_.refs_6_.refs_8_.refs_10_ = f32[384,256]{1,0:T(8,128)S(1)} collective-permute-done((f32[384,256]{1,0:T(8,128)S(1)}, f32[384,256]{1,0:T(8,128)S(1)}, u32[]{:S(2)}, u32[]{:S(2)}) %collective-permute-start.5) | collective-permute-done | bytes 393248 | tf_op jit(solution)/shard_map/ppermute | solution.py:550
  24.3 1.0 %transform.1 = (f32[192,256]{1,0:T(8,128)S(1)}, f32[192,256]{1,0:T(8,128)S(1)}, f32[192,256]{1,0:T(8,128)S(1)}, f32[192,256]{1,0:T(8,128)S(1)}) custom-call(f32[128,128]{1,0:T(8,128)S(1)} %copy-done.8, f32[128,128]{1,0:T(8,128)S(1)} %copy-done.7, f32[3,128,256]{2,1,0:T(8,128)S(1)} %copy-done.3, f32[192,256]{1,0:T(8,128)S(1)} %get-tuple-element.23.refs_1_.refs_0_.refs_3_, ...), custom_call_target="tpu_custom_call" | custom-call | bytes 3000000 | tf_op jit(solution)/shard_map/transform/pallas_call | solution.py:135
  25.4 1.9 %collective-permute-start.7 = (f32[192,256]{1,0:T(8,128)S(1)}, f32[192,256]{1,0:T(8,128)S(1)}, u32[]{:S(2)}, u32[]{:S(2)}) collective-permute-start(f32[192,256]{1,0:T(8,128)S(1)} %get-tuple-element.32), channel_id=1, source_target_pairs={{0,4},{1,5},{2,6},{3,7},{4,0},{5,1},{6,2},{7,3},{8,12},{9,13},{10,... | collective-permute-start | bytes 589832 | tf_op jit(solution)/shard_map/ppermute | solution.py:542
  27.3 1.6 %collective-permute-start.8 = (f32[192,256]{1,0:T(8,128)S(1)}, f32[192,256]{1,0:T(8,128)S(1)}, u32[]{:S(2)}, u32[]{:S(2)}) collective-permute-start(f32[192,256]{1,0:T(8,128)S(1)} %get-tuple-element.33), channel_id=1, source_target_pairs={{0,6},{1,7},{2,4},{3,5},{4,2},{5,3},{6,0},{7,1},{8,14},{9,15},{10,... | collective-permute-start | bytes 589832 | tf_op jit(solution)/shard_map/ppermute | solution.py:542
  29.5 8.0 %magnetic_terms.1 = (f32[96,6144]{1,0:T(8,128)S(1)}, f32[8,128]{1,0:T(8,128)S(1)}) custom-call(s32[1]{0:T(128)S(6)} %copy.13.live, s32[6,1024]{1,0:T(8,128)S(1)} %copy-done.2, f32[6,6,1024]{2,1,0:T(8,128)S(1)} %copy-done.4, f32[6,6,1024]{2,1,0:T(8,128)S(1)} %copy-done.5, f32[96,2048]{1,0:T(8,128)S(1)} %bitcast.5, ...), custom_call_target="tpu_custom_call" | custom-call | bytes 24000000 | tf_op jit(solution)/shard_map/magnetic_terms/pallas_call | solution.py:322
  37.6 3.4 %collective-permute-done.7.refs_2_.refs_4_ = f32[192,256]{1,0:T(8,128)S(1)} collective-permute-done((f32[192,256]{1,0:T(8,128)S(1)}, f32[192,256]{1,0:T(8,128)S(1)}, u32[]{:S(2)}, u32[]{:S(2)}) %collective-permute-start.7) | collective-permute-done | bytes 196640 | tf_op jit(solution)/shard_map/ppermute | solution.py:542
  41.0 5.2 %collective-permute-done.8.refs_3_.refs_6_ = f32[192,256]{1,0:T(8,128)S(1)} collective-permute-done((f32[192,256]{1,0:T(8,128)S(1)}, f32[192,256]{1,0:T(8,128)S(1)}, u32[]{:S(2)}, u32[]{:S(2)}) %collective-permute-start.8) | collective-permute-done | bytes 196640 | tf_op jit(solution)/shard_map/ppermute | solution.py:542
  46.2 0.5 lower_halves.3
  46.8 1.7 %collective-permute-done.9.refs_1_.refs_3_.refs_5_.refs_7_ = f32[384,256]{1,0:T(8,128)S(1)} collective-permute-done((f32[384,256]{1,0:T(8,128)S(1)}, f32[384,256]{1,0:T(8,128)S(1)}, u32[]{:S(2)}, u32[]{:S(2)}) %collective-permute-start.9) | collective-permute-done | bytes 393248 | tf_op jit(solution)/shard_map/ppermute | solution.py:550
  48.5 1.2 %interface_values.3 = (f32[96,256]{1,0:T(8,128)S(1)}, f32[96,256]{1,0:T(8,128)S(1)}) custom-call(s32[1,2]{1,0:T(1,128)S(1)} %copy-done.12, s32[1,512]{1,0:T(1,128)S(1)} %copy-done.10, f32[192,256]{1,0:T(8,128)S(1)} %get-tuple-element.29.refs_3_.refs_0_, f32[384,256]{1,0:T(8,128)S(1)} %collective-permute-done.9.refs_1_.refs_3_.refs_5_.refs_7_, ...), custom_call_target="tpu_custom_call" | custom-call | bytes 3000000 | tf_op jit(solution)/shard_map/interface_values/pallas_call | solution.py:244
  49.7 3.4 %collective-permute-start.10 = (f32[96,256]{1,0:T(8,128)S(1)}, f32[96,256]{1,0:T(8,128)S(1)}, u32[]{:S(2)}, u32[]{:S(2)}) collective-permute-start(f32[96,256]{1,0:T(8,128)S(1)} %get-tuple-element.36), channel_id=1, source_target_pairs={{0,8},{8,16},{16,24},{1,9},{9,17},{17,25},{2,10},{10,18},{18,26},{... | collective-permute-start | bytes 294920 | tf_op jit(solution)/shard_map/ppermute | solution.py:555
  53.1 3.4 %collective-permute-start.11 = (f32[96,256]{1,0:T(8,128)S(1)}, f32[96,256]{1,0:T(8,128)S(1)}, u32[]{:S(2)}, u32[]{:S(2)}) collective-permute-start(f32[96,256]{1,0:T(8,128)S(1)} %get-tuple-element.37), channel_id=1, source_target_pairs={{8,0},{16,8},{24,16},{9,1},{17,9},{25,17},{10,2},{18,10},{26,18},{... | collective-permute-start | bytes 294920 | tf_op jit(solution)/shard_map/ppermute | solution.py:556
  56.4 6.6 %gathered.1 = (f32[96,6144]{1,0:T(8,128)S(1)}, f32[8,128]{1,0:T(8,128)}) custom-call(s32[1]{0:T(128)S(6)} %copy.13.live, s32[6,1024]{1,0:T(8,128)S(1)} %copy-done.2, f32[192,256]{1,0:T(8,128)S(1)} %get-tuple-element.29.refs_3_.refs_0_, f32[384,256]{1,0:T(8,128)S(1)} %collective-permute-done.9.refs_1_.refs_3_.refs_5_.refs_7_, ...), custom_call_target="tpu_custom_call" | custom-call | bytes 12000000 | tf_op jit(solution)/shard_map/gathered/pallas_call | solution.py:375
  63.1 5.7 %ghost_terms.1 = (bf16[192,6144]{1,0:T(8,128)(2,1)S(1)}, f32[96,256]{1,0:T(8,128)S(1)}, f32[96,256]{1,0:T(8,128)S(1)}) custom-call(s32[1]{0:T(128)S(6)} %copy.13.live, s32[6,1024]{1,0:T(8,128)S(1)} %copy-done.2, f32[6,6,1024]{2,1,0:T(8,128)S(1)} %copy-done.6, f32[96,6144]{1,0:T(8,128)S(1)} %get-tuple-element.30.magnetic_part, ...), custom_call_target="tpu_custom_call" | custom-call | bytes 24000000 | tf_op jit(solution)/shard_map/ghost_terms/pallas_call | solution.py:451
  68.8 2.5 %collective-permute-start.12 = (f32[96,256]{1,0:T(8,128)S(1)}, f32[96,256]{1,0:T(8,128)S(1)}, u32[]{:S(2)}, u32[]{:S(2)}) collective-permute-start(f32[96,256]{1,0:T(8,128)S(1)} %get-tuple-element.39), channel_id=1, source_target_pairs={{0,8},{8,16},{16,24},{1,9},{9,17},{17,25},{2,10},{10,18},{18,26},{... | collective-permute-start | bytes 294920 | tf_op jit(solution)/shard_map/ppermute | solution.py:555
  71.3 4.3 %collective-permute-start.13 = (f32[96,256]{1,0:T(8,128)S(1)}, f32[96,256]{1,0:T(8,128)S(1)}, u32[]{:S(2)}, u32[]{:S(2)}) collective-permute-start(f32[96,256]{1,0:T(8,128)S(1)} %get-tuple-element.40), channel_id=1, source_target_pairs={{8,0},{16,8},{24,16},{9,1},{17,9},{25,17},{10,2},{18,10},{26,18},{... | collective-permute-start | bytes 294920 | tf_op jit(solution)/shard_map/ppermute | solution.py:556
  75.5 6.8 %own_sums.1.sums = f32[96,2048]{1,0:T(8,128)S(1)} custom-call(s32[1]{0:T(128)S(6)} %copy.13.live, s32[6,1024]{1,0:T(8,128)S(1)} %copy-done.2, bf16[192,6144]{1,0:T(8,128)(2,1)S(1)} %get-tuple-element.38.terms), custom_call_target="tpu_custom_call" | custom-call | bytes 27000000 | tf_op jit(solution)/shard_map/own_sums/pallas_call | solution.py:499
  82.4 2.3 %finish.1 = f32[96,2048]{1,0:T(8,128)} custom-call(s32[1,2]{1,0:T(1,128)S(1)} %copy-done.13, s32[1,512]{1,0:T(1,128)S(1)} %copy-done.10, f32[96,2048]{1,0:T(8,128)S(1)} %bitcast.6, f32[96,2048]{1,0:T(8,128)S(1)} %own_sums.1.sums, f32[96,256]{1,0:T(8,128)S(1)} %collective-permute-done.12.left, f32[96,256]{1,0:T(8,128)S(1)} %collective-permute-done.13.right, ...), custom_call_target="tpu_custom_call" | custom-call | bytes 9000000 | tf_op jit(solution)/shard_map/finish/pallas_call | solution.py:527
  (35 shorter events, 0.3 us)
Async XLA Ops:
  0.0 1.1 %copy-start = (f32[2,6,8,2048]{3,2,1,0:T(8,128)S(1)}, f32[2,6,8,2048]{3,2,1,0:T(8,128)}, u32[]{:S(2)}) copy-start(f32[2,6,8,2048]{3,2,1,0:T(8,128)} %param.12) | copy-start | bytes 2359300
  1.1 23.1 %copy-start.3 = (f32[3,128,256]{2,1,0:T(8,128)S(1)}, f32[3,128,256]{2,1,0:T(8,128)}, u32[]{:S(2)}) copy-start(f32[3,128,256]{2,1,0:T(8,128)} %refs_2_.1) | copy-start | bytes 1179652
  1.1 23.1 %copy-start.7 = (f32[128,128]{1,0:T(8,128)S(1)}, f32[128,128]{1,0:T(8,128)}, u32[]{:S(2)}) copy-start(f32[128,128]{1,0:T(8,128)} %constant.5.clone.refs_1_) | copy-start | bytes 196612
  1.1 23.1 %copy-start.8 = (f32[128,128]{1,0:T(8,128)S(1)}, f32[128,128]{1,0:T(8,128)}, u32[]{:S(2)}) copy-start(f32[128,128]{1,0:T(8,128)} %constant.4.clone.refs_0_) | copy-start | bytes 196612
  1.4 16.3 %collective-permute-start.2 = (f32[192,256]{1,0:T(8,128)S(1)}, f32[192,256]{1,0:T(8,128)S(1)}, u32[]{:S(2)}, u32[]{:S(2)}) collective-permute-start(f32[192,256]{1,0:T(8,128)S(1)} %get-tuple-element.26), channel_id=1, source_target_pairs={{0,2},{1,3},{2,0},{3,1},{4,6},{5,7},{6,4},{7,5},{8,10},{9,11},{10,... | collective-permute-start | bytes 589832 | tf_op jit(solution)/shard_map/ppermute | solution.py:542
  3.0 14.6 %collective-permute-start.3 = (f32[192,256]{1,0:T(8,128)S(1)}, f32[192,256]{1,0:T(8,128)S(1)}, u32[]{:S(2)}, u32[]{:S(2)}) collective-permute-start(f32[192,256]{1,0:T(8,128)S(1)} %get-tuple-element.27), channel_id=1, source_target_pairs={{0,4},{1,5},{2,6},{3,7},{4,0},{5,1},{6,2},{7,3},{8,12},{9,13},{10,... | collective-permute-start | bytes 589832 | tf_op jit(solution)/shard_map/ppermute | solution.py:542
  3.3 18.6 %collective-permute-start.4 = (f32[192,256]{1,0:T(8,128)S(1)}, f32[192,256]{1,0:T(8,128)S(1)}, u32[]{:S(2)}, u32[]{:S(2)}) collective-permute-start(f32[192,256]{1,0:T(8,128)S(1)} %get-tuple-element.28), channel_id=1, source_target_pairs={{0,6},{1,7},{2,4},{3,5},{4,2},{5,3},{6,0},{7,1},{8,14},{9,15},{10,... | collective-permute-start | bytes 589832 | tf_op jit(solution)/shard_map/ppermute | solution.py:542
  4.9 0.7 copy-start.9
  5.6 0.7 copy-start.12
  7.5 22.0 %copy-start.1 = (f32[2,6,8,2048]{3,2,1,0:T(8,128)S(1)}, f32[2,6,8,2048]{3,2,1,0:T(8,128)}, u32[]{:S(2)}) copy-start(f32[2,6,8,2048]{3,2,1,0:T(8,128)} %param.12) | copy-start | bytes 2359300
  7.5 22.0 %copy-start.2 = (s32[6,1024]{1,0:T(8,128)S(1)}, s32[6,1024]{1,0:T(8,128)}, u32[]{:S(2)}) copy-start(s32[6,1024]{1,0:T(8,128)} %conn.7) | copy-start | bytes 73732
  7.5 22.0 %copy-start.4 = (f32[6,6,1024]{2,1,0:T(8,128)S(1)}, f32[6,6,1024]{2,1,0:T(8,128)}, u32[]{:S(2)}) copy-start(f32[6,6,1024]{2,1,0:T(8,128)} %stiffness.1) | copy-start | bytes 442372
  7.6 22.0 %copy-start.5 = (f32[6,6,1024]{2,1,0:T(8,128)S(1)}, f32[6,6,1024]{2,1,0:T(8,128)}, u32[]{:S(2)}) copy-start(f32[6,6,1024]{2,1,0:T(8,128)} %mass_r.1) | copy-start | bytes 442372
  7.6 8.4 %collective-permute-start = (f32[96,256]{1,0:T(8,128)S(1)}, f32[96,256]{1,0:T(8,128)S(1)}, u32[]{:S(2)}, u32[]{:S(2)}) collective-permute-start(f32[96,256]{1,0:T(8,128)S(1)} %get-tuple-element.24), channel_id=1, source_target_pairs={{0,8},{8,16},{16,24},{1,9},{9,17},{17,25},{2,10},{10,18},{18,26},{... | collective-permute-start | bytes 294920 | tf_op jit(solution)/shard_map/ppermute | solution.py:555
  11.1 6.5 %collective-permute-start.1 = (f32[96,256]{1,0:T(8,128)S(1)}, f32[96,256]{1,0:T(8,128)S(1)}, u32[]{:S(2)}, u32[]{:S(2)}) collective-permute-start(f32[96,256]{1,0:T(8,128)S(1)} %get-tuple-element.25), channel_id=1, source_target_pairs={{8,0},{16,8},{24,16},{9,1},{17,9},{25,17},{10,2},{18,10},{26,18},{... | collective-permute-start | bytes 294920 | tf_op jit(solution)/shard_map/ppermute | solution.py:556
  22.5 26.1 %copy-start.10 = (s32[1,512]{1,0:T(1,128)S(1)}, s32[1,512]{1,0:T(1,128)}, u32[]{:S(2)}) copy-start(s32[1,512]{1,0:T(1,128)} %interface.5) | copy-start | bytes 6148
  22.5 1.8 %collective-permute-start.5 = (f32[384,256]{1,0:T(8,128)S(1)}, f32[384,256]{1,0:T(8,128)S(1)}, u32[]{:S(2)}, u32[]{:S(2)}) collective-permute-start(f32[384,256]{1,0:T(8,128)S(1)} %lower_halves.2), channel_id=1, source_target_pairs={{0,1},{1,0},{2,3},{3,2},{4,5},{5,4},{6,7},{7,6},{8,9},{9,8},{10,11... | collective-permute-start | bytes 1179656 | tf_op jit(solution)/shard_map/ppermute | solution.py:550
  25.3 12.3 %collective-permute-start.6 = (f32[192,256]{1,0:T(8,128)S(1)}, f32[192,256]{1,0:T(8,128)S(1)}, u32[]{:S(2)}, u32[]{:S(2)}) collective-permute-start(f32[192,256]{1,0:T(8,128)S(1)} %get-tuple-element.31), channel_id=1, source_target_pairs={{0,2},{1,3},{2,0},{3,1},{4,6},{5,7},{6,4},{7,5},{8,10},{9,11},{10,... | collective-permute-start | bytes 589832 | tf_op jit(solution)/shard_map/ppermute | solution.py:542
  25.4 15.6 %collective-permute-start.7 = (f32[192,256]{1,0:T(8,128)S(1)}, f32[192,256]{1,0:T(8,128)S(1)}, u32[]{:S(2)}, u32[]{:S(2)}) collective-permute-start(f32[192,256]{1,0:T(8,128)S(1)} %get-tuple-element.32), channel_id=1, source_target_pairs={{0,4},{1,5},{2,6},{3,7},{4,0},{5,1},{6,2},{7,3},{8,12},{9,13},{10,... | collective-permute-start | bytes 589832 | tf_op jit(solution)/shard_map/ppermute | solution.py:542
  27.3 18.9 %collective-permute-start.8 = (f32[192,256]{1,0:T(8,128)S(1)}, f32[192,256]{1,0:T(8,128)S(1)}, u32[]{:S(2)}, u32[]{:S(2)}) collective-permute-start(f32[192,256]{1,0:T(8,128)S(1)} %get-tuple-element.33), channel_id=1, source_target_pairs={{0,6},{1,7},{2,4},{3,5},{4,2},{5,3},{6,0},{7,1},{8,14},{9,15},{10,... | collective-permute-start | bytes 589832 | tf_op jit(solution)/shard_map/ppermute | solution.py:542
  46.7 16.4 %copy-start.6 = (f32[6,6,1024]{2,1,0:T(8,128)S(1)}, f32[6,6,1024]{2,1,0:T(8,128)}, u32[]{:S(2)}) copy-start(f32[6,6,1024]{2,1,0:T(8,128)} %coupling.1) | copy-start | bytes 442372
  46.7 1.8 %collective-permute-start.9 = (f32[384,256]{1,0:T(8,128)S(1)}, f32[384,256]{1,0:T(8,128)S(1)}, u32[]{:S(2)}, u32[]{:S(2)}) collective-permute-start(f32[384,256]{1,0:T(8,128)S(1)} %lower_halves.3), channel_id=1, source_target_pairs={{0,1},{1,0},{2,3},{3,2},{4,5},{5,4},{6,7},{7,6},{8,9},{9,8},{10,11... | collective-permute-start | bytes 1179656 | tf_op jit(solution)/shard_map/ppermute | solution.py:550
  49.7 13.4 %collective-permute-start.10 = (f32[96,256]{1,0:T(8,128)S(1)}, f32[96,256]{1,0:T(8,128)S(1)}, u32[]{:S(2)}, u32[]{:S(2)}) collective-permute-start(f32[96,256]{1,0:T(8,128)S(1)} %get-tuple-element.36), channel_id=1, source_target_pairs={{0,8},{8,16},{16,24},{1,9},{9,17},{17,25},{2,10},{10,18},{18,26},{... | collective-permute-start | bytes 294920 | tf_op jit(solution)/shard_map/ppermute | solution.py:555
  53.1 10.0 %collective-permute-start.11 = (f32[96,256]{1,0:T(8,128)S(1)}, f32[96,256]{1,0:T(8,128)S(1)}, u32[]{:S(2)}, u32[]{:S(2)}) collective-permute-start(f32[96,256]{1,0:T(8,128)S(1)} %get-tuple-element.37), channel_id=1, source_target_pairs={{8,0},{16,8},{24,16},{9,1},{17,9},{25,17},{10,2},{18,10},{26,18},{... | collective-permute-start | bytes 294920 | tf_op jit(solution)/shard_map/ppermute | solution.py:556
  68.8 13.6 %copy-start.11 = (f32[2048]{0:T(1024)S(1)}, f32[2048]{0:T(1024)}, u32[]{:S(2)}) copy-start(f32[2048]{0:T(1024)} %param.17) | copy-start | bytes 24580
  68.8 13.6 %copy-start.13 = (s32[1,2]{1,0:T(1,128)S(1)}, s32[1,2]{1,0:T(1,128)}, u32[]{:S(2)}) copy-start(s32[1,2]{1,0:T(1,128)} %counts.5) | copy-start | bytes 28
  68.8 13.6 %collective-permute-start.12 = (f32[96,256]{1,0:T(8,128)S(1)}, f32[96,256]{1,0:T(8,128)S(1)}, u32[]{:S(2)}, u32[]{:S(2)}) collective-permute-start(f32[96,256]{1,0:T(8,128)S(1)} %get-tuple-element.39), channel_id=1, source_target_pairs={{0,8},{8,16},{16,24},{1,9},{9,17},{17,25},{2,10},{10,18},{18,26},{... | collective-permute-start | bytes 294920 | tf_op jit(solution)/shard_map/ppermute | solution.py:555
  71.3 11.1 %collective-permute-start.13 = (f32[96,256]{1,0:T(8,128)S(1)}, f32[96,256]{1,0:T(8,128)S(1)}, u32[]{:S(2)}, u32[]{:S(2)}) collective-permute-start(f32[96,256]{1,0:T(8,128)S(1)} %get-tuple-element.40), channel_id=1, source_target_pairs={{8,0},{16,8},{24,16},{9,1},{17,9},{25,17},{10,2},{18,10},{26,18},{... | collective-permute-start | bytes 294920 | tf_op jit(solution)/shard_map/ppermute | solution.py:556

commit v3 on v2

--- a/solution.py
+++ b/solution.py
@@ -39,8 +39,8 @@
     return [block.array for block in blocks]
 
 
-def params():
-    return pltpu.CompilerParams(vmem_limit_bytes=KERNEL_VMEM)
+def params(vmem=KERNEL_VMEM):
+    return pltpu.CompilerParams(vmem_limit_bytes=vmem)
 
 
 def cost(us):
@@ -145,11 +145,11 @@
     )(inverse, forward, velocity, *arrays(blocks))
 
 
-def pack_kernel(rows, slab, values, *refs):
-    outs, sems = refs[:-1], refs[-1]
+def pack_kernel(chips, rows, slab, values, *refs):
+    outs, sems = refs[-1 - len(chips) : -1], refs[-1]
     copies = []
-    for at in range(2 * len(outs)):
-        start = pl.multiple_of(base_of(at, slab), 128)
+    for at in range(2 * len(chips)):
+        start = pl.multiple_of(base_of(2 * chips[at // 2] + at % 2, slab), 128)
         half = at % 2
         copies.append(
             pltpu.make_async_copy(
@@ -164,19 +164,39 @@
         copy.wait()
 
 
-def pack(values, members, slab):
+def pack(values, chips, slab, after):
     rows = values.shape[0]
     anywhere = pl.BlockSpec(memory_space=pl.ANY)
     return pl.pallas_call(
-        functools.partial(pack_kernel, rows, slab),
-        in_specs=[anywhere],
-        out_specs=[anywhere] * (members // 2),
-        out_shape=[jax.ShapeDtypeStruct((2 * rows, slab), f32)] * (members // 2),
-        scratch_shapes=[pltpu.SemaphoreType.DMA((members,))],
-        compiler_params=params(),
-        cost_estimate=cost(1),
+        functools.partial(pack_kernel, chips, rows, slab),
+        in_specs=[pl.BlockSpec(memory_space=pltpu.HBM)] + [anywhere] * len(after),
+        out_specs=[anywhere] * len(chips),
+        out_shape=[jax.ShapeDtypeStruct((2 * rows, slab), f32)] * len(chips),
+        scratch_shapes=[pltpu.SemaphoreType.DMA((2 * len(chips),))],
+        compiler_params=params(),
+        cost_estimate=cost(0.5),
         name="pack",
-    )(values)
+    )(values, *after)
+
+
+def relay_kernel(source, *refs):
+    copy = pltpu.make_async_copy(source, refs[-2], refs[-1])
+    copy.start()
+    copy.wait()
+
+
+def relay(source, after):
+    anywhere = pl.BlockSpec(memory_space=pl.ANY)
+    return pl.pallas_call(
+        relay_kernel,
+        in_specs=[anywhere] * (1 + len(after)),
+        out_specs=anywhere,
+        out_shape=jax.ShapeDtypeStruct(source.shape, f32),
+        scratch_shapes=[pltpu.SemaphoreType.DMA],
+        compiler_params=params(),
+        cost_estimate=cost(0.5),
+        name="relay",
+    )(source, *after)
 
 
 def lower_halves_kernel(count, *refs):
@@ -209,17 +229,28 @@
     )(*blocks, *after)
 
 
+def even_partition():
+    return lax.rem(lax.axis_index("mesh"), 2) == 0
+
+
 def interface_ids(interface, counts):
     width = interface.shape[1]
     cap = width // 2
     lists = jnp.broadcast_to(interface[...], (8, width))
     shifted = pltpu.roll(lists, lax.rem(width - counts[0, 0], width), 1)
-    return jnp.concatenate([lists[:1, :cap], shifted[:1, :cap]], 1)
+    left, right = lists[:1, :cap], shifted[:1, :cap]
+    even = even_partition()
+    return jnp.concatenate([jnp.where(even, right, left), jnp.where(even, left, right)], 1)
+
+
+def by_partner(ids, first, cap):
+    swapped = jnp.where(ids < first + cap, ids + cap, ids - cap)
+    return jnp.where((ids >= first) & even_partition(), swapped, ids)
 
 
 def interface_kernel(count, steps, counts, interface, *refs):
     blocks = refs[:count]
-    left, right, hot = refs[-3:]
+    one, two, hot = refs[-3:]
     width = interface.shape[1]
     ids = interface_ids(interface, counts)
     row = 0
@@ -233,8 +264,8 @@
         row += size
     values = jnp.concatenate(stacked, 1)
     got = halves_sum(jnp.dot(values, hot[...], preferred_element_type=f32))
-    left[...] = got[:, : width // 2]
-    right[...] = got[:, width // 2 :]
+    one[...] = got[:, : width // 2]
+    two[...] = got[:, width // 2 :]
 
 
 def interface_values(blocks, steps, counts, interface, us, after=()):
@@ -295,7 +326,8 @@
     bases = [0]
     for block in blocks[:-1]:
         bases.append(bases[-1] + block.shape[1])
-    fill_gather(hot, live_rows(conn, live, pl.program_id(0)), blocks, bases, tile)
+    ids = by_partner(live_rows(conn, live, pl.program_id(0)), bases[1], blocks[1].shape[1])
+    fill_gather(hot, ids, blocks, bases, tile)
     lane = lax.broadcasted_iota(jnp.int32, (8, tile), 0)
     squares = (own_member() * mode_dev + lax.rem(lane, mode_dev)).astype(f32) ** 2
     got = halves_sum(jnp.dot(values[...], hot[...], preferred_element_type=f32))
@@ -417,7 +449,7 @@
         fill_values(values, (left, right))
         total_sums[...] = jnp.zeros_like(total_sums)
 
-    ids = live_rows(conn, live, step)
+    ids = by_partner(live_rows(conn, live, step), first, cap)
     fill_gather(hot, ids, (left, right), (first, first + cap), tile)
     got = electric_part[...] + halves_sum(
         jnp.dot(values[...], hot[...], preferred_element_type=f32)
@@ -513,26 +545,39 @@
     )(live, conn, terms)
 
 
-def finish_kernel(counts, interface, magnetic, sums, left, right, inv_mass, out):
-    width = interface.shape[1]
-    nodes = out.shape[1]
-    iota = lax.broadcasted_iota(jnp.int32, (width, nodes), 1)
-    hot = one_hot(iota, columns_of(interface_ids(interface, counts))[:, :1])
+def interface_hot_kernel(counts, interface, out):
+    iota = lax.broadcasted_iota(jnp.int32, out.shape, 1)
+    out[...] = one_hot(iota, columns_of(interface_ids(interface, counts))[:, :1])
+
+
+def interface_hot(counts, interface, nodes):
+    return pl.pallas_call(
+        interface_hot_kernel,
+        in_specs=[
+            pl.BlockSpec(memory_space=pltpu.SMEM),
+            pl.BlockSpec(memory_space=pltpu.VMEM),
+        ],
+        out_shape=jax.ShapeDtypeStruct((interface.shape[1], nodes), bf16),
+        compiler_params=params(),
+        cost_estimate=cost(1),
+        name="interface_hot",
+    )(counts, interface)
+
+
+def finish_kernel(hot, magnetic, sums, left, right, inv_mass, out):
     values = jnp.concatenate([split_rows(left[...]), split_rows(right[...])], 1)
-    extra = halves_sum(jnp.dot(values, hot, preferred_element_type=f32))
+    extra = halves_sum(jnp.dot(values, hot[...], preferred_element_type=f32))
     out[...] = magnetic[...] + time_step * inv_mass[...] * (sums[...] + extra)
 
 
-def finish(counts, interface, magnetic, sums, left, right, inv_mass):
+def finish(hot, magnetic, sums, left, right, inv_mass):
     return pl.pallas_call(
         finish_kernel,
-        in_specs=[pl.BlockSpec(memory_space=pltpu.SMEM)]
-        + [pl.BlockSpec(memory_space=pltpu.VMEM)] * 6,
         out_shape=jax.ShapeDtypeStruct(magnetic.shape, f32),
         compiler_params=params(),
-        cost_estimate=cost(3),
+        cost_estimate=cost(2),
         name="finish",
-    )(counts, interface, magnetic, sums, left, right, inv_mass)
+    )(hot, magnetic, sums, left, right, inv_mass)
 
 
 def between_chips(blocks):
@@ -550,11 +595,14 @@
     return lax.ppermute(lower_halves(blocks, after), "mode", [(k, k ^ 1) for k in range(members)])
 
 
-def neighbours(to_left, to_right):
+def neighbours(one, two):
     count = lax.axis_size("mesh")
-    from_left = lax.ppermute(to_right, "mesh", [(i, i + 1) for i in range(count - 1)])
-    from_right = lax.ppermute(to_left, "mesh", [(i + 1, i) for i in range(count - 1)])
-    return from_left, from_right
+    got = []
+    for values, start in ((one, 0), (two, 1)):
+        lower = range(start, count - 1, 2)
+        pairs = [(i, i + 1) for i in lower] + [(i + 1, i) for i in lower]
+        got.append(lax.ppermute(values, "mesh", pairs))
+    return got
 
 
 def on_device(
@@ -567,22 +615,26 @@
     slab = node_dev // members
     values = magnetic.reshape(rows, node_dev)
 
-    packed = pack(values, members, slab)
+    far = pack(values, tuple(range(2, members // 2)), slab, ())
+    near = pack(values, (0, 1), slab, (far[0],))
+    packed = near + far
     kept = between_chips(packed)
     own = Block(values, rows)
     mag_left, mag_right = neighbours(
         *interface_values([own], None, counts, interface, 1, (packed[0],))
     )
     extended = [own, Block(mag_left, rows), Block(mag_right, rows)]
-    swapped = between_cores(kept, (mag_left, mag_right))
+    hot = interface_hot(counts, interface, node_dev)
+    swapped = between_cores(kept, (mag_left, mag_right, hot))
     arrived = []
     for t, block in enumerate(kept):
         arrived += [Block(block, rows), Block(swapped, rows, t)]
     inverse, forward = transform_tables(mode_dev, members)
-    sent = transform(arrived, velocity, inverse, forward, mode_dev, fields)
+    sent = list(transform(arrived, velocity, inverse, forward, mode_dev, fields))
+    sent[1] = relay(sent[1], (sent[2],))
     kept = between_chips(sent)
     magnetic_part, done = magnetic_terms(
-        extended, mode_dev, elem_live, connect, stiffness, mass_r, (sent[0],)
+        extended, mode_dev, elem_live, connect, stiffness, mass_r, (sent[1],)
     )
     swapped = between_cores(kept, (done,))
     electric = []
@@ -596,7 +648,7 @@
     )
     sum_left, sum_right = neighbours(left_sums, right_sums)
     sums = own_sums(elem_live, connect, terms, node_dev)
-    out = finish(counts, interface, values, sums, sum_left, sum_right, inv_mass[None, :])
+    out = finish(hot, values, sums, sum_left, sum_right, inv_mass[None, :])
     return out.reshape(magnetic.shape)
 
 

time: 85 us -> 79.3 us (0.933)
  the two profiles are of different devices: /device:TPU:20 before, /device:TPU:0 now
where the time goes in v3:
time: 79.3 us; the launch traced here: 79 us
  Pallas kernels  34.8 us (44%)
  waiting for transfers between devices  20.5 us (26%)
  starting transfers between devices  19.2 us (24%)
  local copies, waits for them, and re-layouts  3.66 us (5%)
  between operations  0.94 us (1%)
    ppermute x6, waiting for transfers between devices, between_chips(): lax.ppermute(blocks[t], 'mode', [(k, k ^ 2 * t) for k in range(members)])  16 us
    ppermute x6, starting transfers between devices, neighbours(): got.append(lax.ppermute(values, 'mesh', pairs))  9.64 us
    ppermute x6, starting transfers between devices, between_chips(): lax.ppermute(blocks[t], 'mode', [(k, k ^ 2 * t) for k in range(members)])  9.37 us
    pallas_call x1, Pallas kernels, magnetic_terms(): pl.pallas_call(functools.partial(magnetic_terms_kernel, len(blocks), mode...  8.08 us
    pallas_call x1, Pallas kernels, own_sums(): pl.pallas_call(own_sums_kernel, grid=(elems // tile,), in_specs=[pl.Block...  6.82 us
    pallas_call x1, Pallas kernels, gathered(): pl.pallas_call(functools.partial(gather_kernel, len(blocks), steps, adds)...  6.61 us
    pallas_call x1, Pallas kernels, ghost_terms(): pl.pallas_call(functools.partial(ghost_terms_kernel, first), grid=(elems...  5.73 us
    unnamed x30, local copies, waits for them, and re-layouts  3.66 us
  transfers between devices with their start and end apart: 14, of which 6 were waited for; matrix products, arithmetic and copies ran while one was open for 0% of the time, Pallas kernels for 30%

profile of v3, /device:TPU:0, one launch (start us, length us, event | category | flops | bytes accessed | tf_op | source)
XLA Modules:
  0.0 79.0 jit_solution(9522795304849421650)
XLA Ops:
  0.0 1.1 %copy-done = f32[2,6,8,2048]{3,2,1,0:T(8,128)S(1)} copy-done((f32[2,6,8,2048]{3,2,1,0:T(8,128)S(1)}, f32[2,6,8,2048]{3,2,1,0:T(8,128)}, u32[]{:S(2)}) %copy-start) | copy-done | bytes 786456
  1.2 5.1 %collective-permute-start.4 = (f32[192,256]{1,0:T(8,128)S(1)}, f32[192,256]{1,0:T(8,128)S(1)}, u32[]{:S(2)}, u32[]{:S(2)}) collective-permute-start(f32[192,256]{1,0:T(8,128)S(1)} %get-tuple-element.28), channel_id=1, source_target_pairs={{0,6},{1,7},{2,4},{3,5},{4,2},{5,3},{6,0},{7,1},{8,14},{9,15},{10,... | collective-permute-start | bytes 589832 | tf_op jit(solution)/shard_map/ppermute | solution.py:587
  6.5 0.7 collective-permute-start.2
  7.2 1.1 %copy-done.1 = f32[2,6,8,2048]{3,2,1,0:T(8,128)S(1)} copy-done((f32[2,6,8,2048]{3,2,1,0:T(8,128)S(1)}, f32[2,6,8,2048]{3,2,1,0:T(8,128)}, u32[]{:S(2)}) %copy-start.1) | copy-done | bytes 786456
  8.3 0.7 copy-done.10
  9.0 0.7 copy-done.13
  9.6 1.2 %interface_values.2 = (f32[96,256]{1,0:T(8,128)S(1)}, f32[96,256]{1,0:T(8,128)S(1)}) custom-call(s32[1,2]{1,0:T(1,128)S(1)} %copy-done.13, s32[1,512]{1,0:T(1,128)S(1)} %copy-done.10, f32[96,2048]{1,0:T(8,128)S(1)} %bitcast.5, f32[192,256]{1,0:T(8,128)S(1)} %get-tuple-element.24.refs_1_.refs_0_.refs_3_), custom_call_target="tpu_custom_call" | custom-call | bytes 3000000 | tf_op jit(solution)/shard_map/interface_values/pallas_call | solution.py:275
  10.9 1.7 %collective-permute-start = (f32[96,256]{1,0:T(8,128)S(1)}, f32[96,256]{1,0:T(8,128)S(1)}, u32[]{:S(2)}, u32[]{:S(2)}) collective-permute-start(f32[96,256]{1,0:T(8,128)S(1)} %get-tuple-element.25), channel_id=1, source_target_pairs={{0,8},{16,24},{8,0},{24,16},{1,9},{17,25},{9,1},{25,17},{2,10},{18... | collective-permute-start | bytes 294920 | tf_op jit(solution)/shard_map/ppermute | solution.py:604
  12.6 0.8 collective-permute-start.1
  13.4 1.1 %interface_hot.1.refs_6_.hot = bf16[512,2048]{1,0:T(8,128)(2,1)S(1)} custom-call(s32[1,2]{1,0:T(1,128)S(1)} %copy-done.13, s32[1,512]{1,0:T(1,128)S(1)} %copy-done.10), custom_call_target="tpu_custom_call" | custom-call | bytes 3000000 | tf_op jit(solution)/shard_map/interface_hot/pallas_call | solution.py:554
  14.5 1.0 %collective-permute-done.refs_4_.refs_1_ = f32[96,256]{1,0:T(8,128)S(1)} collective-permute-done((f32[96,256]{1,0:T(8,128)S(1)}, f32[96,256]{1,0:T(8,128)S(1)}, u32[]{:S(2)}, u32[]{:S(2)}) %collective-permute-start) | collective-permute-done | bytes 98336 | tf_op jit(solution)/shard_map/ppermute | solution.py:604
  15.5 7.5 %collective-permute-done.3.refs_2_.refs_7_ = f32[192,256]{1,0:T(8,128)S(1)} collective-permute-done((f32[192,256]{1,0:T(8,128)S(1)}, f32[192,256]{1,0:T(8,128)S(1)}, u32[]{:S(2)}, u32[]{:S(2)}) %collective-permute-start.3) | collective-permute-done | bytes 196640 | tf_op jit(solution)/shard_map/ppermute | solution.py:587
  23.1 0.5 lower_halves.2
  23.7 1.7 %collective-permute-done.5.refs_4_.refs_6_.refs_8_.refs_10_ = f32[384,256]{1,0:T(8,128)S(1)} collective-permute-done((f32[384,256]{1,0:T(8,128)S(1)}, f32[384,256]{1,0:T(8,128)S(1)}, u32[]{:S(2)}, u32[]{:S(2)}) %collective-permute-start.5) | collective-permute-done | bytes 393248 | tf_op jit(solution)/shard_map/ppermute | solution.py:595
  25.4 1.0 %transform.1 = (f32[192,256]{1,0:T(8,128)S(1)}, f32[192,256]{1,0:T(8,128)S(1)}, f32[192,256]{1,0:T(8,128)S(1)}, f32[192,256]{1,0:T(8,128)S(1)}) custom-call(f32[128,128]{1,0:T(8,128)S(1)} %copy-done.9, f32[128,128]{1,0:T(8,128)S(1)} %copy-done.8, f32[3,128,256]{2,1,0:T(8,128)S(1)} %copy-done.4, f32[192,256]{1,0:T(8,128)S(1)} %get-tuple-element.24.refs_1_.refs_0_.refs_3_, ...), custom_call_target="tpu_custom_call" | custom-call | bytes 3000000 | tf_op jit(solution)/shard_map/transform/pallas_call | solution.py:135
  26.5 0.3 relay.1.refs_3_
  26.8 2.5 %collective-permute-start.8 = (f32[192,256]{1,0:T(8,128)S(1)}, f32[192,256]{1,0:T(8,128)S(1)}, u32[]{:S(2)}, u32[]{:S(2)}) collective-permute-start(f32[192,256]{1,0:T(8,128)S(1)} %get-tuple-element.33), channel_id=1, source_target_pairs={{0,6},{1,7},{2,4},{3,5},{4,2},{5,3},{6,0},{7,1},{8,14},{9,15},{10,... | collective-permute-start | bytes 589832 | tf_op jit(solution)/shard_map/ppermute | solution.py:587
  29.4 0.9 %collective-permute-start.7 = (f32[192,256]{1,0:T(8,128)S(1)}, f32[192,256]{1,0:T(8,128)S(1)}, u32[]{:S(2)}, u32[]{:S(2)}) collective-permute-start(f32[192,256]{1,0:T(8,128)S(1)} %get-tuple-element.30.refs_0_), channel_id=1, source_target_pairs={{0,4},{1,5},{2,6},{3,7},{4,0},{5,1},{6,2},{7,3},{8,12},{9,13},{10,... | collective-permute-start | bytes 589832 | tf_op jit(solution)/shard_map/ppermute | solution.py:587
  31.0 8.1 %magnetic_terms.1 = (f32[96,6144]{1,0:T(8,128)S(1)}, f32[8,128]{1,0:T(8,128)S(1)}) custom-call(s32[1]{0:T(128)S(6)} %copy.13.live, s32[6,1024]{1,0:T(8,128)S(1)} %copy-done.3, f32[6,6,1024]{2,1,0:T(8,128)S(1)} %copy-done.5, f32[6,6,1024]{2,1,0:T(8,128)S(1)} %copy-done.6, f32[96,2048]{1,0:T(8,128)S(1)} %bitcast.6, ...), custom_call_target="tpu_custom_call" | custom-call | bytes 24000000 | tf_op jit(solution)/shard_map/magnetic_terms/pallas_call | solution.py:354
  39.1 0.2 collective-permute-done.8.refs_3_.refs_6_
  39.3 8.3 %collective-permute-done.7.refs_2_.refs_4_ = f32[192,256]{1,0:T(8,128)S(1)} collective-permute-done((f32[192,256]{1,0:T(8,128)S(1)}, f32[192,256]{1,0:T(8,128)S(1)}, u32[]{:S(2)}, u32[]{:S(2)}) %collective-permute-start.7) | collective-permute-done | bytes 196640 | tf_op jit(solution)/shard_map/ppermute | solution.py:587
  47.6 0.5 lower_halves.3
  48.2 1.7 %collective-permute-done.9.refs_1_.refs_3_.refs_5_.refs_7_ = f32[384,256]{1,0:T(8,128)S(1)} collective-permute-done((f32[384,256]{1,0:T(8,128)S(1)}, f32[384,256]{1,0:T(8,128)S(1)}, u32[]{:S(2)}, u32[]{:S(2)}) %collective-permute-start.9) | collective-permute-done | bytes 393248 | tf_op jit(solution)/shard_map/ppermute | solution.py:595
  49.9 1.2 %interface_values.3 = (f32[96,256]{1,0:T(8,128)S(1)}, f32[96,256]{1,0:T(8,128)S(1)}) custom-call(s32[1,2]{1,0:T(1,128)S(1)} %copy-done.14, s32[1,512]{1,0:T(1,128)S(1)} %copy-done.11, f32[192,256]{1,0:T(8,128)S(1)} %get-tuple-element.32.refs_0_, f32[384,256]{1,0:T(8,128)S(1)} %collective-permute-done.9.refs_1_.refs_3_.refs_5_.refs_7_, ...), custom_call_target="tpu_custom_call" | custom-call | bytes 3000000 | tf_op jit(solution)/shard_map/interface_values/pallas_call | solution.py:275
  51.1 1.6 %collective-permute-start.10 = (f32[96,256]{1,0:T(8,128)S(1)}, f32[96,256]{1,0:T(8,128)S(1)}, u32[]{:S(2)}, u32[]{:S(2)}) collective-permute-start(f32[96,256]{1,0:T(8,128)S(1)} %get-tuple-element.36), channel_id=1, source_target_pairs={{0,8},{16,24},{8,0},{24,16},{1,9},{17,25},{9,1},{25,17},{2,10},{18... | collective-permute-start | bytes 294920 | tf_op jit(solution)/shard_map/ppermute | solution.py:604
  52.7 0.7 collective-permute-start.11
  53.4 6.6 %gathered.1 = (f32[96,6144]{1,0:T(8,128)S(1)}, f32[8,128]{1,0:T(8,128)}) custom-call(s32[1]{0:T(128)S(6)} %copy.13.live, s32[6,1024]{1,0:T(8,128)S(1)} %copy-done.3, f32[192,256]{1,0:T(8,128)S(1)} %get-tuple-element.32.refs_0_, f32[384,256]{1,0:T(8,128)S(1)} %collective-permute-done.9.refs_1_.refs_3_.refs_5_.refs_7_, ...), custom_call_target="tpu_custom_call" | custom-call | bytes 12000000 | tf_op jit(solution)/shard_map/gathered/pallas_call | solution.py:407
  60.0 5.7 %ghost_terms.1 = (bf16[192,6144]{1,0:T(8,128)(2,1)S(1)}, f32[96,256]{1,0:T(8,128)S(1)}, f32[96,256]{1,0:T(8,128)S(1)}) custom-call(s32[1]{0:T(128)S(6)} %copy.13.live, s32[6,1024]{1,0:T(8,128)S(1)} %copy-done.3, f32[6,6,1024]{2,1,0:T(8,128)S(1)} %copy-done.7, f32[96,6144]{1,0:T(8,128)S(1)} %get-tuple-element.31.magnetic_part, ...), custom_call_target="tpu_custom_call" | custom-call | bytes 24000000 | tf_op jit(solution)/shard_map/ghost_terms/pallas_call | solution.py:483
  65.7 4.3 %collective-permute-start.12 = (f32[96,256]{1,0:T(8,128)S(1)}, f32[96,256]{1,0:T(8,128)S(1)}, u32[]{:S(2)}, u32[]{:S(2)}) collective-permute-start(f32[96,256]{1,0:T(8,128)S(1)} %get-tuple-element.39), channel_id=1, source_target_pairs={{0,8},{16,24},{8,0},{24,16},{1,9},{17,25},{9,1},{25,17},{2,10},{18... | collective-permute-start | bytes 294920 | tf_op jit(solution)/shard_map/ppermute | solution.py:604
  70.0 0.7 collective-permute-start.13
  70.7 6.8 %own_sums.1.sums = f32[96,2048]{1,0:T(8,128)S(1)} custom-call(s32[1]{0:T(128)S(6)} %copy.13.live, s32[6,1024]{1,0:T(8,128)S(1)} %copy-done.3, bf16[192,6144]{1,0:T(8,128)(2,1)S(1)} %get-tuple-element.38.terms), custom_call_target="tpu_custom_call" | custom-call | bytes 27000000 | tf_op jit(solution)/shard_map/own_sums/pallas_call | solution.py:531
  77.5 1.5 %finish.1 = f32[96,2048]{1,0:T(8,128)} custom-call(bf16[512,2048]{1,0:T(8,128)(2,1)S(1)} %interface_hot.1.refs_6_.hot, f32[96,2048]{1,0:T(8,128)S(1)} %bitcast.7, f32[96,2048]{1,0:T(8,128)S(1)} %own_sums.1.sums, f32[96,256]{1,0:T(8,128)S(1)} %collective-permute-done.12.left, f32[96,256]{1,0:T(8,128)S(1)} %collective-permute-done.13.right, f32[1,2048]{1,0:T(1,128)S(1)} %bitcast.8), custom_call_target="tpu_custom_call" | custom-call | bytes 6000000 | tf_op jit(solution)/shard_map/finish/pallas_call | solution.py:574
  (40 shorter events, 0.5 us)
Async XLA Ops:
  0.0 1.1 %copy-start = (f32[2,6,8,2048]{3,2,1,0:T(8,128)S(1)}, f32[2,6,8,2048]{3,2,1,0:T(8,128)}, u32[]{:S(2)}) copy-start(f32[2,6,8,2048]{3,2,1,0:T(8,128)} %param.12) | copy-start | bytes 2359300
  1.2 14.3 %collective-permute-start.4 = (f32[192,256]{1,0:T(8,128)S(1)}, f32[192,256]{1,0:T(8,128)S(1)}, u32[]{:S(2)}, u32[]{:S(2)}) collective-permute-start(f32[192,256]{1,0:T(8,128)S(1)} %get-tuple-element.28), channel_id=1, source_target_pairs={{0,6},{1,7},{2,4},{3,5},{4,2},{5,3},{6,0},{7,1},{8,14},{9,15},{10,... | collective-permute-start | bytes 589832 | tf_op jit(solution)/shard_map/ppermute | solution.py:587
  6.4 16.7 %collective-permute-start.3 = (f32[192,256]{1,0:T(8,128)S(1)}, f32[192,256]{1,0:T(8,128)S(1)}, u32[]{:S(2)}, u32[]{:S(2)}) collective-permute-start(f32[192,256]{1,0:T(8,128)S(1)} %get-tuple-element.23.refs_0_), channel_id=1, source_target_pairs={{0,4},{1,5},{2,6},{3,7},{4,0},{5,1},{6,2},{7,3},{8,12},{9,13},{10,... | collective-permute-start | bytes 589832 | tf_op jit(solution)/shard_map/ppermute | solution.py:587
  6.5 16.6 %collective-permute-start.2 = (f32[192,256]{1,0:T(8,128)S(1)}, f32[192,256]{1,0:T(8,128)S(1)}, u32[]{:S(2)}, u32[]{:S(2)}) collective-permute-start(f32[192,256]{1,0:T(8,128)S(1)} %get-tuple-element.27), channel_id=1, source_target_pairs={{0,2},{1,3},{2,0},{3,1},{4,6},{5,7},{6,4},{7,5},{8,10},{9,11},{10,... | collective-permute-start | bytes 589832 | tf_op jit(solution)/shard_map/ppermute | solution.py:587
  7.2 1.1 %copy-start.1 = (f32[2,6,8,2048]{3,2,1,0:T(8,128)S(1)}, f32[2,6,8,2048]{3,2,1,0:T(8,128)}, u32[]{:S(2)}) copy-start(f32[2,6,8,2048]{3,2,1,0:T(8,128)} %param.12) | copy-start | bytes 2359300
  8.3 0.7 copy-start.10
  9.0 0.7 copy-start.13
  10.9 4.7 %collective-permute-start = (f32[96,256]{1,0:T(8,128)S(1)}, f32[96,256]{1,0:T(8,128)S(1)}, u32[]{:S(2)}, u32[]{:S(2)}) collective-permute-start(f32[96,256]{1,0:T(8,128)S(1)} %get-tuple-element.25), channel_id=1, source_target_pairs={{0,8},{16,24},{8,0},{24,16},{1,9},{17,25},{9,1},{25,17},{2,10},{18... | collective-permute-start | bytes 294920 | tf_op jit(solution)/shard_map/ppermute | solution.py:604
  12.6 12.9 %copy-start.4 = (f32[3,128,256]{2,1,0:T(8,128)S(1)}, f32[3,128,256]{2,1,0:T(8,128)}, u32[]{:S(2)}) copy-start(f32[3,128,256]{2,1,0:T(8,128)} %refs_2_.1) | copy-start | bytes 1179652
  12.6 12.9 %copy-start.8 = (f32[128,128]{1,0:T(8,128)S(1)}, f32[128,128]{1,0:T(8,128)}, u32[]{:S(2)}) copy-start(f32[128,128]{1,0:T(8,128)} %constant.5.clone.refs_1_) | copy-start | bytes 196612
  12.6 12.9 %copy-start.9 = (f32[128,128]{1,0:T(8,128)S(1)}, f32[128,128]{1,0:T(8,128)}, u32[]{:S(2)}) copy-start(f32[128,128]{1,0:T(8,128)} %constant.4.clone.refs_0_) | copy-start | bytes 196612
  12.6 3.0 %collective-permute-start.1 = (f32[96,256]{1,0:T(8,128)S(1)}, f32[96,256]{1,0:T(8,128)S(1)}, u32[]{:S(2)}, u32[]{:S(2)}) collective-permute-start(f32[96,256]{1,0:T(8,128)S(1)} %get-tuple-element.26), channel_id=1, source_target_pairs={{8,16},{16,8},{9,17},{17,9},{10,18},{18,10},{11,19},{19,11},{12,20... | collective-permute-start | bytes 294920 | tf_op jit(solution)/shard_map/ppermute | solution.py:604
  23.6 7.4 %copy-start.2 = (f32[2,6,8,2048]{3,2,1,0:T(8,128)S(1)}, f32[2,6,8,2048]{3,2,1,0:T(8,128)}, u32[]{:S(2)}) copy-start(f32[2,6,8,2048]{3,2,1,0:T(8,128)} %param.12) | copy-start | bytes 2359300
  23.6 7.4 %copy-start.3 = (s32[6,1024]{1,0:T(8,128)S(1)}, s32[6,1024]{1,0:T(8,128)}, u32[]{:S(2)}) copy-start(s32[6,1024]{1,0:T(8,128)} %conn.7) | copy-start | bytes 73732
  23.6 7.4 %copy-start.5 = (f32[6,6,1024]{2,1,0:T(8,128)S(1)}, f32[6,6,1024]{2,1,0:T(8,128)}, u32[]{:S(2)}) copy-start(f32[6,6,1024]{2,1,0:T(8,128)} %stiffness.1) | copy-start | bytes 442372
  23.6 7.4 %copy-start.6 = (f32[6,6,1024]{2,1,0:T(8,128)S(1)}, f32[6,6,1024]{2,1,0:T(8,128)}, u32[]{:S(2)}) copy-start(f32[6,6,1024]{2,1,0:T(8,128)} %mass_r.1) | copy-start | bytes 442372
  23.6 1.8 %collective-permute-start.5 = (f32[384,256]{1,0:T(8,128)S(1)}, f32[384,256]{1,0:T(8,128)S(1)}, u32[]{:S(2)}, u32[]{:S(2)}) collective-permute-start(f32[384,256]{1,0:T(8,128)S(1)} %lower_halves.2), channel_id=1, source_target_pairs={{0,1},{1,0},{2,3},{3,2},{4,5},{5,4},{6,7},{7,6},{8,9},{9,8},{10,11... | collective-permute-start | bytes 1179656 | tf_op jit(solution)/shard_map/ppermute | solution.py:595
  26.5 23.5 %copy-start.11 = (s32[1,512]{1,0:T(1,128)S(1)}, s32[1,512]{1,0:T(1,128)}, u32[]{:S(2)}) copy-start(s32[1,512]{1,0:T(1,128)} %interface.5) | copy-start | bytes 6148
  26.5 23.4 %copy-start.14 = (s32[1,2]{1,0:T(1,128)S(1)}, s32[1,2]{1,0:T(1,128)}, u32[]{:S(2)}) copy-start(s32[1,2]{1,0:T(1,128)} %counts.5) | copy-start | bytes 28
  26.8 12.3 %collective-permute-start.6 = (f32[192,256]{1,0:T(8,128)S(1)}, f32[192,256]{1,0:T(8,128)S(1)}, u32[]{:S(2)}, u32[]{:S(2)}) collective-permute-start(f32[192,256]{1,0:T(8,128)S(1)} %relay.1.refs_3_), channel_id=1, source_target_pairs={{0,2},{1,3},{2,0},{3,1},{4,6},{5,7},{6,4},{7,5},{8,10},{9,11},{10,... | collective-permute-start | bytes 589832 | tf_op jit(solution)/shard_map/ppermute | solution.py:587
  26.8 12.5 %collective-permute-start.8 = (f32[192,256]{1,0:T(8,128)S(1)}, f32[192,256]{1,0:T(8,128)S(1)}, u32[]{:S(2)}, u32[]{:S(2)}) collective-permute-start(f32[192,256]{1,0:T(8,128)S(1)} %get-tuple-element.33), channel_id=1, source_target_pairs={{0,6},{1,7},{2,4},{3,5},{4,2},{5,3},{6,0},{7,1},{8,14},{9,15},{10,... | collective-permute-start | bytes 589832 | tf_op jit(solution)/shard_map/ppermute | solution.py:587
  29.4 18.2 %collective-permute-start.7 = (f32[192,256]{1,0:T(8,128)S(1)}, f32[192,256]{1,0:T(8,128)S(1)}, u32[]{:S(2)}, u32[]{:S(2)}) collective-permute-start(f32[192,256]{1,0:T(8,128)S(1)} %get-tuple-element.30.refs_0_), channel_id=1, source_target_pairs={{0,4},{1,5},{2,6},{3,7},{4,0},{5,1},{6,2},{7,3},{8,12},{9,13},{10,... | collective-permute-start | bytes 589832 | tf_op jit(solution)/shard_map/ppermute | solution.py:587
  48.1 11.9 %copy-start.7 = (f32[6,6,1024]{2,1,0:T(8,128)S(1)}, f32[6,6,1024]{2,1,0:T(8,128)}, u32[]{:S(2)}) copy-start(f32[6,6,1024]{2,1,0:T(8,128)} %coupling.1) | copy-start | bytes 442372
  48.1 1.8 %collective-permute-start.9 = (f32[384,256]{1,0:T(8,128)S(1)}, f32[384,256]{1,0:T(8,128)S(1)}, u32[]{:S(2)}, u32[]{:S(2)}) collective-permute-start(f32[384,256]{1,0:T(8,128)S(1)} %lower_halves.3), channel_id=1, source_target_pairs={{0,1},{1,0},{2,3},{3,2},{4,5},{5,4},{6,7},{7,6},{8,9},{9,8},{10,11... | collective-permute-start | bytes 1179656 | tf_op jit(solution)/shard_map/ppermute | solution.py:595
  51.1 8.8 %collective-permute-start.10 = (f32[96,256]{1,0:T(8,128)S(1)}, f32[96,256]{1,0:T(8,128)S(1)}, u32[]{:S(2)}, u32[]{:S(2)}) collective-permute-start(f32[96,256]{1,0:T(8,128)S(1)} %get-tuple-element.36), channel_id=1, source_target_pairs={{0,8},{16,24},{8,0},{24,16},{1,9},{17,25},{9,1},{25,17},{2,10},{18... | collective-permute-start | bytes 294920 | tf_op jit(solution)/shard_map/ppermute | solution.py:604
  52.7 7.3 %collective-permute-start.11 = (f32[96,256]{1,0:T(8,128)S(1)}, f32[96,256]{1,0:T(8,128)S(1)}, u32[]{:S(2)}, u32[]{:S(2)}) collective-permute-start(f32[96,256]{1,0:T(8,128)S(1)} %get-tuple-element.37), channel_id=1, source_target_pairs={{8,16},{16,8},{9,17},{17,9},{10,18},{18,10},{11,19},{19,11},{12,20... | collective-permute-start | bytes 294920 | tf_op jit(solution)/shard_map/ppermute | solution.py:604
  65.7 11.8 %copy-start.12 = (f32[2048]{0:T(1024)S(1)}, f32[2048]{0:T(1024)}, u32[]{:S(2)}) copy-start(f32[2048]{0:T(1024)} %param.17) | copy-start | bytes 24580
  65.7 11.8 %collective-permute-start.12 = (f32[96,256]{1,0:T(8,128)S(1)}, f32[96,256]{1,0:T(8,128)S(1)}, u32[]{:S(2)}, u32[]{:S(2)}) collective-permute-start(f32[96,256]{1,0:T(8,128)S(1)} %get-tuple-element.39), channel_id=1, source_target_pairs={{0,8},{16,24},{8,0},{24,16},{1,9},{17,25},{9,1},{25,17},{2,10},{18... | collective-permute-start | bytes 294920 | tf_op jit(solution)/shard_map/ppermute | solution.py:604
  70.0 7.5 %collective-permute-start.13 = (f32[96,256]{1,0:T(8,128)S(1)}, f32[96,256]{1,0:T(8,128)S(1)}, u32[]{:S(2)}, u32[]{:S(2)}) collective-permute-start(f32[96,256]{1,0:T(8,128)S(1)} %get-tuple-element.40), channel_id=1, source_target_pairs={{8,16},{16,8},{9,17},{17,9},{10,18},{18,10},{11,19},{19,11},{12,20... | collective-permute-start | bytes 294920 | tf_op jit(solution)/shard_map/ppermute | solution.py:604

commit v4 on v3

--- a/solution.py
+++ b/solution.py
@@ -37,6 +37,26 @@
 
 def arrays(blocks):
     return [block.array for block in blocks]
+
+
+def operands(blocks):
+    given, places = [], []
+    for block in blocks:
+        found = [array is block.array for array in given]
+        if True not in found:
+            found.append(True)
+            given.append(block.array)
+        places.append((found.index(True), block.at * block.rows, block.rows))
+    return given, tuple(places)
+
+
+def views(places, refs):
+    return [refs[at].at[low : low + rows, :] for at, low, rows in places]
+
+
+vmem = pl.BlockSpec(memory_space=pltpu.VMEM)
+smem = pl.BlockSpec(memory_space=pltpu.SMEM)
+anywhere = pl.BlockSpec(memory_space=pl.ANY)
 
 
 def params(vmem=KERNEL_VMEM):
@@ -224,7 +244,7 @@
         out_shape=jax.ShapeDtypeStruct((len(blocks) * rows, width), f32),
         scratch_shapes=[pltpu.SemaphoreType.DMA((len(blocks),))],
         compiler_params=params(),
-        cost_estimate=cost(0.5),
+        cost_estimate=cost(0.01),
         name="lower_halves",
     )(*blocks, *after)
 
@@ -248,19 +268,19 @@
     return jnp.where((ids >= first) & even_partition(), swapped, ids)
 
 
-def interface_kernel(count, steps, counts, interface, *refs):
-    blocks = refs[:count]
+def interface_kernel(places, steps, counts, interface, *refs):
     one, two, hot = refs[-3:]
     width = interface.shape[1]
     ids = interface_ids(interface, counts)
     row = 0
     stacked = []
-    for at, block in enumerate(blocks):
+    for view, step in zip(views(places, refs), steps):
+        block = view[...]
         size = block.shape[1]
         iota = lax.broadcasted_iota(jnp.int32, (size, width), 0)
-        base = 0 if steps is None else base_of(steps[at], size)
+        base = 0 if step is None else base_of(step, size)
         hot[row : row + size, :] = one_hot(iota, ids - base)
-        stacked.append(split_rows(block[...]))
+        stacked.append(split_rows(block))
         row += size
     values = jnp.concatenate(stacked, 1)
     got = halves_sum(jnp.dot(values, hot[...], preferred_element_type=f32))
@@ -272,25 +292,24 @@
     rows = blocks[0].shape[0]
     total = sum(block.shape[1] for block in blocks)
     cap = interface.shape[1] // 2
-    return pl.pallas_call(
-        functools.partial(interface_kernel, len(blocks), steps),
-        grid=(1,),
-        in_specs=[pl.BlockSpec(memory_space=pltpu.SMEM), whole_block(interface.shape)]
-        + specs(blocks)
+    given, places = operands(blocks)
+    return pl.pallas_call(
+        functools.partial(interface_kernel, places, steps),
+        in_specs=[pl.BlockSpec(memory_space=pltpu.SMEM)]
+        + [vmem] * (1 + len(given))
         + [pl.BlockSpec(memory_space=pl.ANY)] * len(after),
-        out_specs=[whole_block((rows, cap))] * 2,
         out_shape=[jax.ShapeDtypeStruct((rows, cap), f32)] * 2,
         scratch_shapes=[pltpu.VMEM((total, 2 * cap), bf16)],
         compiler_params=params(),
         cost_estimate=cost(us),
         name="interface_values",
-    )(counts, interface, *arrays(blocks), *after)
-
-
-def live_rows(conn, live, tile_at):
-    tile = conn.shape[1]
-    element = tile_at * tile + lax.broadcasted_iota(jnp.int32, conn.shape, 1)
-    return jnp.where(element < live[0], conn[...], -1)
+    )(counts, interface, *given, *after)
+
+
+def tile_ids(conn, live, at, tile):
+    ids = conn[:, at * tile : (at + 1) * tile]
+    element = at * tile + lax.broadcasted_iota(jnp.int32, ids.shape, 1)
+    return jnp.where(element < live[0], ids, -1)
 
 
 def fill_gather(hot, conn, blocks, bases, tile):
@@ -313,36 +332,35 @@
         column += size
 
 
-def magnetic_terms_kernel(count, mode_dev, live, conn, stiffness, mass_r, *refs):
-    blocks = refs[:count]
-    out, done, values, hot, operator = refs[-5:]
-    tile = conn.shape[1]
+def magnetic_terms_kernel(places, mode_dev, live, conn, stiffness, mass_r, *refs):
+    blocks = views(places, refs)
+    out, done, values, hots, operator = refs[-5:]
+    tile = operator.shape[2]
     done[...] = jnp.zeros_like(done)
-
-    @pl.when(pl.program_id(0) == 0)
-    def _():
-        fill_values(values, blocks)
-
+    fill_values(values, blocks)
     bases = [0]
     for block in blocks[:-1]:
         bases.append(bases[-1] + block.shape[1])
-    ids = by_partner(live_rows(conn, live, pl.program_id(0)), bases[1], blocks[1].shape[1])
-    fill_gather(hot, ids, blocks, bases, tile)
     lane = lax.broadcasted_iota(jnp.int32, (8, tile), 0)
     squares = (own_member() * mode_dev + lax.rem(lane, mode_dev)).astype(f32) ** 2
-    got = halves_sum(jnp.dot(values[...], hot[...], preferred_element_type=f32))
-    for a in range(6):
-        for b in range(6):
-            operator[a * 6 + b] = diffusivity * (
-                stiffness[a, b : b + 1, :] + squares * mass_r[a, b : b + 1, :]
-            )
-    for low in range(0, out.shape[0], 8):
+    for step in range(out.shape[0]):
+        hot = hots.at[step % 2]
+        ids = by_partner(tile_ids(conn, live, step, tile), bases[1], blocks[1].shape[1])
+        fill_gather(hot, ids, blocks, bases, tile)
+        got = halves_sum(jnp.dot(values[...], hot[...], preferred_element_type=f32))
+        at = slice(step * tile, (step + 1) * tile)
         for a in range(6):
-            total = None
             for b in range(6):
-                term = operator[a * 6 + b] * got[low : low + 8, b * tile : (b + 1) * tile]
-                total = term if total is None else total + term
-            out[low : low + 8, a * tile : (a + 1) * tile] = total
+                operator[a * 6 + b] = diffusivity * (
+                    stiffness[a, b : b + 1, at] + squares * mass_r[a, b : b + 1, at]
+                )
+        for low in range(0, out.shape[1], 8):
+            for a in range(6):
+                total = None
+                for b in range(6):
+                    term = operator[a * 6 + b] * got[low : low + 8, b * tile : (b + 1) * tile]
+                    total = term if total is None else total + term
+                out[step, low : low + 8, a * tile : (a + 1) * tile] = total
 
 
 def magnetic_terms(blocks, mode_dev, live, conn, stiffness, mass_r, after):
@@ -350,82 +368,55 @@
     elems = conn.shape[1]
     tile = ELEM_TILE
     total = sum(block.shape[1] for block in blocks)
-    elem_block = pl.BlockSpec((6, 6, tile), lambda j: (0, 0, j))
-    return pl.pallas_call(
-        functools.partial(magnetic_terms_kernel, len(blocks), mode_dev),
-        grid=(elems // tile,),
-        in_specs=[
-            pl.BlockSpec(memory_space=pltpu.SMEM),
-            pl.BlockSpec((6, tile), lambda j: (0, j)),
-            elem_block,
-            elem_block,
-        ]
-        + specs(blocks)
-        + [pl.BlockSpec(memory_space=pl.ANY)] * len(after),
-        out_specs=[pl.BlockSpec((rows, 6 * tile), lambda j: (0, j)), whole_block((8, 128))],
+    given, places = operands(blocks)
+    return pl.pallas_call(
+        functools.partial(magnetic_terms_kernel, places, mode_dev),
+        in_specs=[smem] + [vmem] * (3 + len(given)) + [anywhere] * len(after),
         out_shape=[
-            jax.ShapeDtypeStruct((rows, 6 * elems), f32),
+            jax.ShapeDtypeStruct((elems // tile, rows, 6 * tile), f32),
             jax.ShapeDtypeStruct((8, 128), f32),
         ],
         scratch_shapes=[
             pltpu.VMEM((2 * rows, total), bf16),
-            pltpu.VMEM((total, 6 * tile), bf16),
+            pltpu.VMEM((2, total, 6 * tile), bf16),
             pltpu.VMEM((36, 8, tile), f32),
         ],
-        compiler_params=params(),
-        cost_estimate=cost(8),
+        compiler_params=params(28 << 20),
+        cost_estimate=cost(30),
         name="magnetic_terms",
-    )(live, conn, stiffness, mass_r, *arrays(blocks), *after)
-
-
-def gather_kernel(count, steps, adds, live, conn, *refs):
-    blocks = refs[:count]
-    refs = refs[count:]
-    if adds:
-        earlier, refs = refs[0], refs[1:]
-    out, done, values, hot = refs
-    done[...] = jnp.zeros_like(done)
-    tile = conn.shape[1]
-
-    @pl.when(pl.program_id(0) == 0)
-    def _():
-        fill_values(values, blocks)
-
+    )(live, conn, stiffness, mass_r, *given, *after)
+
+
+def gather_kernel(places, steps, live, conn, *refs):
+    blocks = views(places, refs)
+    out, values, hots = refs[-3:]
+    tile = out.shape[2] // 6
+    fill_values(values, blocks)
     bases = [base_of(step, block.shape[1]) for step, block in zip(steps, blocks)]
-    fill_gather(hot, live_rows(conn, live, pl.program_id(0)), blocks, bases, tile)
-    got = halves_sum(jnp.dot(values[...], hot[...], preferred_element_type=f32))
-    out[...] = got + earlier[...] if adds else got
-
-
-def gathered(blocks, steps, live, conn, earlier, us):
+    for step in range(out.shape[0]):
+        hot = hots.at[step % 2]
+        fill_gather(hot, tile_ids(conn, live, step, tile), blocks, bases, tile)
+        out[step] = halves_sum(jnp.dot(values[...], hot[...], preferred_element_type=f32))
+
+
+def gathered(blocks, steps, live, conn):
     rows = blocks[0].shape[0]
     elems = conn.shape[1]
     tile = ELEM_TILE
     total = sum(block.shape[1] for block in blocks)
-    wide = pl.BlockSpec((rows, 6 * tile), lambda j: (0, j))
-    adds = earlier is not None
-    return pl.pallas_call(
-        functools.partial(gather_kernel, len(blocks), steps, adds),
-        grid=(elems // tile,),
-        in_specs=[
-            pl.BlockSpec(memory_space=pltpu.SMEM),
-            pl.BlockSpec((6, tile), lambda j: (0, j)),
-        ]
-        + specs(blocks)
-        + [wide] * adds,
-        out_specs=[wide, whole_block((8, 128))],
-        out_shape=[
-            jax.ShapeDtypeStruct((rows, 6 * elems), f32),
-            jax.ShapeDtypeStruct((8, 128), f32),
-        ],
+    given, places = operands(blocks)
+    return pl.pallas_call(
+        functools.partial(gather_kernel, places, steps),
+        in_specs=[smem] + [vmem] * (1 + len(given)),
+        out_shape=jax.ShapeDtypeStruct((elems // tile, rows, 6 * tile), f32),
         scratch_shapes=[
             pltpu.VMEM((2 * rows, total), bf16),
-            pltpu.VMEM((total, 6 * tile), bf16),
+            pltpu.VMEM((2, total, 6 * tile), bf16),
         ],
-        compiler_params=params(),
-        cost_estimate=cost(us),
+        compiler_params=params(28 << 20),
+        cost_estimate=cost(5),
         name="gathered",
-    )(live, conn, *arrays(blocks), *([earlier] * adds))
+    )(live, conn, *given)
 
 
 def fill_scatter(hot, conn_columns, first, tile):
@@ -438,75 +429,54 @@
 
 def ghost_terms_kernel(
     first, live, conn, coupling, magnetic_part, electric_part, left, right,
-    terms, left_sums, right_sums, values, hot, hot_columns, total_sums
+    terms, left_sums, right_sums, values, hots, hots_columns
 ):
-    step = pl.program_id(0)
-    tile = conn.shape[1]
-    cap = left.shape[1]
-
-    @pl.when(step == 0)
-    def _():
-        fill_values(values, (left, right))
-        total_sums[...] = jnp.zeros_like(total_sums)
-
-    ids = by_partner(live_rows(conn, live, step), first, cap)
-    fill_gather(hot, ids, (left, right), (first, first + cap), tile)
-    got = electric_part[...] + halves_sum(
-        jnp.dot(values[...], hot[...], preferred_element_type=f32)
-    )
-    rows = got.shape[0]
-    for low in range(0, rows, 16):
-        for a in range(6):
-            at = slice(a * tile, (a + 1) * tile)
-            total = -magnetic_part[low : low + 16, at]
-            for b in range(6):
-                total = total + coupling[a, b : b + 1, :] * got[low : low + 16, b * tile : (b + 1) * tile]
-            high = total.astype(bf16)
-            terms[low : low + 16, at] = high
-            terms[rows + low : rows + low + 16, at] = (total - high.astype(f32)).astype(bf16)
-    fill_scatter(hot_columns, columns_of(ids), first, tile)
-    total_sums[...] += halves_sum(
-        jnp.dot(terms[...], hot_columns[...], preferred_element_type=f32)
-    )
-
-    @pl.when(step == pl.num_programs(0) - 1)
-    def _():
-        left_sums[...] = total_sums[:, :cap]
-        right_sums[...] = total_sums[:, cap:]
+    tile = terms.shape[2] // 6
+    rows, cap = left.shape
+    fill_values(values, (left, right))
+    sums = None
+    for step in range(terms.shape[0]):
+        hot, hot_columns = hots.at[step % 2], hots_columns.at[step % 2]
+        ids = by_partner(tile_ids(conn, live, step, tile), first, cap)
+        fill_gather(hot, ids, (left, right), (first, first + cap), tile)
+        fill_scatter(hot_columns, columns_of(ids), first, tile)
+        got = electric_part[step] + halves_sum(
+            jnp.dot(values[...], hot[...], preferred_element_type=f32)
+        )
+        across = slice(step * tile, (step + 1) * tile)
+        for low in range(0, rows, 16):
+            for a in range(6):
+                at = slice(a * tile, (a + 1) * tile)
+                total = -magnetic_part[step, low : low + 16, at]
+                for b in range(6):
+                    total = total + coupling[a, b : b + 1, across] * got[low : low + 16, b * tile : (b + 1) * tile]
+                high = total.astype(bf16)
+                terms[step, low : low + 16, at] = high
+                terms[step, rows + low : rows + low + 16, at] = (total - high.astype(f32)).astype(bf16)
+        part = halves_sum(jnp.dot(terms[step], hot_columns[...], preferred_element_type=f32))
+        if step == 0:
+            left_sums[...] = part[:, :cap]
+            right_sums[...] = part[:, cap:]
+        else:
+            left_sums[...] += part[:, :cap]
+            right_sums[...] += part[:, cap:]
 
 
 def ghost_terms(first, live, conn, coupling, magnetic_part, electric_part, left, right):
     rows, cap = left.shape
-    elems = conn.shape[1]
-    tile = ELEM_TILE
-    wide = pl.BlockSpec((rows, 6 * tile), lambda j: (0, j))
+    steps, _, wide = electric_part.shape
     return pl.pallas_call(
         functools.partial(ghost_terms_kernel, first),
-        grid=(elems // tile,),
-        in_specs=[
-            pl.BlockSpec(memory_space=pltpu.SMEM),
-            pl.BlockSpec((6, tile), lambda j: (0, j)),
-            pl.BlockSpec((6, 6, tile), lambda j: (0, 0, j)),
-            wide,
-            wide,
-            whole_block((rows, cap)),
-            whole_block((rows, cap)),
-        ],
-        out_specs=[
-            pl.BlockSpec((2 * rows, 6 * tile), lambda j: (0, j)),
-            whole_block((rows, cap)),
-            whole_block((rows, cap)),
-        ],
+        in_specs=[smem] + [vmem] * 6,
         out_shape=[
-            jax.ShapeDtypeStruct((2 * rows, 6 * elems), bf16),
+            jax.ShapeDtypeStruct((steps, 2 * rows, wide), bf16),
             jax.ShapeDtypeStruct((rows, cap), f32),
             jax.ShapeDtypeStruct((rows, cap), f32),
         ],
         scratch_shapes=[
             pltpu.VMEM((2 * rows, 2 * cap), bf16),
-            pltpu.VMEM((2 * cap, 6 * tile), bf16),
-            pltpu.VMEM((6 * tile, 2 * cap), bf16),
-            pltpu.VMEM((rows, 2 * cap), f32),
+            pltpu.VMEM((2, 2 * cap, wide), bf16),
+            pltpu.VMEM((2, wide, 2 * cap), bf16),
         ],
         compiler_params=params(),
         cost_estimate=cost(8),
@@ -514,31 +484,25 @@
     )(live, conn, coupling, magnetic_part, electric_part, left, right)
 
 
-def own_sums_kernel(live, conn, terms, out, hot):
-    @pl.when(pl.program_id(0) == 0)
-    def _():
-        out[...] = jnp.zeros_like(out)
-
-    columns = columns_of(live_rows(conn, live, pl.program_id(0)))
-    fill_scatter(hot, columns, 0, conn.shape[1])
-    out[...] += halves_sum(jnp.dot(terms[...], hot[...], preferred_element_type=f32))
+def own_sums_kernel(live, conn, terms, out, hots):
+    tile = terms.shape[2] // 6
+    for step in range(terms.shape[0]):
+        hot = hots.at[step % 2]
+        fill_scatter(hot, columns_of(tile_ids(conn, live, step, tile)), 0, tile)
+        part = halves_sum(jnp.dot(terms[step], hot[...], preferred_element_type=f32))
+        if step == 0:
+            out[...] = part
+        else:
+            out[...] += part
 
 
 def own_sums(live, conn, terms, nodes):
-    rows = terms.shape[0] // 2
-    tile = ELEM_TILE
-    elems = conn.shape[1]
+    rows, wide = terms.shape[1] // 2, terms.shape[2]
     return pl.pallas_call(
         own_sums_kernel,
-        grid=(elems // tile,),
-        in_specs=[
-            pl.BlockSpec(memory_space=pltpu.SMEM),
-            pl.BlockSpec((6, tile), lambda j: (0, j)),
-            pl.BlockSpec((2 * rows, 6 * tile), lambda j: (0, j)),
-        ],
-        out_specs=whole_block((rows, nodes)),
+        in_specs=[smem, vmem, vmem],
         out_shape=jax.ShapeDtypeStruct((rows, nodes), f32),
-        scratch_shapes=[pltpu.VMEM((6 * tile, nodes), bf16)],
+        scratch_shapes=[pltpu.VMEM((2, wide, nodes), bf16)],
         compiler_params=params(),
         cost_estimate=cost(9),
         name="own_sums",
@@ -621,7 +585,7 @@
     kept = between_chips(packed)
     own = Block(values, rows)
     mag_left, mag_right = neighbours(
-        *interface_values([own], None, counts, interface, 1, (packed[0],))
+        *interface_values([own], (None,), counts, interface, 1, (packed[0],))
     )
     extended = [own, Block(mag_left, rows), Block(mag_right, rows)]
     hot = interface_hot(counts, interface, node_dev)
@@ -636,13 +600,16 @@
     magnetic_part, done = magnetic_terms(
         extended, mode_dev, elem_live, connect, stiffness, mass_r, (sent[1],)
     )
-    swapped = between_cores(kept, (done,))
+    steps = tuple(range(members))
     electric = []
-    for t, block in enumerate(kept):
+    swapped = between_cores(kept[:2], (done,))
+    for t, block in enumerate(kept[:2]):
         electric += [Block(block, rows), Block(swapped, rows, t)]
-    steps = tuple(range(members))
+    swapped = between_cores(kept[2:], ())
+    for t, block in enumerate(kept[2:]):
+        electric += [Block(block, rows), Block(swapped, rows, t)]
     ele_left, ele_right = neighbours(*interface_values(electric, steps, counts, interface, 1))
-    electric_part, _ = gathered(electric, steps, elem_live, connect, None, 4)
+    electric_part = gathered(electric, steps, elem_live, connect)
     terms, left_sums, right_sums = ghost_terms(
         node_dev, elem_live, connect, coupling, magnetic_part, electric_part, ele_left, ele_right
     )

time: 79.3 us -> 73.6 us (0.928)
  Pallas kernels: 34.8 us -> 30.2 us
  waiting for transfers between devices: 20.5 us -> 17.4 us
  starting transfers between devices: 19.2 us -> 21.1 us
    pallas_call x6, Pallas kernels: 29.6 us -> 25 us  [the longest x1 7.24 us: magnetic_terms(): pl.pallas_call(functools.partial(magnetic_terms_kernel, places, mode_dev)...]
    ppermute x6, waiting for transfers between devices: 16 us -> 13.5 us  [between_chips(): lax.ppermute(blocks[t], 'mode', [(k, k ^ 2 * t) for k in range(members)])]
    ppermute x6, starting transfers between devices: 9.37 us -> 10.3 us  [between_chips(): lax.ppermute(blocks[t], 'mode', [(k, k ^ 2 * t) for k in range(members)])]
    ppermute x2 -> x3, waiting for transfers between devices: 3.42 us -> 2.78 us  [between_cores(): lax.ppermute(lower_halves(blocks, after), 'mode', [(k, k ^ 1) for k in ra...]
  transfers between devices with their start and end apart: 14 -> 15, of which waited for: 6 -> 6; matrix products, arithmetic and copies ran while one was open for 0% -> 0% of each run, Pallas kernels for 30% -> 29%
where the time goes in v4:
time: 73.6 us; the launch traced here: 73.3 us
  Pallas kernels  30.2 us (41%)
  starting transfers between devices  21.1 us (29%)
  waiting for transfers between devices  17.4 us (24%)
  local copies, waits for them, and re-layouts  3.66 us (5%)
  between operations  0.98 us (1%)
    ppermute x6, waiting for transfers between devices, between_chips(): lax.ppermute(blocks[t], 'mode', [(k, k ^ 2 * t) for k in range(members)])  13.5 us
    ppermute x6, starting transfers between devices, between_chips(): lax.ppermute(blocks[t], 'mode', [(k, k ^ 2 * t) for k in range(members)])  10.3 us
    ppermute x6, starting transfers between devices, neighbours(): got.append(lax.ppermute(values, 'mesh', pairs))  10.1 us
    pallas_call x1, Pallas kernels, magnetic_terms(): pl.pallas_call(functools.partial(magnetic_terms_kernel, places, mode_dev)...  7.24 us
    pallas_call x1, Pallas kernels, own_sums(): pl.pallas_call(own_sums_kernel, in_specs=[smem, vmem, vmem], out_shape=ja...  5.45 us
    pallas_call x1, Pallas kernels, gathered(): pl.pallas_call(functools.partial(gather_kernel, places, steps), in_specs=...  5.18 us
    pallas_call x1, Pallas kernels, ghost_terms(): pl.pallas_call(functools.partial(ghost_terms_kernel, first), in_specs=[sm...  4.75 us
    unnamed x30, local copies, waits for them, and re-layouts  3.66 us
  transfers between devices with their start and end apart: 15, of which 6 were waited for; matrix products, arithmetic and copies ran while one was open for 0% of the time, Pallas kernels for 29%

profile of v4, /device:TPU:0, one launch (start us, length us, event | category | flops | bytes accessed | tf_op | source)
XLA Modules:
  0.0 73.3 jit_solution(9341004306626483245)
XLA Ops:
  0.0 1.1 %copy-done = f32[2,6,8,2048]{3,2,1,0:T(8,128)S(1)} copy-done((f32[2,6,8,2048]{3,2,1,0:T(8,128)S(1)}, f32[2,6,8,2048]{3,2,1,0:T(8,128)}, u32[]{:S(2)}) %copy-start) | copy-done | bytes 786456
  1.2 5.1 %collective-permute-start.4 = (f32[192,256]{1,0:T(8,128)S(1)}, f32[192,256]{1,0:T(8,128)S(1)}, u32[]{:S(2)}, u32[]{:S(2)}) collective-permute-start(f32[192,256]{1,0:T(8,128)S(1)} %get-tuple-element.27), channel_id=1, source_target_pairs={{0,6},{1,7},{2,4},{3,5},{4,2},{5,3},{6,0},{7,1},{8,14},{9,15},{10,... | collective-permute-start | bytes 589832 | tf_op jit(solution)/shard_map/ppermute | solution.py:551
  6.5 0.7 collective-permute-start.2
  7.2 1.1 %copy-done.1 = f32[2,6,8,2048]{3,2,1,0:T(8,128)S(1)} copy-done((f32[2,6,8,2048]{3,2,1,0:T(8,128)S(1)}, f32[2,6,8,2048]{3,2,1,0:T(8,128)}, u32[]{:S(2)}) %copy-start.1) | copy-done | bytes 786456
  8.3 0.7 copy-done.10
  9.0 0.7 copy-done.13
  9.6 1.2 %interface_values.2 = (f32[96,256]{1,0:T(8,128)S(1)}, f32[96,256]{1,0:T(8,128)S(1)}) custom-call(s32[1,2]{1,0:T(1,128)S(1)} %copy-done.13, s32[1,512]{1,0:T(1,128)S(1)} %copy-done.10, f32[96,2048]{1,0:T(8,128)S(1)} %bitcast.5, f32[192,256]{1,0:T(8,128)S(1)} %get-tuple-element.23.refs_1_.refs_0_.refs_3_), custom_call_target="tpu_custom_call" | custom-call | bytes 3000000 | tf_op jit(solution)/shard_map/interface_values/pallas_call | solution.py:296
  10.9 1.7 %collective-permute-start = (f32[96,256]{1,0:T(8,128)S(1)}, f32[96,256]{1,0:T(8,128)S(1)}, u32[]{:S(2)}, u32[]{:S(2)}) collective-permute-start(f32[96,256]{1,0:T(8,128)S(1)} %get-tuple-element.24), channel_id=1, source_target_pairs={{0,8},{16,24},{8,0},{24,16},{1,9},{17,25},{9,1},{25,17},{2,10},{18... | collective-permute-start | bytes 294920 | tf_op jit(solution)/shard_map/ppermute | solution.py:568
  12.6 0.8 %collective-permute-start.1 = (f32[96,256]{1,0:T(8,128)S(1)}, f32[96,256]{1,0:T(8,128)S(1)}, u32[]{:S(2)}, u32[]{:S(2)}) collective-permute-start(f32[96,256]{1,0:T(8,128)S(1)} %get-tuple-element.25), channel_id=1, source_target_pairs={{8,16},{16,8},{9,17},{17,9},{10,18},{18,10},{11,19},{19,11},{12,20... | collective-permute-start | bytes 294920 | tf_op jit(solution)/shard_map/ppermute | solution.py:568
  13.4 1.1 %interface_hot.1.refs_6_.hot = bf16[512,2048]{1,0:T(8,128)(2,1)S(1)} custom-call(s32[1,2]{1,0:T(1,128)S(1)} %copy-done.13, s32[1,512]{1,0:T(1,128)S(1)} %copy-done.10), custom_call_target="tpu_custom_call" | custom-call | bytes 3000000 | tf_op jit(solution)/shard_map/interface_hot/pallas_call | solution.py:518
  14.5 1.0 %collective-permute-done.refs_4_.refs_1_ = f32[96,256]{1,0:T(8,128)S(1)} collective-permute-done((f32[96,256]{1,0:T(8,128)S(1)}, f32[96,256]{1,0:T(8,128)S(1)}, u32[]{:S(2)}, u32[]{:S(2)}) %collective-permute-start) | collective-permute-done | bytes 98336 | tf_op jit(solution)/shard_map/ppermute | solution.py:568
  15.5 7.5 %collective-permute-done.3.refs_2_.refs_7_ = f32[192,256]{1,0:T(8,128)S(1)} collective-permute-done((f32[192,256]{1,0:T(8,128)S(1)}, f32[192,256]{1,0:T(8,128)S(1)}, u32[]{:S(2)}, u32[]{:S(2)}) %collective-permute-start.3) | collective-permute-done | bytes 196640 | tf_op jit(solution)/shard_map/ppermute | solution.py:551
  23.1 0.5 lower_halves.3
  23.7 1.7 %collective-permute-done.5.refs_4_.refs_6_.refs_8_.refs_10_ = f32[384,256]{1,0:T(8,128)S(1)} collective-permute-done((f32[384,256]{1,0:T(8,128)S(1)}, f32[384,256]{1,0:T(8,128)S(1)}, u32[]{:S(2)}, u32[]{:S(2)}) %collective-permute-start.5) | collective-permute-done | bytes 393248 | tf_op jit(solution)/shard_map/ppermute | solution.py:559
  25.4 1.0 %transform.1 = (f32[192,256]{1,0:T(8,128)S(1)}, f32[192,256]{1,0:T(8,128)S(1)}, f32[192,256]{1,0:T(8,128)S(1)}, f32[192,256]{1,0:T(8,128)S(1)}) custom-call(f32[128,128]{1,0:T(8,128)S(1)} %copy-done.9, f32[128,128]{1,0:T(8,128)S(1)} %copy-done.8, f32[3,128,256]{2,1,0:T(8,128)S(1)} %copy-done.4, f32[192,256]{1,0:T(8,128)S(1)} %get-tuple-element.23.refs_1_.refs_0_.refs_3_, ...), custom_call_target="tpu_custom_call" | custom-call | bytes 3000000 | tf_op jit(solution)/shard_map/transform/pallas_call | solution.py:155
  26.5 2.5 %collective-permute-start.9 = (f32[192,256]{1,0:T(8,128)S(1)}, f32[192,256]{1,0:T(8,128)S(1)}, u32[]{:S(2)}, u32[]{:S(2)}) collective-permute-start(f32[192,256]{1,0:T(8,128)S(1)} %get-tuple-element.33), channel_id=1, source_target_pairs={{0,6},{1,7},{2,4},{3,5},{4,2},{5,3},{6,0},{7,1},{8,14},{9,15},{10,... | collective-permute-start | bytes 589832 | tf_op jit(solution)/shard_map/ppermute | solution.py:551
  29.3 2.0 %collective-permute-start.6 = (f32[192,256]{1,0:T(8,128)S(1)}, f32[192,256]{1,0:T(8,128)S(1)}, u32[]{:S(2)}, u32[]{:S(2)}) collective-permute-start(f32[192,256]{1,0:T(8,128)S(1)} %relay.1.refs_3_), channel_id=1, source_target_pairs={{0,2},{1,3},{2,0},{3,1},{4,6},{5,7},{6,4},{7,5},{8,10},{9,11},{10,... | collective-permute-start | bytes 589832 | tf_op jit(solution)/shard_map/ppermute | solution.py:551
  31.9 7.2 %magnetic_terms.1 = (f32[4,96,1536]{2,1,0:T(8,128)S(1)}, f32[8,128]{1,0:T(8,128)S(1)}) custom-call(s32[1]{0:T(128)S(6)} %copy.13.live, s32[6,1024]{1,0:T(8,128)S(1)} %copy-done.3, f32[6,6,1024]{2,1,0:T(8,128)S(1)} %copy-done.5, f32[6,6,1024]{2,1,0:T(8,128)S(1)} %copy-done.6, f32[96,2048]{1,0:T(8,128)S(1)} %bitcast.6, ...), custom_call_target="tpu_custom_call" | custom-call | bytes 90000000 | tf_op jit(solution)/shard_map/magnetic_terms/pallas_call | solution.py:372
  39.2 6.0 %collective-permute-done.8.refs_0_.refs_3_ = f32[192,256]{1,0:T(8,128)S(1)} collective-permute-done((f32[192,256]{1,0:T(8,128)S(1)}, f32[192,256]{1,0:T(8,128)S(1)}, u32[]{:S(2)}, u32[]{:S(2)}) %collective-permute-start.8) | collective-permute-done | bytes 196640 | tf_op jit(solution)/shard_map/ppermute | solution.py:551
  45.6 0.3 lower_halves.4
  45.9 0.5 collective-permute-start.7
  46.4 0.6 collective-permute-done.10.refs_4_
  47.0 0.5 collective-permute-done.7.refs_1_
  47.5 1.2 %interface_values.3 = (f32[96,256]{1,0:T(8,128)S(1)}, f32[96,256]{1,0:T(8,128)S(1)}) custom-call(s32[1,2]{1,0:T(1,128)S(1)} %copy-done.14, s32[1,512]{1,0:T(1,128)S(1)} %copy-done.11, f32[192,256]{1,0:T(8,128)S(1)} %get-tuple-element.31.refs_0_, f32[192,256]{1,0:T(8,128)S(1)} %collective-permute-done.7.refs_1_, ...), custom_call_target="tpu_custom_call" | custom-call | bytes 3000000 | tf_op jit(solution)/shard_map/interface_values/pallas_call | solution.py:296
  48.7 1.6 %collective-permute-start.11 = (f32[96,256]{1,0:T(8,128)S(1)}, f32[96,256]{1,0:T(8,128)S(1)}, u32[]{:S(2)}, u32[]{:S(2)}) collective-permute-start(f32[96,256]{1,0:T(8,128)S(1)} %get-tuple-element.34), channel_id=1, source_target_pairs={{0,8},{16,24},{8,0},{24,16},{1,9},{17,25},{9,1},{25,17},{2,10},{18... | collective-permute-start | bytes 294920 | tf_op jit(solution)/shard_map/ppermute | solution.py:568
  50.3 0.8 %collective-permute-start.12 = (f32[96,256]{1,0:T(8,128)S(1)}, f32[96,256]{1,0:T(8,128)S(1)}, u32[]{:S(2)}, u32[]{:S(2)}) collective-permute-start(f32[96,256]{1,0:T(8,128)S(1)} %get-tuple-element.35), channel_id=1, source_target_pairs={{8,16},{16,8},{9,17},{17,9},{10,18},{18,10},{11,19},{19,11},{12,20... | collective-permute-start | bytes 294920 | tf_op jit(solution)/shard_map/ppermute | solution.py:568
  51.1 5.2 %gathered.1.electric_part = f32[4,96,1536]{2,1,0:T(8,128)S(1)} custom-call(s32[1]{0:T(128)S(6)} %copy.13.live, s32[6,1024]{1,0:T(8,128)S(1)} %copy-done.3, f32[192,256]{1,0:T(8,128)S(1)} %get-tuple-element.31.refs_0_, f32[192,256]{1,0:T(8,128)S(1)} %collective-permute-done.7.refs_1_, f32[192,256]{1,0:T(8,128)S(1)} %collective-permute-done.6.refs_1_.refs_2_, ...), custom_call_target="tpu_custom_call" | custom-call | bytes 15000000 | tf_op jit(solution)/shard_map/gathered/pallas_call | solution.py:408
  56.3 4.7 %ghost_terms.1 = (bf16[4,192,1536]{2,1,0:T(8,128)(2,1)S(1)}, f32[96,256]{1,0:T(8,128)S(1)}, f32[96,256]{1,0:T(8,128)S(1)}) custom-call(s32[1]{0:T(128)S(6)} %copy.13.live, s32[6,1024]{1,0:T(8,128)S(1)} %copy-done.3, f32[6,6,1024]{2,1,0:T(8,128)S(1)} %copy-done.7, f32[4,96,1536]{2,1,0:T(8,128)S(1)} %get-tuple-element.30.magnetic_part, ...), custom_call_target="tpu_custom_call" | custom-call | bytes 24000000 | tf_op jit(solution)/shard_map/ghost_terms/pallas_call | solution.py:468
  61.1 4.3 %collective-permute-start.13 = (f32[96,256]{1,0:T(8,128)S(1)}, f32[96,256]{1,0:T(8,128)S(1)}, u32[]{:S(2)}, u32[]{:S(2)}) collective-permute-start(f32[96,256]{1,0:T(8,128)S(1)} %get-tuple-element.37), channel_id=1, source_target_pairs={{0,8},{16,24},{8,0},{24,16},{1,9},{17,25},{9,1},{25,17},{2,10},{18... | collective-permute-start | bytes 294920 | tf_op jit(solution)/shard_map/ppermute | solution.py:568
  65.4 0.9 %collective-permute-start.14 = (f32[96,256]{1,0:T(8,128)S(1)}, f32[96,256]{1,0:T(8,128)S(1)}, u32[]{:S(2)}, u32[]{:S(2)}) collective-permute-start(f32[96,256]{1,0:T(8,128)S(1)} %get-tuple-element.38), channel_id=1, source_target_pairs={{8,16},{16,8},{9,17},{17,9},{10,18},{18,10},{11,19},{19,11},{12,20... | collective-permute-start | bytes 294920 | tf_op jit(solution)/shard_map/ppermute | solution.py:568
  66.3 5.4 %own_sums.1.sums = f32[96,2048]{1,0:T(8,128)S(1)} custom-call(s32[1]{0:T(128)S(6)} %copy.13.live, s32[6,1024]{1,0:T(8,128)S(1)} %copy-done.3, bf16[4,192,1536]{2,1,0:T(8,128)(2,1)S(1)} %get-tuple-element.36.terms), custom_call_target="tpu_custom_call" | custom-call | bytes 27000000 | tf_op jit(solution)/shard_map/own_sums/pallas_call | solution.py:501
  71.8 1.5 %finish.1 = f32[96,2048]{1,0:T(8,128)} custom-call(bf16[512,2048]{1,0:T(8,128)(2,1)S(1)} %interface_hot.1.refs_6_.hot, f32[96,2048]{1,0:T(8,128)S(1)} %bitcast.7, f32[96,2048]{1,0:T(8,128)S(1)} %own_sums.1.sums, f32[96,256]{1,0:T(8,128)S(1)} %collective-permute-done.13.left, f32[96,256]{1,0:T(8,128)S(1)} %collective-permute-done.14.right, f32[1,2048]{1,0:T(1,128)S(1)} %bitcast.8), custom_call_target="tpu_custom_call" | custom-call | bytes 6000000 | tf_op jit(solution)/shard_map/finish/pallas_call | solution.py:538
  (43 shorter events, 0.9 us)
Async XLA Ops:
  0.0 1.1 %copy-start = (f32[2,6,8,2048]{3,2,1,0:T(8,128)S(1)}, f32[2,6,8,2048]{3,2,1,0:T(8,128)}, u32[]{:S(2)}) copy-start(f32[2,6,8,2048]{3,2,1,0:T(8,128)} %param.12) | copy-start | bytes 2359300
  1.2 14.3 %collective-permute-start.4 = (f32[192,256]{1,0:T(8,128)S(1)}, f32[192,256]{1,0:T(8,128)S(1)}, u32[]{:S(2)}, u32[]{:S(2)}) collective-permute-start(f32[192,256]{1,0:T(8,128)S(1)} %get-tuple-element.27), channel_id=1, source_target_pairs={{0,6},{1,7},{2,4},{3,5},{4,2},{5,3},{6,0},{7,1},{8,14},{9,15},{10,... | collective-permute-start | bytes 589832 | tf_op jit(solution)/shard_map/ppermute | solution.py:551
  6.4 16.7 %collective-permute-start.3 = (f32[192,256]{1,0:T(8,128)S(1)}, f32[192,256]{1,0:T(8,128)S(1)}, u32[]{:S(2)}, u32[]{:S(2)}) collective-permute-start(f32[192,256]{1,0:T(8,128)S(1)} %get-tuple-element.22.refs_0_), channel_id=1, source_target_pairs={{0,4},{1,5},{2,6},{3,7},{4,0},{5,1},{6,2},{7,3},{8,12},{9,13},{10,... | collective-permute-start | bytes 589832 | tf_op jit(solution)/shard_map/ppermute | solution.py:551
  6.5 16.6 %collective-permute-start.2 = (f32[192,256]{1,0:T(8,128)S(1)}, f32[192,256]{1,0:T(8,128)S(1)}, u32[]{:S(2)}, u32[]{:S(2)}) collective-permute-start(f32[192,256]{1,0:T(8,128)S(1)} %get-tuple-element.26), channel_id=1, source_target_pairs={{0,2},{1,3},{2,0},{3,1},{4,6},{5,7},{6,4},{7,5},{8,10},{9,11},{10,... | collective-permute-start | bytes 589832 | tf_op jit(solution)/shard_map/ppermute | solution.py:551
  7.2 1.1 %copy-start.1 = (f32[2,6,8,2048]{3,2,1,0:T(8,128)S(1)}, f32[2,6,8,2048]{3,2,1,0:T(8,128)}, u32[]{:S(2)}) copy-start(f32[2,6,8,2048]{3,2,1,0:T(8,128)} %param.12) | copy-start | bytes 2359300
  8.3 0.7 copy-start.10
  9.0 0.7 copy-start.13
  10.9 4.7 %collective-permute-start = (f32[96,256]{1,0:T(8,128)S(1)}, f32[96,256]{1,0:T(8,128)S(1)}, u32[]{:S(2)}, u32[]{:S(2)}) collective-permute-start(f32[96,256]{1,0:T(8,128)S(1)} %get-tuple-element.24), channel_id=1, source_target_pairs={{0,8},{16,24},{8,0},{24,16},{1,9},{17,25},{9,1},{25,17},{2,10},{18... | collective-permute-start | bytes 294920 | tf_op jit(solution)/shard_map/ppermute | solution.py:568
  12.6 12.9 %copy-start.4 = (f32[3,128,256]{2,1,0:T(8,128)S(1)}, f32[3,128,256]{2,1,0:T(8,128)}, u32[]{:S(2)}) copy-start(f32[3,128,256]{2,1,0:T(8,128)} %refs_2_.1) | copy-start | bytes 1179652
  12.6 12.9 %copy-start.8 = (f32[128,128]{1,0:T(8,128)S(1)}, f32[128,128]{1,0:T(8,128)}, u32[]{:S(2)}) copy-start(f32[128,128]{1,0:T(8,128)} %constant.5.clone.refs_1_) | copy-start | bytes 196612
  12.6 12.9 %copy-start.9 = (f32[128,128]{1,0:T(8,128)S(1)}, f32[128,128]{1,0:T(8,128)}, u32[]{:S(2)}) copy-start(f32[128,128]{1,0:T(8,128)} %constant.4.clone.refs_0_) | copy-start | bytes 196612
  12.6 3.0 %collective-permute-start.1 = (f32[96,256]{1,0:T(8,128)S(1)}, f32[96,256]{1,0:T(8,128)S(1)}, u32[]{:S(2)}, u32[]{:S(2)}) collective-permute-start(f32[96,256]{1,0:T(8,128)S(1)} %get-tuple-element.25), channel_id=1, source_target_pairs={{8,16},{16,8},{9,17},{17,9},{10,18},{18,10},{11,19},{19,11},{12,20... | collective-permute-start | bytes 294920 | tf_op jit(solution)/shard_map/ppermute | solution.py:568
  23.6 8.3 %copy-start.2 = (f32[2,6,8,2048]{3,2,1,0:T(8,128)S(1)}, f32[2,6,8,2048]{3,2,1,0:T(8,128)}, u32[]{:S(2)}) copy-start(f32[2,6,8,2048]{3,2,1,0:T(8,128)} %param.12) | copy-start | bytes 2359300
  23.6 8.3 %copy-start.3 = (s32[6,1024]{1,0:T(8,128)S(1)}, s32[6,1024]{1,0:T(8,128)}, u32[]{:S(2)}) copy-start(s32[6,1024]{1,0:T(8,128)} %conn.7) | copy-start | bytes 73732
  23.6 8.3 %copy-start.5 = (f32[6,6,1024]{2,1,0:T(8,128)S(1)}, f32[6,6,1024]{2,1,0:T(8,128)}, u32[]{:S(2)}) copy-start(f32[6,6,1024]{2,1,0:T(8,128)} %stiffness.1) | copy-start | bytes 442372
  23.6 8.3 %copy-start.6 = (f32[6,6,1024]{2,1,0:T(8,128)S(1)}, f32[6,6,1024]{2,1,0:T(8,128)}, u32[]{:S(2)}) copy-start(f32[6,6,1024]{2,1,0:T(8,128)} %mass_r.1) | copy-start | bytes 442372
  23.6 1.8 %collective-permute-start.5 = (f32[384,256]{1,0:T(8,128)S(1)}, f32[384,256]{1,0:T(8,128)S(1)}, u32[]{:S(2)}, u32[]{:S(2)}) collective-permute-start(f32[384,256]{1,0:T(8,128)S(1)} %lower_halves.3), channel_id=1, source_target_pairs={{0,1},{1,0},{2,3},{3,2},{4,5},{5,4},{6,7},{7,6},{8,9},{9,8},{10,11... | collective-permute-start | bytes 1179656 | tf_op jit(solution)/shard_map/ppermute | solution.py:559
  26.5 21.0 %copy-start.11 = (s32[1,512]{1,0:T(1,128)S(1)}, s32[1,512]{1,0:T(1,128)}, u32[]{:S(2)}) copy-start(s32[1,512]{1,0:T(1,128)} %interface.5) | copy-start | bytes 6148
  26.5 21.0 %copy-start.14 = (s32[1,2]{1,0:T(1,128)S(1)}, s32[1,2]{1,0:T(1,128)}, u32[]{:S(2)}) copy-start(s32[1,2]{1,0:T(1,128)} %counts.5) | copy-start | bytes 28
  26.5 12.7 %collective-permute-start.9 = (f32[192,256]{1,0:T(8,128)S(1)}, f32[192,256]{1,0:T(8,128)S(1)}, u32[]{:S(2)}, u32[]{:S(2)}) collective-permute-start(f32[192,256]{1,0:T(8,128)S(1)} %get-tuple-element.33), channel_id=1, source_target_pairs={{0,6},{1,7},{2,4},{3,5},{4,2},{5,3},{6,0},{7,1},{8,14},{9,15},{10,... | collective-permute-start | bytes 589832 | tf_op jit(solution)/shard_map/ppermute | solution.py:551
  29.0 16.2 %collective-permute-start.8 = (f32[192,256]{1,0:T(8,128)S(1)}, f32[192,256]{1,0:T(8,128)S(1)}, u32[]{:S(2)}, u32[]{:S(2)}) collective-permute-start(f32[192,256]{1,0:T(8,128)S(1)} %get-tuple-element.29.refs_0_), channel_id=1, source_target_pairs={{0,4},{1,5},{2,6},{3,7},{4,0},{5,1},{6,2},{7,3},{8,12},{9,13},{10,... | collective-permute-start | bytes 589832 | tf_op jit(solution)/shard_map/ppermute | solution.py:551
  29.3 16.3 %collective-permute-start.6 = (f32[192,256]{1,0:T(8,128)S(1)}, f32[192,256]{1,0:T(8,128)S(1)}, u32[]{:S(2)}, u32[]{:S(2)}) collective-permute-start(f32[192,256]{1,0:T(8,128)S(1)} %relay.1.refs_3_), channel_id=1, source_target_pairs={{0,2},{1,3},{2,0},{3,1},{4,6},{5,7},{6,4},{7,5},{8,10},{9,11},{10,... | collective-permute-start | bytes 589832 | tf_op jit(solution)/shard_map/ppermute | solution.py:551
  45.5 1.5 %collective-permute-start.10 = (f32[192,256]{1,0:T(8,128)S(1)}, f32[192,256]{1,0:T(8,128)S(1)}, u32[]{:S(2)}, u32[]{:S(2)}) collective-permute-start(f32[192,256]{1,0:T(8,128)S(1)} %lower_halves.5), channel_id=1, source_target_pairs={{0,1},{1,0},{2,3},{3,2},{4,5},{5,4},{6,7},{7,6},{8,9},{9,8},{10,11... | collective-permute-start | bytes 589832 | tf_op jit(solution)/shard_map/ppermute | solution.py:559
  45.9 10.5 %copy-start.7 = (f32[6,6,1024]{2,1,0:T(8,128)S(1)}, f32[6,6,1024]{2,1,0:T(8,128)}, u32[]{:S(2)}) copy-start(f32[6,6,1024]{2,1,0:T(8,128)} %coupling.1) | copy-start | bytes 442372
  45.9 1.6 %collective-permute-start.7 = (f32[192,256]{1,0:T(8,128)S(1)}, f32[192,256]{1,0:T(8,128)S(1)}, u32[]{:S(2)}, u32[]{:S(2)}) collective-permute-start(f32[192,256]{1,0:T(8,128)S(1)} %lower_halves.4), channel_id=1, source_target_pairs={{0,1},{1,0},{2,3},{3,2},{4,5},{5,4},{6,7},{7,6},{8,9},{9,8},{10,11... | collective-permute-start | bytes 589832 | tf_op jit(solution)/shard_map/ppermute | solution.py:559
  48.7 7.6 %collective-permute-start.11 = (f32[96,256]{1,0:T(8,128)S(1)}, f32[96,256]{1,0:T(8,128)S(1)}, u32[]{:S(2)}, u32[]{:S(2)}) collective-permute-start(f32[96,256]{1,0:T(8,128)S(1)} %get-tuple-element.34), channel_id=1, source_target_pairs={{0,8},{16,24},{8,0},{24,16},{1,9},{17,25},{9,1},{25,17},{2,10},{18... | collective-permute-start | bytes 294920 | tf_op jit(solution)/shard_map/ppermute | solution.py:568
  50.3 6.0 %collective-permute-start.12 = (f32[96,256]{1,0:T(8,128)S(1)}, f32[96,256]{1,0:T(8,128)S(1)}, u32[]{:S(2)}, u32[]{:S(2)}) collective-permute-start(f32[96,256]{1,0:T(8,128)S(1)} %get-tuple-element.35), channel_id=1, source_target_pairs={{8,16},{16,8},{9,17},{17,9},{10,18},{18,10},{11,19},{19,11},{12,20... | collective-permute-start | bytes 294920 | tf_op jit(solution)/shard_map/ppermute | solution.py:568
  61.1 10.7 %copy-start.12 = (f32[2048]{0:T(1024)S(1)}, f32[2048]{0:T(1024)}, u32[]{:S(2)}) copy-start(f32[2048]{0:T(1024)} %param.17) | copy-start | bytes 24580
  61.1 10.7 %collective-permute-start.13 = (f32[96,256]{1,0:T(8,128)S(1)}, f32[96,256]{1,0:T(8,128)S(1)}, u32[]{:S(2)}, u32[]{:S(2)}) collective-permute-start(f32[96,256]{1,0:T(8,128)S(1)} %get-tuple-element.37), channel_id=1, source_target_pairs={{0,8},{16,24},{8,0},{24,16},{1,9},{17,25},{9,1},{25,17},{2,10},{18... | collective-permute-start | bytes 294920 | tf_op jit(solution)/shard_map/ppermute | solution.py:568
  65.4 6.4 %collective-permute-start.14 = (f32[96,256]{1,0:T(8,128)S(1)}, f32[96,256]{1,0:T(8,128)S(1)}, u32[]{:S(2)}, u32[]{:S(2)}) collective-permute-start(f32[96,256]{1,0:T(8,128)S(1)} %get-tuple-element.38), channel_id=1, source_target_pairs={{8,16},{16,8},{9,17},{17,9},{10,18},{18,10},{11,19},{19,11},{12,20... | collective-permute-start | bytes 294920 | tf_op jit(solution)/shard_map/ppermute | solution.py:568

commit v5 on v4

--- a/solution.py
+++ b/solution.py
@@ -268,24 +268,26 @@
     return jnp.where((ids >= first) & even_partition(), swapped, ids)
 
 
+def member_hot(out, ids, steps, slab):
+    for at, step in enumerate(steps):
+        iota = lax.broadcasted_iota(jnp.int32, (slab, ids.shape[1]), 0)
+        base = 0 if step is None else base_of(step, slab)
+        out[at * slab : (at + 1) * slab, :] = one_hot(iota, ids - base)
+
+
 def interface_kernel(places, steps, counts, interface, *refs):
     one, two, hot = refs[-3:]
-    width = interface.shape[1]
-    ids = interface_ids(interface, counts)
-    row = 0
-    stacked = []
-    for view, step in zip(views(places, refs), steps):
-        block = view[...]
-        size = block.shape[1]
-        iota = lax.broadcasted_iota(jnp.int32, (size, width), 0)
-        base = 0 if step is None else base_of(step, size)
-        hot[row : row + size, :] = one_hot(iota, ids - base)
-        stacked.append(split_rows(block))
-        row += size
-    values = jnp.concatenate(stacked, 1)
+    blocks = views(places, refs)
+    member_hot(hot, interface_ids(interface, counts), steps, blocks[0].shape[1])
+    picked_values(blocks, hot, one, two)
+
+
+def picked_values(blocks, hot, one, two):
+    cap = one.shape[1]
+    values = jnp.concatenate([split_rows(block[...]) for block in blocks], 1)
     got = halves_sum(jnp.dot(values, hot[...], preferred_element_type=f32))
-    one[...] = got[:, : width // 2]
-    two[...] = got[:, width // 2 :]
+    one[...] = got[:, :cap]
+    two[...] = got[:, cap:]
 
 
 def interface_values(blocks, steps, counts, interface, us, after=()):
@@ -295,15 +297,30 @@
     given, places = operands(blocks)
     return pl.pallas_call(
         functools.partial(interface_kernel, places, steps),
-        in_specs=[pl.BlockSpec(memory_space=pltpu.SMEM)]
-        + [vmem] * (1 + len(given))
-        + [pl.BlockSpec(memory_space=pl.ANY)] * len(after),
+        in_specs=[smem] + [vmem] * (1 + len(given)) + [anywhere] * len(after),
         out_shape=[jax.ShapeDtypeStruct((rows, cap), f32)] * 2,
         scratch_shapes=[pltpu.VMEM((total, 2 * cap), bf16)],
         compiler_params=params(),
         cost_estimate=cost(us),
         name="interface_values",
     )(counts, interface, *given, *after)
+
+
+def picked_kernel(places, hot, *refs):
+    picked_values(views(places, refs), hot, *refs[-2:])
+
+
+def picked(blocks, hot):
+    rows = blocks[0].shape[0]
+    given, places = operands(blocks)
+    return pl.pallas_call(
+        functools.partial(picked_kernel, places),
+        in_specs=[vmem] * (1 + len(given)),
+        out_shape=[jax.ShapeDtypeStruct((rows, hot.shape[1] // 2), f32)] * 2,
+        compiler_params=params(),
+        cost_estimate=cost(1),
+        name="picked",
+    )(hot, *given)
 
 
 def tile_ids(conn, live, at, tile):
@@ -509,35 +526,54 @@
     )(live, conn, terms)
 
 
-def interface_hot_kernel(counts, interface, out):
-    iota = lax.broadcasted_iota(jnp.int32, out.shape, 1)
-    out[...] = one_hot(iota, columns_of(interface_ids(interface, counts))[:, :1])
-
-
-def interface_hot(counts, interface, nodes):
-    return pl.pallas_call(
-        interface_hot_kernel,
-        in_specs=[
-            pl.BlockSpec(memory_space=pltpu.SMEM),
-            pl.BlockSpec(memory_space=pltpu.VMEM),
+def interface_hot_kernel(steps, counts, interface, by_slot, by_node):
+    ids = interface_ids(interface, counts)
+    iota = lax.broadcasted_iota(jnp.int32, by_slot.shape, 1)
+    by_slot[...] = one_hot(iota, columns_of(ids)[:, :1])
+    member_hot(by_node, ids, steps, by_node.shape[0] // len(steps))
+
+
+def interface_hot(counts, interface, nodes, steps):
+    slots = interface.shape[1]
+    return pl.pallas_call(
+        functools.partial(interface_hot_kernel, steps),
+        in_specs=[smem, vmem],
+        out_shape=[
+            jax.ShapeDtypeStruct((slots, nodes), bf16),
+            jax.ShapeDtypeStruct((nodes, slots), bf16),
         ],
-        out_shape=jax.ShapeDtypeStruct((interface.shape[1], nodes), bf16),
-        compiler_params=params(),
-        cost_estimate=cost(1),
+        compiler_params=params(),
+        cost_estimate=cost(2),
         name="interface_hot",
     )(counts, interface)
 
 
-def finish_kernel(hot, magnetic, sums, left, right, inv_mass, out):
+def finish_kernel(hot, magnetic, sums, left, right, inv_mass, out, parts, sems):
     values = jnp.concatenate([split_rows(left[...]), split_rows(right[...])], 1)
-    extra = halves_sum(jnp.dot(values, hot[...], preferred_element_type=f32))
-    out[...] = magnetic[...] + time_step * inv_mass[...] * (sums[...] + extra)
+    count, _, width = parts.shape
+    copies = []
+    for part in range(count):
+        at = slice(part * width, (part + 1) * width)
+        extra = halves_sum(jnp.dot(values, hot[:, at], preferred_element_type=f32))
+        parts[part] = magnetic[:, at] + time_step * inv_mass[:, at] * (sums[:, at] + extra)
+        copies.append(pltpu.make_async_copy(parts.at[part], out.at[:, at], sems.at[part]))
+        copies[-1].start()
+    for copy in copies:
+        copy.wait()
 
 
 def finish(hot, magnetic, sums, left, right, inv_mass):
+    rows, nodes = magnetic.shape
+    count = 4
     return pl.pallas_call(
         finish_kernel,
-        out_shape=jax.ShapeDtypeStruct(magnetic.shape, f32),
+        in_specs=[vmem] * 6,
+        out_specs=anywhere,
+        out_shape=jax.ShapeDtypeStruct((rows, nodes), f32),
+        scratch_shapes=[
+            pltpu.VMEM((count, rows, nodes // count), f32),
+            pltpu.SemaphoreType.DMA((count,)),
+        ],
         compiler_params=params(),
         cost_estimate=cost(2),
         name="finish",
@@ -588,7 +624,8 @@
         *interface_values([own], (None,), counts, interface, 1, (packed[0],))
     )
     extended = [own, Block(mag_left, rows), Block(mag_right, rows)]
-    hot = interface_hot(counts, interface, node_dev)
+    steps = tuple(range(members))
+    hot, node_hot = interface_hot(counts, interface, node_dev, steps)
     swapped = between_cores(kept, (mag_left, mag_right, hot))
     arrived = []
     for t, block in enumerate(kept):
@@ -600,7 +637,6 @@
     magnetic_part, done = magnetic_terms(
         extended, mode_dev, elem_live, connect, stiffness, mass_r, (sent[1],)
     )
-    steps = tuple(range(members))
     electric = []
     swapped = between_cores(kept[:2], (done,))
     for t, block in enumerate(kept[:2]):
@@ -608,7 +644,7 @@
     swapped = between_cores(kept[2:], ())
     for t, block in enumerate(kept[2:]):
         electric += [Block(block, rows), Block(swapped, rows, t)]
-    ele_left, ele_right = neighbours(*interface_values(electric, steps, counts, interface, 1))
+    ele_left, ele_right = neighbours(*picked(electric, node_hot))
     electric_part = gathered(electric, steps, elem_live, connect)
     terms, left_sums, right_sums = ghost_terms(
         node_dev, elem_live, connect, coupling, magnetic_part, electric_part, ele_left, ele_right

time: 73.6 us -> 72.9 us (level)
    pallas_call x2 -> x3, Pallas kernels: 2.63 us -> 3.85 us  [the longest x1 1.94 us: interface_hot(): pl.pallas_call(functools.partial(interface_hot_kernel, steps), in_specs=[...]
    pallas_call x2 -> x1, Pallas kernels: 2.41 us -> 1.2 us  [interface_values(): pl.pallas_call(functools.partial(interface_kernel, places, steps), in_spe...]
    unnamed x30 -> x26, local copies, waits for them, and re-layouts: 3.66 us -> 3.65 us
  transfers between devices with their start and end apart: 15 -> 15, of which waited for: 6 -> 6; matrix products, arithmetic and copies ran while one was open for 0% -> 0% of each run, Pallas kernels for 29% -> 30%
where the time goes in v5:
time: 72.9 us; the launch traced here: 72.6 us
  Pallas kernels  30.2 us (41%)
  starting transfers between devices  20.9 us (29%)
  waiting for transfers between devices  16.7 us (23%)
  local copies, waits for them, and re-layouts  3.65 us (5%)
  between operations  1.14 us (2%)
    ppermute x6, waiting for transfers between devices, between_chips(): lax.ppermute(blocks[t], 'mode', [(k, k ^ 2 * t) for k in range(members)])  13.5 us
    ppermute x6, starting transfers between devices, between_chips(): lax.ppermute(blocks[t], 'mode', [(k, k ^ 2 * t) for k in range(members)])  10.3 us
    ppermute x6, starting transfers between devices, neighbours(): got.append(lax.ppermute(values, 'mesh', pairs))  9.95 us
    pallas_call x1, Pallas kernels, magnetic_terms(): pl.pallas_call(functools.partial(magnetic_terms_kernel, places, mode_dev)...  7.25 us
    pallas_call x1, Pallas kernels, own_sums(): pl.pallas_call(own_sums_kernel, in_specs=[smem, vmem, vmem], out_shape=ja...  5.45 us
    pallas_call x1, Pallas kernels, gathered(): pl.pallas_call(functools.partial(gather_kernel, places, steps), in_specs=...  5.18 us
    pallas_call x1, Pallas kernels, ghost_terms(): pl.pallas_call(functools.partial(ghost_terms_kernel, first), in_specs=[sm...  4.69 us
    unnamed x26, local copies, waits for them, and re-layouts  3.65 us
  transfers between devices with their start and end apart: 15, of which 6 were waited for; matrix products, arithmetic and copies ran while one was open for 0% of the time, Pallas kernels for 30%

profile of v5, /device:TPU:0, one launch (start us, length us, event | category | flops | bytes accessed | tf_op | source)
XLA Modules:
  0.0 72.6 jit_solution(11955350484534653634)
XLA Ops:
  0.0 1.1 %copy-done = f32[2,6,8,2048]{3,2,1,0:T(8,128)S(1)} copy-done((f32[2,6,8,2048]{3,2,1,0:T(8,128)S(1)}, f32[2,6,8,2048]{3,2,1,0:T(8,128)}, u32[]{:S(2)}) %copy-start) | copy-done | bytes 786456
  1.2 5.1 %collective-permute-start.4 = (f32[192,256]{1,0:T(8,128)S(1)}, f32[192,256]{1,0:T(8,128)S(1)}, u32[]{:S(2)}, u32[]{:S(2)}) collective-permute-start(f32[192,256]{1,0:T(8,128)S(1)} %get-tuple-element.30), channel_id=1, source_target_pairs={{0,6},{1,7},{2,4},{3,5},{4,2},{5,3},{6,0},{7,1},{8,14},{9,15},{10,... | collective-permute-start | bytes 589832 | tf_op jit(solution)/shard_map/ppermute | solution.py:587
  6.5 0.7 collective-permute-start.2
  7.2 1.1 %copy-done.1 = f32[2,6,8,2048]{3,2,1,0:T(8,128)S(1)} copy-done((f32[2,6,8,2048]{3,2,1,0:T(8,128)S(1)}, f32[2,6,8,2048]{3,2,1,0:T(8,128)}, u32[]{:S(2)}) %copy-start.1) | copy-done | bytes 786456
  8.3 0.7 copy-done.11
  9.0 0.7 copy-done.12
  9.7 1.2 %interface_values.1 = (f32[96,256]{1,0:T(8,128)S(1)}, f32[96,256]{1,0:T(8,128)S(1)}) custom-call(s32[1,2]{1,0:T(1,128)S(1)} %copy-done.12, s32[1,512]{1,0:T(1,128)S(1)} %copy-done.11, f32[96,2048]{1,0:T(8,128)S(1)} %bitcast.5, f32[192,256]{1,0:T(8,128)S(1)} %get-tuple-element.26.refs_1_.refs_0_.refs_3_), custom_call_target="tpu_custom_call" | custom-call | bytes 3000000 | tf_op jit(solution)/shard_map/interface_values/pallas_call | solution.py:298
  10.9 1.7 %collective-permute-start = (f32[96,256]{1,0:T(8,128)S(1)}, f32[96,256]{1,0:T(8,128)S(1)}, u32[]{:S(2)}, u32[]{:S(2)}) collective-permute-start(f32[96,256]{1,0:T(8,128)S(1)} %get-tuple-element.27), channel_id=1, source_target_pairs={{0,8},{16,24},{8,0},{24,16},{1,9},{17,25},{9,1},{25,17},{2,10},{18... | collective-permute-start | bytes 294920 | tf_op jit(solution)/shard_map/ppermute | solution.py:604
  12.6 0.7 collective-permute-start.1
  13.2 1.9 %interface_hot.1 = (bf16[512,2048]{1,0:T(8,128)(2,1)S(1)}, bf16[2048,512]{1,0:T(8,128)(2,1)S(1)}) custom-call(s32[1,2]{1,0:T(1,128)S(1)} %copy-done.12, s32[1,512]{1,0:T(1,128)S(1)} %copy-done.11), custom_call_target="tpu_custom_call" | custom-call | bytes 6000000 | tf_op jit(solution)/shard_map/interface_hot/pallas_call | solution.py:538
  15.2 0.4 collective-permute-done.refs_4_.refs_1_
  15.5 7.5 %collective-permute-done.3.refs_2_.refs_7_ = f32[192,256]{1,0:T(8,128)S(1)} collective-permute-done((f32[192,256]{1,0:T(8,128)S(1)}, f32[192,256]{1,0:T(8,128)S(1)}, u32[]{:S(2)}, u32[]{:S(2)}) %collective-permute-start.3) | collective-permute-done | bytes 196640 | tf_op jit(solution)/shard_map/ppermute | solution.py:587
  23.1 0.5 lower_halves.3
  23.7 1.7 %collective-permute-done.5.refs_4_.refs_6_.refs_8_.refs_10_ = f32[384,256]{1,0:T(8,128)S(1)} collective-permute-done((f32[384,256]{1,0:T(8,128)S(1)}, f32[384,256]{1,0:T(8,128)S(1)}, u32[]{:S(2)}, u32[]{:S(2)}) %collective-permute-start.5) | collective-permute-done | bytes 393248 | tf_op jit(solution)/shard_map/ppermute | solution.py:595
  25.4 1.0 %transform.1 = (f32[192,256]{1,0:T(8,128)S(1)}, f32[192,256]{1,0:T(8,128)S(1)}, f32[192,256]{1,0:T(8,128)S(1)}, f32[192,256]{1,0:T(8,128)S(1)}) custom-call(f32[128,128]{1,0:T(8,128)S(1)} %copy-done.9, f32[128,128]{1,0:T(8,128)S(1)} %copy-done.8, f32[3,128,256]{2,1,0:T(8,128)S(1)} %copy-done.4, f32[192,256]{1,0:T(8,128)S(1)} %get-tuple-element.26.refs_1_.refs_0_.refs_3_, ...), custom_call_target="tpu_custom_call" | custom-call | bytes 3000000 | tf_op jit(solution)/shard_map/transform/pallas_call | solution.py:155
  26.5 2.5 %collective-permute-start.9 = (f32[192,256]{1,0:T(8,128)S(1)}, f32[192,256]{1,0:T(8,128)S(1)}, u32[]{:S(2)}, u32[]{:S(2)}) collective-permute-start(f32[192,256]{1,0:T(8,128)S(1)} %get-tuple-element.36), channel_id=1, source_target_pairs={{0,6},{1,7},{2,4},{3,5},{4,2},{5,3},{6,0},{7,1},{8,14},{9,15},{10,... | collective-permute-start | bytes 589832 | tf_op jit(solution)/shard_map/ppermute | solution.py:587
  29.3 2.0 %collective-permute-start.6 = (f32[192,256]{1,0:T(8,128)S(1)}, f32[192,256]{1,0:T(8,128)S(1)}, u32[]{:S(2)}, u32[]{:S(2)}) collective-permute-start(f32[192,256]{1,0:T(8,128)S(1)} %relay.1.refs_3_), channel_id=1, source_target_pairs={{0,2},{1,3},{2,0},{3,1},{4,6},{5,7},{6,4},{7,5},{8,10},{9,11},{10,... | collective-permute-start | bytes 589832 | tf_op jit(solution)/shard_map/ppermute | solution.py:587
  31.9 7.3 %magnetic_terms.1 = (f32[4,96,1536]{2,1,0:T(8,128)S(1)}, f32[8,128]{1,0:T(8,128)S(1)}) custom-call(s32[1]{0:T(128)S(6)} %copy.13.live, s32[6,1024]{1,0:T(8,128)S(1)} %copy-done.3, f32[6,6,1024]{2,1,0:T(8,128)S(1)} %copy-done.5, f32[6,6,1024]{2,1,0:T(8,128)S(1)} %copy-done.6, f32[96,2048]{1,0:T(8,128)S(1)} %bitcast.6, ...), custom_call_target="tpu_custom_call" | custom-call | bytes 90000000 | tf_op jit(solution)/shard_map/magnetic_terms/pallas_call | solution.py:389
  39.2 6.0 %collective-permute-done.8.refs_0_.refs_3_ = f32[192,256]{1,0:T(8,128)S(1)} collective-permute-done((f32[192,256]{1,0:T(8,128)S(1)}, f32[192,256]{1,0:T(8,128)S(1)}, u32[]{:S(2)}, u32[]{:S(2)}) %collective-permute-start.8) | collective-permute-done | bytes 196640 | tf_op jit(solution)/shard_map/ppermute | solution.py:587
  45.6 0.3 lower_halves.4
  45.8 0.5 collective-permute-start.7
  46.4 0.6 collective-permute-done.10.refs_4_
  47.0 0.5 collective-permute-done.7.refs_1_
  47.4 0.6 picked.1
  48.0 1.6 %collective-permute-start.11 = (f32[96,256]{1,0:T(8,128)S(1)}, f32[96,256]{1,0:T(8,128)S(1)}, u32[]{:S(2)}, u32[]{:S(2)}) collective-permute-start(f32[96,256]{1,0:T(8,128)S(1)} %get-tuple-element.38), channel_id=1, source_target_pairs={{0,8},{16,24},{8,0},{24,16},{1,9},{17,25},{9,1},{25,17},{2,10},{18... | collective-permute-start | bytes 294920 | tf_op jit(solution)/shard_map/ppermute | solution.py:604
  49.6 0.8 %collective-permute-start.12 = (f32[96,256]{1,0:T(8,128)S(1)}, f32[96,256]{1,0:T(8,128)S(1)}, u32[]{:S(2)}, u32[]{:S(2)}) collective-permute-start(f32[96,256]{1,0:T(8,128)S(1)} %get-tuple-element.39), channel_id=1, source_target_pairs={{8,16},{16,8},{9,17},{17,9},{10,18},{18,10},{11,19},{19,11},{12,20... | collective-permute-start | bytes 294920 | tf_op jit(solution)/shard_map/ppermute | solution.py:604
  50.4 5.2 %gathered.1.electric_part = f32[4,96,1536]{2,1,0:T(8,128)S(1)} custom-call(s32[1]{0:T(128)S(6)} %copy.13.live, s32[6,1024]{1,0:T(8,128)S(1)} %copy-done.3, f32[192,256]{1,0:T(8,128)S(1)} %get-tuple-element.34.refs_0_, f32[192,256]{1,0:T(8,128)S(1)} %collective-permute-done.7.refs_1_, f32[192,256]{1,0:T(8,128)S(1)} %collective-permute-done.6.refs_1_.refs_2_, ...), custom_call_target="tpu_custom_call" | custom-call | bytes 15000000 | tf_op jit(solution)/shard_map/gathered/pallas_call | solution.py:425
  55.7 4.7 %ghost_terms.1 = (bf16[4,192,1536]{2,1,0:T(8,128)(2,1)S(1)}, f32[96,256]{1,0:T(8,128)S(1)}, f32[96,256]{1,0:T(8,128)S(1)}) custom-call(s32[1]{0:T(128)S(6)} %copy.13.live, s32[6,1024]{1,0:T(8,128)S(1)} %copy-done.3, f32[6,6,1024]{2,1,0:T(8,128)S(1)} %copy-done.7, f32[4,96,1536]{2,1,0:T(8,128)S(1)} %get-tuple-element.33.magnetic_part, ...), custom_call_target="tpu_custom_call" | custom-call | bytes 24000000 | tf_op jit(solution)/shard_map/ghost_terms/pallas_call | solution.py:485
  60.4 4.3 %collective-permute-start.13 = (f32[96,256]{1,0:T(8,128)S(1)}, f32[96,256]{1,0:T(8,128)S(1)}, u32[]{:S(2)}, u32[]{:S(2)}) collective-permute-start(f32[96,256]{1,0:T(8,128)S(1)} %get-tuple-element.41), channel_id=1, source_target_pairs={{0,8},{16,24},{8,0},{24,16},{1,9},{17,25},{9,1},{25,17},{2,10},{18... | collective-permute-start | bytes 294920 | tf_op jit(solution)/shard_map/ppermute | solution.py:604
  64.7 0.9 %collective-permute-start.14 = (f32[96,256]{1,0:T(8,128)S(1)}, f32[96,256]{1,0:T(8,128)S(1)}, u32[]{:S(2)}, u32[]{:S(2)}) collective-permute-start(f32[96,256]{1,0:T(8,128)S(1)} %get-tuple-element.42), channel_id=1, source_target_pairs={{8,16},{16,8},{9,17},{17,9},{10,18},{18,10},{11,19},{19,11},{12,20... | collective-permute-start | bytes 294920 | tf_op jit(solution)/shard_map/ppermute | solution.py:604
  65.6 5.4 %own_sums.1.sums = f32[96,2048]{1,0:T(8,128)S(1)} custom-call(s32[1]{0:T(128)S(6)} %copy.13.live, s32[6,1024]{1,0:T(8,128)S(1)} %copy-done.3, bf16[4,192,1536]{2,1,0:T(8,128)(2,1)S(1)} %get-tuple-element.40.terms), custom_call_target="tpu_custom_call" | custom-call | bytes 27000000 | tf_op jit(solution)/shard_map/own_sums/pallas_call | solution.py:518
  71.1 1.3 %finish.1 = f32[96,2048]{1,0:T(8,128)} custom-call(bf16[512,2048]{1,0:T(8,128)(2,1)S(1)} %get-tuple-element.24.refs_6_.hot, f32[96,2048]{1,0:T(8,128)S(1)} %bitcast.7, f32[96,2048]{1,0:T(8,128)S(1)} %own_sums.1.sums, f32[96,256]{1,0:T(8,128)S(1)} %collective-permute-done.13.left, f32[96,256]{1,0:T(8,128)S(1)} %collective-permute-done.14.right, ...), custom_call_target="tpu_custom_call" | custom-call | bytes 6000000 | tf_op jit(solution)/shard_map/finish/pallas_call | solution.py:568
  (39 shorter events, 0.9 us)
Async XLA Ops:
  0.0 1.1 %copy-start = (f32[2,6,8,2048]{3,2,1,0:T(8,128)S(1)}, f32[2,6,8,2048]{3,2,1,0:T(8,128)}, u32[]{:S(2)}) copy-start(f32[2,6,8,2048]{3,2,1,0:T(8,128)} %param.12) | copy-start | bytes 2359300
  1.2 14.3 %collective-permute-start.4 = (f32[192,256]{1,0:T(8,128)S(1)}, f32[192,256]{1,0:T(8,128)S(1)}, u32[]{:S(2)}, u32[]{:S(2)}) collective-permute-start(f32[192,256]{1,0:T(8,128)S(1)} %get-tuple-element.30), channel_id=1, source_target_pairs={{0,6},{1,7},{2,4},{3,5},{4,2},{5,3},{6,0},{7,1},{8,14},{9,15},{10,... | collective-permute-start | bytes 589832 | tf_op jit(solution)/shard_map/ppermute | solution.py:587
  6.4 16.7 %collective-permute-start.3 = (f32[192,256]{1,0:T(8,128)S(1)}, f32[192,256]{1,0:T(8,128)S(1)}, u32[]{:S(2)}, u32[]{:S(2)}) collective-permute-start(f32[192,256]{1,0:T(8,128)S(1)} %get-tuple-element.25.refs_0_), channel_id=1, source_target_pairs={{0,4},{1,5},{2,6},{3,7},{4,0},{5,1},{6,2},{7,3},{8,12},{9,13},{10,... | collective-permute-start | bytes 589832 | tf_op jit(solution)/shard_map/ppermute | solution.py:587
  6.4 19.1 %copy-start.4 = (f32[3,128,256]{2,1,0:T(8,128)S(1)}, f32[3,128,256]{2,1,0:T(8,128)}, u32[]{:S(2)}) copy-start(f32[3,128,256]{2,1,0:T(8,128)} %refs_2_.1) | copy-start | bytes 1179652
  6.4 19.1 %copy-start.8 = (f32[128,128]{1,0:T(8,128)S(1)}, f32[128,128]{1,0:T(8,128)}, u32[]{:S(2)}) copy-start(f32[128,128]{1,0:T(8,128)} %constant.5.clone.refs_1_) | copy-start | bytes 196612
  6.4 19.1 %copy-start.9 = (f32[128,128]{1,0:T(8,128)S(1)}, f32[128,128]{1,0:T(8,128)}, u32[]{:S(2)}) copy-start(f32[128,128]{1,0:T(8,128)} %constant.4.clone.refs_0_) | copy-start | bytes 196612
  6.5 16.6 %collective-permute-start.2 = (f32[192,256]{1,0:T(8,128)S(1)}, f32[192,256]{1,0:T(8,128)S(1)}, u32[]{:S(2)}, u32[]{:S(2)}) collective-permute-start(f32[192,256]{1,0:T(8,128)S(1)} %get-tuple-element.29), channel_id=1, source_target_pairs={{0,2},{1,3},{2,0},{3,1},{4,6},{5,7},{6,4},{7,5},{8,10},{9,11},{10,... | collective-permute-start | bytes 589832 | tf_op jit(solution)/shard_map/ppermute | solution.py:587
  7.2 1.1 %copy-start.1 = (f32[2,6,8,2048]{3,2,1,0:T(8,128)S(1)}, f32[2,6,8,2048]{3,2,1,0:T(8,128)}, u32[]{:S(2)}) copy-start(f32[2,6,8,2048]{3,2,1,0:T(8,128)} %param.12) | copy-start | bytes 2359300
  8.3 0.7 copy-start.11
  9.0 0.7 copy-start.12
  10.9 4.7 %collective-permute-start = (f32[96,256]{1,0:T(8,128)S(1)}, f32[96,256]{1,0:T(8,128)S(1)}, u32[]{:S(2)}, u32[]{:S(2)}) collective-permute-start(f32[96,256]{1,0:T(8,128)S(1)} %get-tuple-element.27), channel_id=1, source_target_pairs={{0,8},{16,24},{8,0},{24,16},{1,9},{17,25},{9,1},{25,17},{2,10},{18... | collective-permute-start | bytes 294920 | tf_op jit(solution)/shard_map/ppermute | solution.py:604
  12.6 3.0 %collective-permute-start.1 = (f32[96,256]{1,0:T(8,128)S(1)}, f32[96,256]{1,0:T(8,128)S(1)}, u32[]{:S(2)}, u32[]{:S(2)}) collective-permute-start(f32[96,256]{1,0:T(8,128)S(1)} %get-tuple-element.28), channel_id=1, source_target_pairs={{8,16},{16,8},{9,17},{17,9},{10,18},{18,10},{11,19},{19,11},{12,20... | collective-permute-start | bytes 294920 | tf_op jit(solution)/shard_map/ppermute | solution.py:604
  23.6 8.3 %copy-start.2 = (f32[2,6,8,2048]{3,2,1,0:T(8,128)S(1)}, f32[2,6,8,2048]{3,2,1,0:T(8,128)}, u32[]{:S(2)}) copy-start(f32[2,6,8,2048]{3,2,1,0:T(8,128)} %param.12) | copy-start | bytes 2359300
  23.6 8.3 %copy-start.3 = (s32[6,1024]{1,0:T(8,128)S(1)}, s32[6,1024]{1,0:T(8,128)}, u32[]{:S(2)}) copy-start(s32[6,1024]{1,0:T(8,128)} %conn.7) | copy-start | bytes 73732
  23.6 8.3 %copy-start.5 = (f32[6,6,1024]{2,1,0:T(8,128)S(1)}, f32[6,6,1024]{2,1,0:T(8,128)}, u32[]{:S(2)}) copy-start(f32[6,6,1024]{2,1,0:T(8,128)} %stiffness.1) | copy-start | bytes 442372
  23.6 8.3 %copy-start.6 = (f32[6,6,1024]{2,1,0:T(8,128)S(1)}, f32[6,6,1024]{2,1,0:T(8,128)}, u32[]{:S(2)}) copy-start(f32[6,6,1024]{2,1,0:T(8,128)} %mass_r.1) | copy-start | bytes 442372
  23.6 1.8 %collective-permute-start.5 = (f32[384,256]{1,0:T(8,128)S(1)}, f32[384,256]{1,0:T(8,128)S(1)}, u32[]{:S(2)}, u32[]{:S(2)}) collective-permute-start(f32[384,256]{1,0:T(8,128)S(1)} %lower_halves.3), channel_id=1, source_target_pairs={{0,1},{1,0},{2,3},{3,2},{4,5},{5,4},{6,7},{7,6},{8,9},{9,8},{10,11... | collective-permute-start | bytes 1179656 | tf_op jit(solution)/shard_map/ppermute | solution.py:595
  26.5 12.7 %collective-permute-start.9 = (f32[192,256]{1,0:T(8,128)S(1)}, f32[192,256]{1,0:T(8,128)S(1)}, u32[]{:S(2)}, u32[]{:S(2)}) collective-permute-start(f32[192,256]{1,0:T(8,128)S(1)} %get-tuple-element.36), channel_id=1, source_target_pairs={{0,6},{1,7},{2,4},{3,5},{4,2},{5,3},{6,0},{7,1},{8,14},{9,15},{10,... | collective-permute-start | bytes 589832 | tf_op jit(solution)/shard_map/ppermute | solution.py:587
  29.0 16.2 %collective-permute-start.8 = (f32[192,256]{1,0:T(8,128)S(1)}, f32[192,256]{1,0:T(8,128)S(1)}, u32[]{:S(2)}, u32[]{:S(2)}) collective-permute-start(f32[192,256]{1,0:T(8,128)S(1)} %get-tuple-element.32.refs_0_), channel_id=1, source_target_pairs={{0,4},{1,5},{2,6},{3,7},{4,0},{5,1},{6,2},{7,3},{8,12},{9,13},{10,... | collective-permute-start | bytes 589832 | tf_op jit(solution)/shard_map/ppermute | solution.py:587
  29.3 16.3 %collective-permute-start.6 = (f32[192,256]{1,0:T(8,128)S(1)}, f32[192,256]{1,0:T(8,128)S(1)}, u32[]{:S(2)}, u32[]{:S(2)}) collective-permute-start(f32[192,256]{1,0:T(8,128)S(1)} %relay.1.refs_3_), channel_id=1, source_target_pairs={{0,2},{1,3},{2,0},{3,1},{4,6},{5,7},{6,4},{7,5},{8,10},{9,11},{10,... | collective-permute-start | bytes 589832 | tf_op jit(solution)/shard_map/ppermute | solution.py:587
  45.5 1.5 %collective-permute-start.10 = (f32[192,256]{1,0:T(8,128)S(1)}, f32[192,256]{1,0:T(8,128)S(1)}, u32[]{:S(2)}, u32[]{:S(2)}) collective-permute-start(f32[192,256]{1,0:T(8,128)S(1)} %lower_halves.5), channel_id=1, source_target_pairs={{0,1},{1,0},{2,3},{3,2},{4,5},{5,4},{6,7},{7,6},{8,9},{9,8},{10,11... | collective-permute-start | bytes 589832 | tf_op jit(solution)/shard_map/ppermute | solution.py:595
  45.8 1.6 %collective-permute-start.7 = (f32[192,256]{1,0:T(8,128)S(1)}, f32[192,256]{1,0:T(8,128)S(1)}, u32[]{:S(2)}, u32[]{:S(2)}) collective-permute-start(f32[192,256]{1,0:T(8,128)S(1)} %lower_halves.4), channel_id=1, source_target_pairs={{0,1},{1,0},{2,3},{3,2},{4,5},{5,4},{6,7},{7,6},{8,9},{9,8},{10,11... | collective-permute-start | bytes 589832 | tf_op jit(solution)/shard_map/ppermute | solution.py:595
  48.0 7.6 %copy-start.7 = (f32[6,6,1024]{2,1,0:T(8,128)S(1)}, f32[6,6,1024]{2,1,0:T(8,128)}, u32[]{:S(2)}) copy-start(f32[6,6,1024]{2,1,0:T(8,128)} %coupling.1) | copy-start | bytes 442372
  48.0 7.6 %collective-permute-start.11 = (f32[96,256]{1,0:T(8,128)S(1)}, f32[96,256]{1,0:T(8,128)S(1)}, u32[]{:S(2)}, u32[]{:S(2)}) collective-permute-start(f32[96,256]{1,0:T(8,128)S(1)} %get-tuple-element.38), channel_id=1, source_target_pairs={{0,8},{16,24},{8,0},{24,16},{1,9},{17,25},{9,1},{25,17},{2,10},{18... | collective-permute-start | bytes 294920 | tf_op jit(solution)/shard_map/ppermute | solution.py:604
  49.6 6.0 %collective-permute-start.12 = (f32[96,256]{1,0:T(8,128)S(1)}, f32[96,256]{1,0:T(8,128)S(1)}, u32[]{:S(2)}, u32[]{:S(2)}) collective-permute-start(f32[96,256]{1,0:T(8,128)S(1)} %get-tuple-element.39), channel_id=1, source_target_pairs={{8,16},{16,8},{9,17},{17,9},{10,18},{18,10},{11,19},{19,11},{12,20... | collective-permute-start | bytes 294920 | tf_op jit(solution)/shard_map/ppermute | solution.py:604
  60.4 10.7 %copy-start.10 = (f32[2048]{0:T(1024)S(1)}, f32[2048]{0:T(1024)}, u32[]{:S(2)}) copy-start(f32[2048]{0:T(1024)} %param.17) | copy-start | bytes 24580
  60.4 10.7 %collective-permute-start.13 = (f32[96,256]{1,0:T(8,128)S(1)}, f32[96,256]{1,0:T(8,128)S(1)}, u32[]{:S(2)}, u32[]{:S(2)}) collective-permute-start(f32[96,256]{1,0:T(8,128)S(1)} %get-tuple-element.41), channel_id=1, source_target_pairs={{0,8},{16,24},{8,0},{24,16},{1,9},{17,25},{9,1},{25,17},{2,10},{18... | collective-permute-start | bytes 294920 | tf_op jit(solution)/shard_map/ppermute | solution.py:604
  64.7 6.4 %collective-permute-start.14 = (f32[96,256]{1,0:T(8,128)S(1)}, f32[96,256]{1,0:T(8,128)S(1)}, u32[]{:S(2)}, u32[]{:S(2)}) collective-permute-start(f32[96,256]{1,0:T(8,128)S(1)} %get-tuple-element.42), channel_id=1, source_target_pairs={{8,16},{16,8},{9,17},{17,9},{10,18},{18,10},{11,19},{19,11},{12,20... | collective-permute-start | bytes 294920 | tf_op jit(solution)/shard_map/ppermute | solution.py:604

commit v6 on v5

--- a/solution.py
+++ b/solution.py
@@ -120,9 +120,10 @@
     return jnp.concatenate([high, low, high], 0)
 
 
-def transform_kernel(members, mode_dev, fields, *refs):
+def transform_kernel(places, mode_dev, fields, *refs):
     inverse, forward, velocity = refs[:3]
-    blocks = refs[3 : 3 + members]
+    blocks = views(places, refs[3:])
+    members = len(blocks)
     outs = refs[-(members // 2) :]
     pair = 2 * mode_dev
     rows = blocks[0].shape[0]
@@ -152,17 +153,15 @@
 def transform(blocks, velocity, inverse, forward, mode_dev, fields):
     members = len(blocks)
     rows, slab = blocks[0].shape
-    return pl.pallas_call(
-        functools.partial(transform_kernel, members, mode_dev, fields),
-        grid=(1,),
-        in_specs=[whole_block(x.shape) for x in (inverse, forward, velocity)]
-        + specs(blocks),
-        out_specs=[whole_block((2 * rows, slab))] * (members // 2),
+    given, places = operands(blocks)
+    return pl.pallas_call(
+        functools.partial(transform_kernel, places, mode_dev, fields),
+        in_specs=[vmem] * (3 + len(given)),
         out_shape=[jax.ShapeDtypeStruct((2 * rows, slab), f32)] * (members // 2),
         compiler_params=params(),
         cost_estimate=cost(1),
         name="transform",
-    )(inverse, forward, velocity, *arrays(blocks))
+    )(inverse, forward, velocity, *given)
 
 
 def pack_kernel(chips, rows, slab, values, *refs):
@@ -444,21 +443,45 @@
         )
 
 
+def ghost_hot_kernel(first, live, conn, by_slot, by_corner):
+    slots, tile = by_slot.shape[1], by_slot.shape[2] // 6
+    for step in range(by_slot.shape[0]):
+        ids = by_partner(tile_ids(conn, live, step, tile), first, slots // 2)
+        iota = lax.broadcasted_iota(jnp.int32, (slots, tile), 0)
+        for corner in range(6):
+            by_slot[step, :, corner * tile : (corner + 1) * tile] = one_hot(
+                iota, ids[corner : corner + 1, :] - first
+            )
+        fill_scatter(by_corner.at[step], columns_of(ids), first, tile)
+
+
+def ghost_hot(first, slots, live, conn):
+    wide = 6 * ELEM_TILE
+    steps = conn.shape[1] // ELEM_TILE
+    return pl.pallas_call(
+        functools.partial(ghost_hot_kernel, first),
+        in_specs=[smem, vmem],
+        out_shape=[
+            jax.ShapeDtypeStruct((steps, slots, wide), bf16),
+            jax.ShapeDtypeStruct((steps, wide, slots), bf16),
+        ],
+        compiler_params=params(),
+        cost_estimate=cost(3),
+        name="ghost_hot",
+    )(live, conn)
+
+
 def ghost_terms_kernel(
-    first, live, conn, coupling, magnetic_part, electric_part, left, right,
-    terms, left_sums, right_sums, values, hots, hots_columns
+    hots, hots_columns, coupling, magnetic_part, electric_part, left, right,
+    terms, left_sums, right_sums, values
 ):
     tile = terms.shape[2] // 6
     rows, cap = left.shape
     fill_values(values, (left, right))
     sums = None
     for step in range(terms.shape[0]):
-        hot, hot_columns = hots.at[step % 2], hots_columns.at[step % 2]
-        ids = by_partner(tile_ids(conn, live, step, tile), first, cap)
-        fill_gather(hot, ids, (left, right), (first, first + cap), tile)
-        fill_scatter(hot_columns, columns_of(ids), first, tile)
         got = electric_part[step] + halves_sum(
-            jnp.dot(values[...], hot[...], preferred_element_type=f32)
+            jnp.dot(values[...], hots[step], preferred_element_type=f32)
         )
         across = slice(step * tile, (step + 1) * tile)
         for low in range(0, rows, 16):
@@ -470,7 +493,7 @@
                 high = total.astype(bf16)
                 terms[step, low : low + 16, at] = high
                 terms[step, rows + low : rows + low + 16, at] = (total - high.astype(f32)).astype(bf16)
-        part = halves_sum(jnp.dot(terms[step], hot_columns[...], preferred_element_type=f32))
+        part = halves_sum(jnp.dot(terms[step], hots_columns[step], preferred_element_type=f32))
         if step == 0:
             left_sums[...] = part[:, :cap]
             right_sums[...] = part[:, cap:]
@@ -479,26 +502,22 @@
             right_sums[...] += part[:, cap:]
 
 
-def ghost_terms(first, live, conn, coupling, magnetic_part, electric_part, left, right):
+def ghost_terms(hots, coupling, magnetic_part, electric_part, left, right):
     rows, cap = left.shape
     steps, _, wide = electric_part.shape
     return pl.pallas_call(
-        functools.partial(ghost_terms_kernel, first),
-        in_specs=[smem] + [vmem] * 6,
+        ghost_terms_kernel,
+        in_specs=[vmem] * 7,
         out_shape=[
             jax.ShapeDtypeStruct((steps, 2 * rows, wide), bf16),
             jax.ShapeDtypeStruct((rows, cap), f32),
             jax.ShapeDtypeStruct((rows, cap), f32),
         ],
-        scratch_shapes=[
-            pltpu.VMEM((2 * rows, 2 * cap), bf16),
-            pltpu.VMEM((2, 2 * cap, wide), bf16),
-            pltpu.VMEM((2, wide, 2 * cap), bf16),
-        ],
+        scratch_shapes=[pltpu.VMEM((2 * rows, 2 * cap), bf16)],
         compiler_params=params(),
         cost_estimate=cost(8),
         name="ghost_terms",
-    )(live, conn, coupling, magnetic_part, electric_part, left, right)
+    )(*hots, coupling, magnetic_part, electric_part, left, right)
 
 
 def own_sums_kernel(live, conn, terms, out, hots):
@@ -626,7 +645,8 @@
     extended = [own, Block(mag_left, rows), Block(mag_right, rows)]
     steps = tuple(range(members))
     hot, node_hot = interface_hot(counts, interface, node_dev, steps)
-    swapped = between_cores(kept, (mag_left, mag_right, hot))
+    ghost_hots = ghost_hot(node_dev, 2 * cap, elem_live, connect)
+    swapped = between_cores(kept, (mag_left, mag_right, hot, ghost_hots[0]))
     arrived = []
     for t, block in enumerate(kept):
         arrived += [Block(block, rows), Block(swapped, rows, t)]
@@ -647,7 +667,7 @@
     ele_left, ele_right = neighbours(*picked(electric, node_hot))
     electric_part = gathered(electric, steps, elem_live, connect)
     terms, left_sums, right_sums = ghost_terms(
-        node_dev, elem_live, connect, coupling, magnetic_part, electric_part, ele_left, ele_right
+        ghost_hots, coupling, magnetic_part, electric_part, ele_left, ele_right
     )
     sum_left, sum_right = neighbours(left_sums, right_sums)
     sums = own_sums(elem_live, connect, terms, node_dev)

time: 72.9 us -> 72.2 us (level)
  waiting for transfers between devices: 16.7 us -> 13 us
  Pallas kernels: 30.2 us -> 33.2 us
    ppermute x6, waiting for transfers between devices: 13.5 us -> 10.2 us  [between_chips(): lax.ppermute(blocks[t], 'mode', [(k, k ^ 2 * t) for k in range(members)])]
    pallas_call x2 -> x3, Pallas kernels: 5.72 us -> 8.54 us  [the longest x1 3.77 us: ghost_terms(): pl.pallas_call(ghost_terms_kernel, in_specs=[vmem] * 7, out_shape=[jax.Sh...]
  transfers between devices with their start and end apart: 15 -> 15, of which waited for: 6 -> 5; matrix products, arithmetic and copies ran while one was open for 0% -> 0% of each run, Pallas kernels for 30% -> 36%
where the time goes in v6:
time: 72.2 us; the launch traced here: 71.9 us
  Pallas kernels  33.2 us (46%)
  starting transfers between devices  21 us (29%)
  waiting for transfers between devices  13 us (18%)
  local copies, waits for them, and re-layouts  3.65 us (5%)
  between operations  1.16 us (2%)
    ppermute x6, starting transfers between devices, between_chips(): lax.ppermute(blocks[t], 'mode', [(k, k ^ 2 * t) for k in range(members)])  10.3 us
    ppermute x6, waiting for transfers between devices, between_chips(): lax.ppermute(blocks[t], 'mode', [(k, k ^ 2 * t) for k in range(members)])  10.2 us
    ppermute x6, starting transfers between devices, neighbours(): got.append(lax.ppermute(values, 'mesh', pairs))  9.96 us
    pallas_call x1, Pallas kernels, magnetic_terms(): pl.pallas_call(functools.partial(magnetic_terms_kernel, places, mode_dev)...  7.25 us
    pallas_call x1, Pallas kernels, own_sums(): pl.pallas_call(own_sums_kernel, in_specs=[smem, vmem, vmem], out_shape=ja...  5.44 us
    pallas_call x1, Pallas kernels, gathered(): pl.pallas_call(functools.partial(gather_kernel, places, steps), in_specs=...  5.22 us
    pallas_call x1, Pallas kernels, ghost_terms(): pl.pallas_call(ghost_terms_kernel, in_specs=[vmem] * 7, out_shape=[jax.Sh...  3.77 us
    pallas_call x1, Pallas kernels, ghost_hot(): pl.pallas_call(functools.partial(ghost_hot_kernel, first), in_specs=[smem...  3.74 us
  transfers between devices with their start and end apart: 15, of which 5 were waited for; matrix products, arithmetic and copies ran while one was open for 0% of the time, Pallas kernels for 36%

profile of v6, /device:TPU:0, one launch (start us, length us, event | category | flops | bytes accessed | tf_op | source)
XLA Modules:
  0.0 71.9 jit_solution(6272902848123112092)
XLA Ops:
  0.0 1.1 %copy-done = f32[2,6,8,2048]{3,2,1,0:T(8,128)S(1)} copy-done((f32[2,6,8,2048]{3,2,1,0:T(8,128)S(1)}, f32[2,6,8,2048]{3,2,1,0:T(8,128)}, u32[]{:S(2)}) %copy-start) | copy-done | bytes 786456
  1.2 5.1 %collective-permute-start.4 = (f32[192,256]{1,0:T(8,128)S(1)}, f32[192,256]{1,0:T(8,128)S(1)}, u32[]{:S(2)}, u32[]{:S(2)}) collective-permute-start(f32[192,256]{1,0:T(8,128)S(1)} %get-tuple-element.34), channel_id=1, source_target_pairs={{0,6},{1,7},{2,4},{3,5},{4,2},{5,3},{6,0},{7,1},{8,14},{9,15},{10,... | collective-permute-start | bytes 589832 | tf_op jit(solution)/shard_map/ppermute | solution.py:606
  6.5 0.7 collective-permute-start.2
  7.2 1.1 %copy-done.1 = f32[2,6,8,2048]{3,2,1,0:T(8,128)S(1)} copy-done((f32[2,6,8,2048]{3,2,1,0:T(8,128)S(1)}, f32[2,6,8,2048]{3,2,1,0:T(8,128)}, u32[]{:S(2)}) %copy-start.1) | copy-done | bytes 786456
  8.3 0.7 copy-done.11
  9.0 0.7 copy-done.12
  9.6 1.2 %interface_values.1 = (f32[96,256]{1,0:T(8,128)S(1)}, f32[96,256]{1,0:T(8,128)S(1)}) custom-call(s32[1,2]{1,0:T(1,128)S(1)} %copy-done.12, s32[1,512]{1,0:T(1,128)S(1)} %copy-done.11, f32[96,2048]{1,0:T(8,128)S(1)} %bitcast.5, f32[192,256]{1,0:T(8,128)S(1)} %get-tuple-element.30.refs_1_.refs_0_.refs_3_), custom_call_target="tpu_custom_call" | custom-call | bytes 3000000 | tf_op jit(solution)/shard_map/interface_values/pallas_call | solution.py:297
  10.9 1.7 %collective-permute-start = (f32[96,256]{1,0:T(8,128)S(1)}, f32[96,256]{1,0:T(8,128)S(1)}, u32[]{:S(2)}, u32[]{:S(2)}) collective-permute-start(f32[96,256]{1,0:T(8,128)S(1)} %get-tuple-element.31), channel_id=1, source_target_pairs={{0,8},{16,24},{8,0},{24,16},{1,9},{17,25},{9,1},{25,17},{2,10},{18... | collective-permute-start | bytes 294920 | tf_op jit(solution)/shard_map/ppermute | solution.py:623
  12.6 0.7 collective-permute-start.1
  13.2 1.9 %interface_hot.1 = (bf16[512,2048]{1,0:T(8,128)(2,1)S(1)}, bf16[2048,512]{1,0:T(8,128)(2,1)S(1)}) custom-call(s32[1,2]{1,0:T(1,128)S(1)} %copy-done.12, s32[1,512]{1,0:T(1,128)S(1)} %copy-done.11), custom_call_target="tpu_custom_call" | custom-call | bytes 6000000 | tf_op jit(solution)/shard_map/interface_hot/pallas_call | solution.py:557
  15.8 3.7 %ghost_hot.1 = (bf16[4,512,1536]{2,1,0:T(8,128)(2,1)S(1)}, bf16[4,1536,512]{2,1,0:T(8,128)(2,1)S(1)}) custom-call(s32[1]{0:T(128)S(6)} %copy.13.live, s32[6,1024]{1,0:T(8,128)S(1)} %copy-done.3), custom_call_target="tpu_custom_call" | custom-call | bytes 9000000 | tf_op jit(solution)/shard_map/ghost_hot/pallas_call | solution.py:461
  19.6 3.4 %collective-permute-done.3.refs_2_.refs_6_ = f32[192,256]{1,0:T(8,128)S(1)} collective-permute-done((f32[192,256]{1,0:T(8,128)S(1)}, f32[192,256]{1,0:T(8,128)S(1)}, u32[]{:S(2)}, u32[]{:S(2)}) %collective-permute-start.3) | collective-permute-done | bytes 196640 | tf_op jit(solution)/shard_map/ppermute | solution.py:606
  23.1 0.7 %lower_halves.3 = f32[384,256]{1,0:T(8,128)S(1)} custom-call(f32[192,256]{1,0:T(8,128)S(1)} %get-tuple-element.30.refs_1_.refs_0_.refs_3_, f32[192,256]{1,0:T(8,128)S(1)} %collective-permute-done.2.refs_1_.refs_5_, f32[192,256]{1,0:T(8,128)S(1)} %collective-permute-done.3.refs_2_.refs_6_, f32[192,256]{1,0:T(8,128)S(1)} %collective-permute-done.4.refs_3_.refs_7_, ...), custom_call_target="tpu_custom_call" | custom-call | bytes 30000 | tf_op jit(solution)/shard_map/lower_halves/pallas_call | solution.py:239
  23.9 1.7 %collective-permute-done.5.refs_4_ = f32[384,256]{1,0:T(8,128)S(1)} collective-permute-done((f32[384,256]{1,0:T(8,128)S(1)}, f32[384,256]{1,0:T(8,128)S(1)}, u32[]{:S(2)}, u32[]{:S(2)}) %collective-permute-start.5) | collective-permute-done | bytes 393248 | tf_op jit(solution)/shard_map/ppermute | solution.py:614
  25.6 1.0 %transform.1 = (f32[192,256]{1,0:T(8,128)S(1)}, f32[192,256]{1,0:T(8,128)S(1)}, f32[192,256]{1,0:T(8,128)S(1)}, f32[192,256]{1,0:T(8,128)S(1)}) custom-call(f32[128,128]{1,0:T(8,128)S(1)} %copy-done.9, f32[128,128]{1,0:T(8,128)S(1)} %copy-done.8, f32[3,128,256]{2,1,0:T(8,128)S(1)} %copy-done.4, f32[192,256]{1,0:T(8,128)S(1)} %get-tuple-element.30.refs_1_.refs_0_.refs_3_, ...), custom_call_target="tpu_custom_call" | custom-call | bytes 3000000 | tf_op jit(solution)/shard_map/transform/pallas_call | solution.py:157
  26.7 2.5 %collective-permute-start.9 = (f32[192,256]{1,0:T(8,128)S(1)}, f32[192,256]{1,0:T(8,128)S(1)}, u32[]{:S(2)}, u32[]{:S(2)}) collective-permute-start(f32[192,256]{1,0:T(8,128)S(1)} %get-tuple-element.40), channel_id=1, source_target_pairs={{0,6},{1,7},{2,4},{3,5},{4,2},{5,3},{6,0},{7,1},{8,14},{9,15},{10,... | collective-permute-start | bytes 589832 | tf_op jit(solution)/shard_map/ppermute | solution.py:606
  29.5 2.0 %collective-permute-start.6 = (f32[192,256]{1,0:T(8,128)S(1)}, f32[192,256]{1,0:T(8,128)S(1)}, u32[]{:S(2)}, u32[]{:S(2)}) collective-permute-start(f32[192,256]{1,0:T(8,128)S(1)} %relay.1.refs_3_), channel_id=1, source_target_pairs={{0,2},{1,3},{2,0},{3,1},{4,6},{5,7},{6,4},{7,5},{8,10},{9,11},{10,... | collective-permute-start | bytes 589832 | tf_op jit(solution)/shard_map/ppermute | solution.py:606
  31.4 7.2 %magnetic_terms.1 = (f32[4,96,1536]{2,1,0:T(8,128)S(1)}, f32[8,128]{1,0:T(8,128)S(1)}) custom-call(s32[1]{0:T(128)S(6)} %copy.13.live, s32[6,1024]{1,0:T(8,128)S(1)} %copy-done.3, f32[6,6,1024]{2,1,0:T(8,128)S(1)} %copy-done.6, f32[6,6,1024]{2,1,0:T(8,128)S(1)} %copy-done.7, f32[96,2048]{1,0:T(8,128)S(1)} %bitcast.6, ...), custom_call_target="tpu_custom_call" | custom-call | bytes 90000000 | tf_op jit(solution)/shard_map/magnetic_terms/pallas_call | solution.py:388
  38.7 6.7 %collective-permute-done.8.refs_0_.refs_3_ = f32[192,256]{1,0:T(8,128)S(1)} collective-permute-done((f32[192,256]{1,0:T(8,128)S(1)}, f32[192,256]{1,0:T(8,128)S(1)}, u32[]{:S(2)}, u32[]{:S(2)}) %collective-permute-start.8) | collective-permute-done | bytes 196640 | tf_op jit(solution)/shard_map/ppermute | solution.py:606
  45.8 0.3 lower_halves.4
  46.0 0.5 collective-permute-start.7
  46.6 0.6 collective-permute-done.10.refs_4_
  47.2 0.5 collective-permute-done.7.refs_1_
  47.6 0.6 picked.1
  48.3 2.5 %collective-permute-start.11 = (f32[96,256]{1,0:T(8,128)S(1)}, f32[96,256]{1,0:T(8,128)S(1)}, u32[]{:S(2)}, u32[]{:S(2)}) collective-permute-start(f32[96,256]{1,0:T(8,128)S(1)} %get-tuple-element.42), channel_id=1, source_target_pairs={{0,8},{16,24},{8,0},{24,16},{1,9},{17,25},{9,1},{25,17},{2,10},{18... | collective-permute-start | bytes 294920 | tf_op jit(solution)/shard_map/ppermute | solution.py:623
  50.7 0.9 %collective-permute-start.12 = (f32[96,256]{1,0:T(8,128)S(1)}, f32[96,256]{1,0:T(8,128)S(1)}, u32[]{:S(2)}, u32[]{:S(2)}) collective-permute-start(f32[96,256]{1,0:T(8,128)S(1)} %get-tuple-element.43), channel_id=1, source_target_pairs={{8,16},{16,8},{9,17},{17,9},{10,18},{18,10},{11,19},{19,11},{12,20... | collective-permute-start | bytes 294920 | tf_op jit(solution)/shard_map/ppermute | solution.py:623
  51.6 5.2 %gathered.1.electric_part = f32[4,96,1536]{2,1,0:T(8,128)S(1)} custom-call(s32[1]{0:T(128)S(6)} %copy.13.live, s32[6,1024]{1,0:T(8,128)S(1)} %copy-done.3, f32[192,256]{1,0:T(8,128)S(1)} %get-tuple-element.38.refs_0_, f32[192,256]{1,0:T(8,128)S(1)} %collective-permute-done.7.refs_1_, f32[192,256]{1,0:T(8,128)S(1)} %collective-permute-done.6.refs_1_.refs_2_, ...), custom_call_target="tpu_custom_call" | custom-call | bytes 15000000 | tf_op jit(solution)/shard_map/gathered/pallas_call | solution.py:424
  56.9 3.8 %ghost_terms.1 = (bf16[4,192,1536]{2,1,0:T(8,128)(2,1)S(1)}, f32[96,256]{1,0:T(8,128)S(1)}, f32[96,256]{1,0:T(8,128)S(1)}) custom-call(bf16[4,512,1536]{2,1,0:T(8,128)(2,1)S(1)} %get-tuple-element.27.refs_7_.hots, bf16[4,1536,512]{2,1,0:T(8,128)(2,1)S(1)} %get-tuple-element.28.hots_columns, f32[6,6,1024]{2,1,0:T(8,128)S(1)} %copy-done.5, ...), custom_call_target="tpu_custom_call" | custom-call | bytes 24000000 | tf_op jit(solution)/shard_map/ghost_terms/pallas_call | solution.py:508
  60.7 3.3 %collective-permute-start.13 = (f32[96,256]{1,0:T(8,128)S(1)}, f32[96,256]{1,0:T(8,128)S(1)}, u32[]{:S(2)}, u32[]{:S(2)}) collective-permute-start(f32[96,256]{1,0:T(8,128)S(1)} %get-tuple-element.45), channel_id=1, source_target_pairs={{0,8},{16,24},{8,0},{24,16},{1,9},{17,25},{9,1},{25,17},{2,10},{18... | collective-permute-start | bytes 294920 | tf_op jit(solution)/shard_map/ppermute | solution.py:623
  64.0 0.9 %collective-permute-start.14 = (f32[96,256]{1,0:T(8,128)S(1)}, f32[96,256]{1,0:T(8,128)S(1)}, u32[]{:S(2)}, u32[]{:S(2)}) collective-permute-start(f32[96,256]{1,0:T(8,128)S(1)} %get-tuple-element.46), channel_id=1, source_target_pairs={{8,16},{16,8},{9,17},{17,9},{10,18},{18,10},{11,19},{19,11},{12,20... | collective-permute-start | bytes 294920 | tf_op jit(solution)/shard_map/ppermute | solution.py:623
  64.9 5.4 %own_sums.1.sums = f32[96,2048]{1,0:T(8,128)S(1)} custom-call(s32[1]{0:T(128)S(6)} %copy.13.live, s32[6,1024]{1,0:T(8,128)S(1)} %copy-done.3, bf16[4,192,1536]{2,1,0:T(8,128)(2,1)S(1)} %get-tuple-element.44.terms), custom_call_target="tpu_custom_call" | custom-call | bytes 27000000 | tf_op jit(solution)/shard_map/own_sums/pallas_call | solution.py:537
  70.4 1.3 %finish.1 = f32[96,2048]{1,0:T(8,128)} custom-call(bf16[512,2048]{1,0:T(8,128)(2,1)S(1)} %get-tuple-element.26.refs_6_.hot, f32[96,2048]{1,0:T(8,128)S(1)} %bitcast.7, f32[96,2048]{1,0:T(8,128)S(1)} %own_sums.1.sums, f32[96,256]{1,0:T(8,128)S(1)} %collective-permute-done.13.left, f32[96,256]{1,0:T(8,128)S(1)} %collective-permute-done.14.right, ...), custom_call_target="tpu_custom_call" | custom-call | bytes 6000000 | tf_op jit(solution)/shard_map/finish/pallas_call | solution.py:587
  (40 shorter events, 0.9 us)
Async XLA Ops:
  0.0 1.1 %copy-start = (f32[2,6,8,2048]{3,2,1,0:T(8,128)S(1)}, f32[2,6,8,2048]{3,2,1,0:T(8,128)}, u32[]{:S(2)}) copy-start(f32[2,6,8,2048]{3,2,1,0:T(8,128)} %param.12) | copy-start | bytes 2359300
  1.1 14.7 %copy-start.3 = (s32[6,1024]{1,0:T(8,128)S(1)}, s32[6,1024]{1,0:T(8,128)}, u32[]{:S(2)}) copy-start(s32[6,1024]{1,0:T(8,128)} %conn.7) | copy-start | bytes 73732
  1.2 18.4 %collective-permute-start.4 = (f32[192,256]{1,0:T(8,128)S(1)}, f32[192,256]{1,0:T(8,128)S(1)}, u32[]{:S(2)}, u32[]{:S(2)}) collective-permute-start(f32[192,256]{1,0:T(8,128)S(1)} %get-tuple-element.34), channel_id=1, source_target_pairs={{0,6},{1,7},{2,4},{3,5},{4,2},{5,3},{6,0},{7,1},{8,14},{9,15},{10,... | collective-permute-start | bytes 589832 | tf_op jit(solution)/shard_map/ppermute | solution.py:606
  6.4 16.7 %collective-permute-start.3 = (f32[192,256]{1,0:T(8,128)S(1)}, f32[192,256]{1,0:T(8,128)S(1)}, u32[]{:S(2)}, u32[]{:S(2)}) collective-permute-start(f32[192,256]{1,0:T(8,128)S(1)} %get-tuple-element.29.refs_0_), channel_id=1, source_target_pairs={{0,4},{1,5},{2,6},{3,7},{4,0},{5,1},{6,2},{7,3},{8,12},{9,13},{10,... | collective-permute-start | bytes 589832 | tf_op jit(solution)/shard_map/ppermute | solution.py:606
  6.5 16.6 %collective-permute-start.2 = (f32[192,256]{1,0:T(8,128)S(1)}, f32[192,256]{1,0:T(8,128)S(1)}, u32[]{:S(2)}, u32[]{:S(2)}) collective-permute-start(f32[192,256]{1,0:T(8,128)S(1)} %get-tuple-element.33), channel_id=1, source_target_pairs={{0,2},{1,3},{2,0},{3,1},{4,6},{5,7},{6,4},{7,5},{8,10},{9,11},{10,... | collective-permute-start | bytes 589832 | tf_op jit(solution)/shard_map/ppermute | solution.py:606
  7.2 1.1 %copy-start.1 = (f32[2,6,8,2048]{3,2,1,0:T(8,128)S(1)}, f32[2,6,8,2048]{3,2,1,0:T(8,128)}, u32[]{:S(2)}) copy-start(f32[2,6,8,2048]{3,2,1,0:T(8,128)} %param.12) | copy-start | bytes 2359300
  8.3 0.7 copy-start.11
  9.0 0.7 copy-start.12
  10.9 8.7 %collective-permute-start = (f32[96,256]{1,0:T(8,128)S(1)}, f32[96,256]{1,0:T(8,128)S(1)}, u32[]{:S(2)}, u32[]{:S(2)}) collective-permute-start(f32[96,256]{1,0:T(8,128)S(1)} %get-tuple-element.31), channel_id=1, source_target_pairs={{0,8},{16,24},{8,0},{24,16},{1,9},{17,25},{9,1},{25,17},{2,10},{18... | collective-permute-start | bytes 294920 | tf_op jit(solution)/shard_map/ppermute | solution.py:623
  12.6 7.0 %collective-permute-start.1 = (f32[96,256]{1,0:T(8,128)S(1)}, f32[96,256]{1,0:T(8,128)S(1)}, u32[]{:S(2)}, u32[]{:S(2)}) collective-permute-start(f32[96,256]{1,0:T(8,128)S(1)} %get-tuple-element.32), channel_id=1, source_target_pairs={{8,16},{16,8},{9,17},{17,9},{10,18},{18,10},{11,19},{19,11},{12,20... | collective-permute-start | bytes 294920 | tf_op jit(solution)/shard_map/ppermute | solution.py:623
  23.1 2.6 %copy-start.4 = (f32[3,128,256]{2,1,0:T(8,128)S(1)}, f32[3,128,256]{2,1,0:T(8,128)}, u32[]{:S(2)}) copy-start(f32[3,128,256]{2,1,0:T(8,128)} %refs_2_.1) | copy-start | bytes 1179652
  23.1 2.6 %copy-start.8 = (f32[128,128]{1,0:T(8,128)S(1)}, f32[128,128]{1,0:T(8,128)}, u32[]{:S(2)}) copy-start(f32[128,128]{1,0:T(8,128)} %constant.5.clone.refs_1_) | copy-start | bytes 196612
  23.1 2.6 %copy-start.9 = (f32[128,128]{1,0:T(8,128)S(1)}, f32[128,128]{1,0:T(8,128)}, u32[]{:S(2)}) copy-start(f32[128,128]{1,0:T(8,128)} %constant.4.clone.refs_0_) | copy-start | bytes 196612
  23.8 7.6 %copy-start.2 = (f32[2,6,8,2048]{3,2,1,0:T(8,128)S(1)}, f32[2,6,8,2048]{3,2,1,0:T(8,128)}, u32[]{:S(2)}) copy-start(f32[2,6,8,2048]{3,2,1,0:T(8,128)} %param.12) | copy-start | bytes 2359300
  23.8 7.6 %copy-start.6 = (f32[6,6,1024]{2,1,0:T(8,128)S(1)}, f32[6,6,1024]{2,1,0:T(8,128)}, u32[]{:S(2)}) copy-start(f32[6,6,1024]{2,1,0:T(8,128)} %stiffness.1) | copy-start | bytes 442372
  23.8 7.6 %copy-start.7 = (f32[6,6,1024]{2,1,0:T(8,128)S(1)}, f32[6,6,1024]{2,1,0:T(8,128)}, u32[]{:S(2)}) copy-start(f32[6,6,1024]{2,1,0:T(8,128)} %mass_r.1) | copy-start | bytes 442372
  23.8 1.8 %collective-permute-start.5 = (f32[384,256]{1,0:T(8,128)S(1)}, f32[384,256]{1,0:T(8,128)S(1)}, u32[]{:S(2)}, u32[]{:S(2)}) collective-permute-start(f32[384,256]{1,0:T(8,128)S(1)} %lower_halves.3), channel_id=1, source_target_pairs={{0,1},{1,0},{2,3},{3,2},{4,5},{5,4},{6,7},{7,6},{8,9},{9,8},{10,11... | collective-permute-start | bytes 1179656 | tf_op jit(solution)/shard_map/ppermute | solution.py:614
  26.7 12.0 %collective-permute-start.9 = (f32[192,256]{1,0:T(8,128)S(1)}, f32[192,256]{1,0:T(8,128)S(1)}, u32[]{:S(2)}, u32[]{:S(2)}) collective-permute-start(f32[192,256]{1,0:T(8,128)S(1)} %get-tuple-element.40), channel_id=1, source_target_pairs={{0,6},{1,7},{2,4},{3,5},{4,2},{5,3},{6,0},{7,1},{8,14},{9,15},{10,... | collective-permute-start | bytes 589832 | tf_op jit(solution)/shard_map/ppermute | solution.py:606
  29.2 16.2 %collective-permute-start.8 = (f32[192,256]{1,0:T(8,128)S(1)}, f32[192,256]{1,0:T(8,128)S(1)}, u32[]{:S(2)}, u32[]{:S(2)}) collective-permute-start(f32[192,256]{1,0:T(8,128)S(1)} %get-tuple-element.36.refs_0_), channel_id=1, source_target_pairs={{0,4},{1,5},{2,6},{3,7},{4,0},{5,1},{6,2},{7,3},{8,12},{9,13},{10,... | collective-permute-start | bytes 589832 | tf_op jit(solution)/shard_map/ppermute | solution.py:606
  29.5 16.3 %collective-permute-start.6 = (f32[192,256]{1,0:T(8,128)S(1)}, f32[192,256]{1,0:T(8,128)S(1)}, u32[]{:S(2)}, u32[]{:S(2)}) collective-permute-start(f32[192,256]{1,0:T(8,128)S(1)} %relay.1.refs_3_), channel_id=1, source_target_pairs={{0,2},{1,3},{2,0},{3,1},{4,6},{5,7},{6,4},{7,5},{8,10},{9,11},{10,... | collective-permute-start | bytes 589832 | tf_op jit(solution)/shard_map/ppermute | solution.py:606
  45.7 1.5 %collective-permute-start.10 = (f32[192,256]{1,0:T(8,128)S(1)}, f32[192,256]{1,0:T(8,128)S(1)}, u32[]{:S(2)}, u32[]{:S(2)}) collective-permute-start(f32[192,256]{1,0:T(8,128)S(1)} %lower_halves.5), channel_id=1, source_target_pairs={{0,1},{1,0},{2,3},{3,2},{4,5},{5,4},{6,7},{7,6},{8,9},{9,8},{10,11... | collective-permute-start | bytes 589832 | tf_op jit(solution)/shard_map/ppermute | solution.py:614
  46.0 1.6 %collective-permute-start.7 = (f32[192,256]{1,0:T(8,128)S(1)}, f32[192,256]{1,0:T(8,128)S(1)}, u32[]{:S(2)}, u32[]{:S(2)}) collective-permute-start(f32[192,256]{1,0:T(8,128)S(1)} %lower_halves.4), channel_id=1, source_target_pairs={{0,1},{1,0},{2,3},{3,2},{4,5},{5,4},{6,7},{7,6},{8,9},{9,8},{10,11... | collective-permute-start | bytes 589832 | tf_op jit(solution)/shard_map/ppermute | solution.py:614
  48.2 8.6 %copy-start.5 = (f32[6,6,1024]{2,1,0:T(8,128)S(1)}, f32[6,6,1024]{2,1,0:T(8,128)}, u32[]{:S(2)}) copy-start(f32[6,6,1024]{2,1,0:T(8,128)} %coupling.1) | copy-start | bytes 442372
  48.3 8.6 %collective-permute-start.11 = (f32[96,256]{1,0:T(8,128)S(1)}, f32[96,256]{1,0:T(8,128)S(1)}, u32[]{:S(2)}, u32[]{:S(2)}) collective-permute-start(f32[96,256]{1,0:T(8,128)S(1)} %get-tuple-element.42), channel_id=1, source_target_pairs={{0,8},{16,24},{8,0},{24,16},{1,9},{17,25},{9,1},{25,17},{2,10},{18... | collective-permute-start | bytes 294920 | tf_op jit(solution)/shard_map/ppermute | solution.py:623
  50.7 6.1 %collective-permute-start.12 = (f32[96,256]{1,0:T(8,128)S(1)}, f32[96,256]{1,0:T(8,128)S(1)}, u32[]{:S(2)}, u32[]{:S(2)}) collective-permute-start(f32[96,256]{1,0:T(8,128)S(1)} %get-tuple-element.43), channel_id=1, source_target_pairs={{8,16},{16,8},{9,17},{17,9},{10,18},{18,10},{11,19},{19,11},{12,20... | collective-permute-start | bytes 294920 | tf_op jit(solution)/shard_map/ppermute | solution.py:623
  60.7 9.7 %copy-start.10 = (f32[2048]{0:T(1024)S(1)}, f32[2048]{0:T(1024)}, u32[]{:S(2)}) copy-start(f32[2048]{0:T(1024)} %param.17) | copy-start | bytes 24580
  60.7 9.7 %collective-permute-start.13 = (f32[96,256]{1,0:T(8,128)S(1)}, f32[96,256]{1,0:T(8,128)S(1)}, u32[]{:S(2)}, u32[]{:S(2)}) collective-permute-start(f32[96,256]{1,0:T(8,128)S(1)} %get-tuple-element.45), channel_id=1, source_target_pairs={{0,8},{16,24},{8,0},{24,16},{1,9},{17,25},{9,1},{25,17},{2,10},{18... | collective-permute-start | bytes 294920 | tf_op jit(solution)/shard_map/ppermute | solution.py:623
  64.0 6.4 %collective-permute-start.14 = (f32[96,256]{1,0:T(8,128)S(1)}, f32[96,256]{1,0:T(8,128)S(1)}, u32[]{:S(2)}, u32[]{:S(2)}) collective-permute-start(f32[96,256]{1,0:T(8,128)S(1)} %get-tuple-element.46), channel_id=1, source_target_pairs={{8,16},{16,8},{9,17},{17,9},{10,18},{18,10},{11,19},{19,11},{12,20... | collective-permute-start | bytes 294920 | tf_op jit(solution)/shard_map/ppermute | solution.py:623

commit v7 on v6

--- a/solution.py
+++ b/solution.py
@@ -349,9 +349,10 @@
 
 
 def magnetic_terms_kernel(places, mode_dev, live, conn, stiffness, mass_r, *refs):
-    blocks = views(places, refs)
-    out, done, values, hots, operator = refs[-5:]
+    *blocks, slab = views(places, refs)
+    out, slab_part, done, values, hots, operator, slab_values, slab_hots = refs[-8:]
     tile = operator.shape[2]
+    fill_values(slab_values, (slab,))
     done[...] = jnp.zeros_like(done)
     fill_values(values, blocks)
     bases = [0]
@@ -361,7 +362,13 @@
     squares = (own_member() * mode_dev + lax.rem(lane, mode_dev)).astype(f32) ** 2
     for step in range(out.shape[0]):
         hot = hots.at[step % 2]
-        ids = by_partner(tile_ids(conn, live, step, tile), bases[1], blocks[1].shape[1])
+        ids = tile_ids(conn, live, step, tile)
+        slab_hot = slab_hots.at[step % 2]
+        fill_gather(slab_hot, ids, (slab,), (base_of(0, slab.shape[1]),), tile)
+        slab_part[step] = halves_sum(
+            jnp.dot(slab_values[...], slab_hot[...], preferred_element_type=f32)
+        )
+        ids = by_partner(ids, bases[1], blocks[1].shape[1])
         fill_gather(hot, ids, blocks, bases, tile)
         got = halves_sum(jnp.dot(values[...], hot[...], preferred_element_type=f32))
         at = slice(step * tile, (step + 1) * tile)
@@ -379,16 +386,17 @@
                 out[step, low : low + 8, a * tile : (a + 1) * tile] = total
 
 
-def magnetic_terms(blocks, mode_dev, live, conn, stiffness, mass_r, after):
+def magnetic_terms(blocks, slab, mode_dev, live, conn, stiffness, mass_r, after):
     rows = blocks[0].shape[0]
     elems = conn.shape[1]
     tile = ELEM_TILE
     total = sum(block.shape[1] for block in blocks)
-    given, places = operands(blocks)
+    given, places = operands(blocks + [slab])
     return pl.pallas_call(
         functools.partial(magnetic_terms_kernel, places, mode_dev),
         in_specs=[smem] + [vmem] * (3 + len(given)) + [anywhere] * len(after),
         out_shape=[
+            jax.ShapeDtypeStruct((elems // tile, rows, 6 * tile), f32),
             jax.ShapeDtypeStruct((elems // tile, rows, 6 * tile), f32),
             jax.ShapeDtypeStruct((8, 128), f32),
         ],
@@ -396,6 +404,8 @@
             pltpu.VMEM((2 * rows, total), bf16),
             pltpu.VMEM((2, total, 6 * tile), bf16),
             pltpu.VMEM((36, 8, tile), f32),
+            pltpu.VMEM((2 * rows, slab.shape[1]), bf16),
+            pltpu.VMEM((2, slab.shape[1], 6 * tile), bf16),
         ],
         compiler_params=params(28 << 20),
         cost_estimate=cost(30),
@@ -403,7 +413,7 @@
     )(live, conn, stiffness, mass_r, *given, *after)
 
 
-def gather_kernel(places, steps, live, conn, *refs):
+def gather_kernel(places, steps, live, conn, earlier, *refs):
     blocks = views(places, refs)
     out, values, hots = refs[-3:]
     tile = out.shape[2] // 6
@@ -412,10 +422,12 @@
     for step in range(out.shape[0]):
         hot = hots.at[step % 2]
         fill_gather(hot, tile_ids(conn, live, step, tile), blocks, bases, tile)
-        out[step] = halves_sum(jnp.dot(values[...], hot[...], preferred_element_type=f32))
-
-
-def gathered(blocks, steps, live, conn):
+        out[step] = earlier[step] + halves_sum(
+            jnp.dot(values[...], hot[...], preferred_element_type=f32)
+        )
+
+
+def gathered(blocks, steps, live, conn, earlier):
     rows = blocks[0].shape[0]
     elems = conn.shape[1]
     tile = ELEM_TILE
@@ -423,7 +435,7 @@
     given, places = operands(blocks)
     return pl.pallas_call(
         functools.partial(gather_kernel, places, steps),
-        in_specs=[smem] + [vmem] * (1 + len(given)),
+        in_specs=[smem] + [vmem] * (2 + len(given)),
         out_shape=jax.ShapeDtypeStruct((elems // tile, rows, 6 * tile), f32),
         scratch_shapes=[
             pltpu.VMEM((2 * rows, total), bf16),
@@ -432,7 +444,7 @@
         compiler_params=params(28 << 20),
         cost_estimate=cost(5),
         name="gathered",
-    )(live, conn, *given)
+    )(live, conn, earlier, *given)
 
 
 def fill_scatter(hot, conn_columns, first, tile):
@@ -654,8 +666,8 @@
     sent = list(transform(arrived, velocity, inverse, forward, mode_dev, fields))
     sent[1] = relay(sent[1], (sent[2],))
     kept = between_chips(sent)
-    magnetic_part, done = magnetic_terms(
-        extended, mode_dev, elem_live, connect, stiffness, mass_r, (sent[1],)
+    magnetic_part, slab_part, done = magnetic_terms(
+        extended, Block(sent[0], rows), mode_dev, elem_live, connect, stiffness, mass_r, (sent[1],)
     )
     electric = []
     swapped = between_cores(kept[:2], (done,))
@@ -665,7 +677,7 @@
     for t, block in enumerate(kept[2:]):
         electric += [Block(block, rows), Block(swapped, rows, t)]
     ele_left, ele_right = neighbours(*picked(electric, node_hot))
-    electric_part = gathered(electric, steps, elem_live, connect)
+    electric_part = gathered(electric[1:], steps[1:], elem_live, connect, slab_part)
     terms, left_sums, right_sums = ghost_terms(
         ghost_hots, coupling, magnetic_part, electric_part, ele_left, ele_right
     )

time: 72.2 us -> 71.7 us (level)
  no operation moved by 1% of the time
where the time goes in v7:
time: 71.7 us; the launch traced here: 71.4 us
  Pallas kernels  33.1 us (46%)
  starting transfers between devices  21 us (29%)
  waiting for transfers between devices  12.4 us (17%)
  local copies, waits for them, and re-layouts  3.65 us (5%)
  between operations  1.16 us (2%)
    ppermute x6, starting transfers between devices, between_chips(): lax.ppermute(blocks[t], 'mode', [(k, k ^ 2 * t) for k in range(members)])  10.3 us
    ppermute x6, starting transfers between devices, neighbours(): got.append(lax.ppermute(values, 'mesh', pairs))  10.1 us
    ppermute x6, waiting for transfers between devices, between_chips(): lax.ppermute(blocks[t], 'mode', [(k, k ^ 2 * t) for k in range(members)])  9.64 us
    pallas_call x1, Pallas kernels, magnetic_terms(): pl.pallas_call(functools.partial(magnetic_terms_kernel, places, mode_dev)...  7.76 us
    pallas_call x1, Pallas kernels, own_sums(): pl.pallas_call(own_sums_kernel, in_specs=[smem, vmem, vmem], out_shape=ja...  5.44 us
    pallas_call x1, Pallas kernels, gathered(): pl.pallas_call(functools.partial(gather_kernel, places, steps), in_specs=...  4.57 us
    pallas_call x1, Pallas kernels, ghost_terms(): pl.pallas_call(ghost_terms_kernel, in_specs=[vmem] * 7, out_shape=[jax.Sh...  3.77 us
    pallas_call x1, Pallas kernels, ghost_hot(): pl.pallas_call(functools.partial(ghost_hot_kernel, first), in_specs=[smem...  3.74 us
  transfers between devices with their start and end apart: 15, of which 5 were waited for; matrix products, arithmetic and copies ran while one was open for 0% of the time, Pallas kernels for 36%

profile of v7, /device:TPU:0, one launch (start us, length us, event | category | flops | bytes accessed | tf_op | source)
XLA Modules:
  0.0 71.4 jit_solution(14424496112241494929)
XLA Ops:
  0.0 1.1 %copy-done = f32[2,6,8,2048]{3,2,1,0:T(8,128)S(1)} copy-done((f32[2,6,8,2048]{3,2,1,0:T(8,128)S(1)}, f32[2,6,8,2048]{3,2,1,0:T(8,128)}, u32[]{:S(2)}) %copy-start) | copy-done | bytes 786456
  1.2 5.1 %collective-permute-start.4 = (f32[192,256]{1,0:T(8,128)S(1)}, f32[192,256]{1,0:T(8,128)S(1)}, u32[]{:S(2)}, u32[]{:S(2)}) collective-permute-start(f32[192,256]{1,0:T(8,128)S(1)} %get-tuple-element.35), channel_id=1, source_target_pairs={{0,6},{1,7},{2,4},{3,5},{4,2},{5,3},{6,0},{7,1},{8,14},{9,15},{10,... | collective-permute-start | bytes 589832 | tf_op jit(solution)/shard_map/ppermute | solution.py:618
  6.5 0.7 collective-permute-start.2
  7.2 1.1 %copy-done.1 = f32[2,6,8,2048]{3,2,1,0:T(8,128)S(1)} copy-done((f32[2,6,8,2048]{3,2,1,0:T(8,128)S(1)}, f32[2,6,8,2048]{3,2,1,0:T(8,128)}, u32[]{:S(2)}) %copy-start.1) | copy-done | bytes 786456
  8.3 0.7 copy-done.11
  9.0 0.7 copy-done.12
  9.6 1.2 %interface_values.1 = (f32[96,256]{1,0:T(8,128)S(1)}, f32[96,256]{1,0:T(8,128)S(1)}) custom-call(s32[1,2]{1,0:T(1,128)S(1)} %copy-done.12, s32[1,512]{1,0:T(1,128)S(1)} %copy-done.11, f32[96,2048]{1,0:T(8,128)S(1)} %bitcast.5, f32[192,256]{1,0:T(8,128)S(1)} %get-tuple-element.31.refs_1_.refs_0_.refs_3_), custom_call_target="tpu_custom_call" | custom-call | bytes 3000000 | tf_op jit(solution)/shard_map/interface_values/pallas_call | solution.py:297
  10.9 1.7 %collective-permute-start = (f32[96,256]{1,0:T(8,128)S(1)}, f32[96,256]{1,0:T(8,128)S(1)}, u32[]{:S(2)}, u32[]{:S(2)}) collective-permute-start(f32[96,256]{1,0:T(8,128)S(1)} %get-tuple-element.32), channel_id=1, source_target_pairs={{0,8},{16,24},{8,0},{24,16},{1,9},{17,25},{9,1},{25,17},{2,10},{18... | collective-permute-start | bytes 294920 | tf_op jit(solution)/shard_map/ppermute | solution.py:635
  12.6 0.7 collective-permute-start.1
  13.2 1.9 %interface_hot.1 = (bf16[512,2048]{1,0:T(8,128)(2,1)S(1)}, bf16[2048,512]{1,0:T(8,128)(2,1)S(1)}) custom-call(s32[1,2]{1,0:T(1,128)S(1)} %copy-done.12, s32[1,512]{1,0:T(1,128)S(1)} %copy-done.11), custom_call_target="tpu_custom_call" | custom-call | bytes 6000000 | tf_op jit(solution)/shard_map/interface_hot/pallas_call | solution.py:569
  15.8 3.7 %ghost_hot.1 = (bf16[4,512,1536]{2,1,0:T(8,128)(2,1)S(1)}, bf16[4,1536,512]{2,1,0:T(8,128)(2,1)S(1)}) custom-call(s32[1]{0:T(128)S(6)} %copy.13.live, s32[6,1024]{1,0:T(8,128)S(1)} %copy-done.3), custom_call_target="tpu_custom_call" | custom-call | bytes 9000000 | tf_op jit(solution)/shard_map/ghost_hot/pallas_call | solution.py:473
  19.6 3.4 %collective-permute-done.3.refs_2_.refs_6_ = f32[192,256]{1,0:T(8,128)S(1)} collective-permute-done((f32[192,256]{1,0:T(8,128)S(1)}, f32[192,256]{1,0:T(8,128)S(1)}, u32[]{:S(2)}, u32[]{:S(2)}) %collective-permute-start.3) | collective-permute-done | bytes 196640 | tf_op jit(solution)/shard_map/ppermute | solution.py:618
  23.1 0.7 %lower_halves.3 = f32[384,256]{1,0:T(8,128)S(1)} custom-call(f32[192,256]{1,0:T(8,128)S(1)} %get-tuple-element.31.refs_1_.refs_0_.refs_3_, f32[192,256]{1,0:T(8,128)S(1)} %collective-permute-done.2.refs_1_.refs_5_, f32[192,256]{1,0:T(8,128)S(1)} %collective-permute-done.3.refs_2_.refs_6_, f32[192,256]{1,0:T(8,128)S(1)} %collective-permute-done.4.refs_3_.refs_7_, ...), custom_call_target="tpu_custom_call" | custom-call | bytes 30000 | tf_op jit(solution)/shard_map/lower_halves/pallas_call | solution.py:239
  23.9 1.7 %collective-permute-done.5.refs_4_ = f32[384,256]{1,0:T(8,128)S(1)} collective-permute-done((f32[384,256]{1,0:T(8,128)S(1)}, f32[384,256]{1,0:T(8,128)S(1)}, u32[]{:S(2)}, u32[]{:S(2)}) %collective-permute-start.5) | collective-permute-done | bytes 393248 | tf_op jit(solution)/shard_map/ppermute | solution.py:626
  25.6 1.0 %transform.1 = (f32[192,256]{1,0:T(8,128)S(1)}, f32[192,256]{1,0:T(8,128)S(1)}, f32[192,256]{1,0:T(8,128)S(1)}, f32[192,256]{1,0:T(8,128)S(1)}) custom-call(f32[128,128]{1,0:T(8,128)S(1)} %copy-done.9, f32[128,128]{1,0:T(8,128)S(1)} %copy-done.8, f32[3,128,256]{2,1,0:T(8,128)S(1)} %copy-done.4, f32[192,256]{1,0:T(8,128)S(1)} %get-tuple-element.31.refs_1_.refs_0_.refs_3_, ...), custom_call_target="tpu_custom_call" | custom-call | bytes 3000000 | tf_op jit(solution)/shard_map/transform/pallas_call | solution.py:157
  26.7 2.5 %collective-permute-start.9 = (f32[192,256]{1,0:T(8,128)S(1)}, f32[192,256]{1,0:T(8,128)S(1)}, u32[]{:S(2)}, u32[]{:S(2)}) collective-permute-start(f32[192,256]{1,0:T(8,128)S(1)} %get-tuple-element.42), channel_id=1, source_target_pairs={{0,6},{1,7},{2,4},{3,5},{4,2},{5,3},{6,0},{7,1},{8,14},{9,15},{10,... | collective-permute-start | bytes 589832 | tf_op jit(solution)/shard_map/ppermute | solution.py:618
  29.5 2.0 %collective-permute-start.6 = (f32[192,256]{1,0:T(8,128)S(1)}, f32[192,256]{1,0:T(8,128)S(1)}, u32[]{:S(2)}, u32[]{:S(2)}) collective-permute-start(f32[192,256]{1,0:T(8,128)S(1)} %relay.1.refs_4_), channel_id=1, source_target_pairs={{0,2},{1,3},{2,0},{3,1},{4,6},{5,7},{6,4},{7,5},{8,10},{9,11},{10,... | collective-permute-start | bytes 589832 | tf_op jit(solution)/shard_map/ppermute | solution.py:618
  31.4 7.8 %magnetic_terms.1 = (f32[4,96,1536]{2,1,0:T(8,128)S(1)}, f32[4,96,1536]{2,1,0:T(8,128)S(1)}, f32[8,128]{1,0:T(8,128)S(1)}) custom-call(s32[1]{0:T(128)S(6)} %copy.13.live, s32[6,1024]{1,0:T(8,128)S(1)} %copy-done.3, f32[6,6,1024]{2,1,0:T(8,128)S(1)} %copy-done.6, f32[6,6,1024]{2,1,0:T(8,128)S(1)} %copy-done.7, f32[96,2048]{1,0:T(8,128)S(1)} %bitcast.6, ...), custom_call_target="tpu_custom_call" | custom-call | bytes 90000000 | tf_op jit(solution)/shard_map/magnetic_terms/pallas_call | solution.py:395
  39.2 6.2 %collective-permute-done.8.refs_0_.refs_2_.refs_3_ = f32[192,256]{1,0:T(8,128)S(1)} collective-permute-done((f32[192,256]{1,0:T(8,128)S(1)}, f32[192,256]{1,0:T(8,128)S(1)}, u32[]{:S(2)}, u32[]{:S(2)}) %collective-permute-start.8) | collective-permute-done | bytes 196640 | tf_op jit(solution)/shard_map/ppermute | solution.py:618
  45.7 0.3 lower_halves.4
  46.0 0.5 collective-permute-start.7
  46.6 0.6 collective-permute-done.10.refs_3_.refs_4_
  47.2 0.5 collective-permute-done.7.refs_0_.refs_1_
  47.6 0.6 picked.1
  48.2 2.5 %collective-permute-start.11 = (f32[96,256]{1,0:T(8,128)S(1)}, f32[96,256]{1,0:T(8,128)S(1)}, u32[]{:S(2)}, u32[]{:S(2)}) collective-permute-start(f32[96,256]{1,0:T(8,128)S(1)} %get-tuple-element.44), channel_id=1, source_target_pairs={{0,8},{16,24},{8,0},{24,16},{1,9},{17,25},{9,1},{25,17},{2,10},{18... | collective-permute-start | bytes 294920 | tf_op jit(solution)/shard_map/ppermute | solution.py:635
  50.7 0.9 %collective-permute-start.12 = (f32[96,256]{1,0:T(8,128)S(1)}, f32[96,256]{1,0:T(8,128)S(1)}, u32[]{:S(2)}, u32[]{:S(2)}) collective-permute-start(f32[96,256]{1,0:T(8,128)S(1)} %get-tuple-element.45), channel_id=1, source_target_pairs={{8,16},{16,8},{9,17},{17,9},{10,18},{18,10},{11,19},{19,11},{12,20... | collective-permute-start | bytes 294920 | tf_op jit(solution)/shard_map/ppermute | solution.py:635
  51.6 4.6 %gathered.1.electric_part = f32[4,96,1536]{2,1,0:T(8,128)S(1)} custom-call(s32[1]{0:T(128)S(6)} %copy.13.live, s32[6,1024]{1,0:T(8,128)S(1)} %copy-done.3, f32[4,96,1536]{2,1,0:T(8,128)S(1)} %get-tuple-element.40.earlier, f32[192,256]{1,0:T(8,128)S(1)} %collective-permute-done.7.refs_0_.refs_1_, f32[192,256]{1,0:T(8,128)S(1)} %collective-permute-done.6.refs_1_.refs_2_, ...), custom_call_target="tpu_custom_call" | custom-call | bytes 15000000 | tf_op jit(solution)/shard_map/gathered/pallas_call | solution.py:436
  56.3 3.8 %ghost_terms.1 = (bf16[4,192,1536]{2,1,0:T(8,128)(2,1)S(1)}, f32[96,256]{1,0:T(8,128)S(1)}, f32[96,256]{1,0:T(8,128)S(1)}) custom-call(bf16[4,512,1536]{2,1,0:T(8,128)(2,1)S(1)} %get-tuple-element.28.refs_7_.hots, bf16[4,1536,512]{2,1,0:T(8,128)(2,1)S(1)} %get-tuple-element.29.hots_columns, f32[6,6,1024]{2,1,0:T(8,128)S(1)} %copy-done.5, ...), custom_call_target="tpu_custom_call" | custom-call | bytes 24000000 | tf_op jit(solution)/shard_map/ghost_terms/pallas_call | solution.py:520
  60.0 3.4 %collective-permute-start.13 = (f32[96,256]{1,0:T(8,128)S(1)}, f32[96,256]{1,0:T(8,128)S(1)}, u32[]{:S(2)}, u32[]{:S(2)}) collective-permute-start(f32[96,256]{1,0:T(8,128)S(1)} %get-tuple-element.47), channel_id=1, source_target_pairs={{0,8},{16,24},{8,0},{24,16},{1,9},{17,25},{9,1},{25,17},{2,10},{18... | collective-permute-start | bytes 294920 | tf_op jit(solution)/shard_map/ppermute | solution.py:635
  63.4 0.9 %collective-permute-start.14 = (f32[96,256]{1,0:T(8,128)S(1)}, f32[96,256]{1,0:T(8,128)S(1)}, u32[]{:S(2)}, u32[]{:S(2)}) collective-permute-start(f32[96,256]{1,0:T(8,128)S(1)} %get-tuple-element.48), channel_id=1, source_target_pairs={{8,16},{16,8},{9,17},{17,9},{10,18},{18,10},{11,19},{19,11},{12,20... | collective-permute-start | bytes 294920 | tf_op jit(solution)/shard_map/ppermute | solution.py:635
  64.4 5.4 %own_sums.1.sums = f32[96,2048]{1,0:T(8,128)S(1)} custom-call(s32[1]{0:T(128)S(6)} %copy.13.live, s32[6,1024]{1,0:T(8,128)S(1)} %copy-done.3, bf16[4,192,1536]{2,1,0:T(8,128)(2,1)S(1)} %get-tuple-element.46.terms), custom_call_target="tpu_custom_call" | custom-call | bytes 27000000 | tf_op jit(solution)/shard_map/own_sums/pallas_call | solution.py:549
  69.8 1.3 %finish.1 = f32[96,2048]{1,0:T(8,128)} custom-call(bf16[512,2048]{1,0:T(8,128)(2,1)S(1)} %get-tuple-element.27.refs_6_.hot, f32[96,2048]{1,0:T(8,128)S(1)} %bitcast.7, f32[96,2048]{1,0:T(8,128)S(1)} %own_sums.1.sums, f32[96,256]{1,0:T(8,128)S(1)} %collective-permute-done.13.left, f32[96,256]{1,0:T(8,128)S(1)} %collective-permute-done.14.right, ...), custom_call_target="tpu_custom_call" | custom-call | bytes 6000000 | tf_op jit(solution)/shard_map/finish/pallas_call | solution.py:599
  (40 shorter events, 0.9 us)
Async XLA Ops:
  0.0 1.1 %copy-start = (f32[2,6,8,2048]{3,2,1,0:T(8,128)S(1)}, f32[2,6,8,2048]{3,2,1,0:T(8,128)}, u32[]{:S(2)}) copy-start(f32[2,6,8,2048]{3,2,1,0:T(8,128)} %param.12) | copy-start | bytes 2359300
  1.1 14.7 %copy-start.3 = (s32[6,1024]{1,0:T(8,128)S(1)}, s32[6,1024]{1,0:T(8,128)}, u32[]{:S(2)}) copy-start(s32[6,1024]{1,0:T(8,128)} %conn.7) | copy-start | bytes 73732
  1.2 18.4 %collective-permute-start.4 = (f32[192,256]{1,0:T(8,128)S(1)}, f32[192,256]{1,0:T(8,128)S(1)}, u32[]{:S(2)}, u32[]{:S(2)}) collective-permute-start(f32[192,256]{1,0:T(8,128)S(1)} %get-tuple-element.35), channel_id=1, source_target_pairs={{0,6},{1,7},{2,4},{3,5},{4,2},{5,3},{6,0},{7,1},{8,14},{9,15},{10,... | collective-permute-start | bytes 589832 | tf_op jit(solution)/shard_map/ppermute | solution.py:618
  6.4 16.7 %collective-permute-start.3 = (f32[192,256]{1,0:T(8,128)S(1)}, f32[192,256]{1,0:T(8,128)S(1)}, u32[]{:S(2)}, u32[]{:S(2)}) collective-permute-start(f32[192,256]{1,0:T(8,128)S(1)} %get-tuple-element.30.refs_0_), channel_id=1, source_target_pairs={{0,4},{1,5},{2,6},{3,7},{4,0},{5,1},{6,2},{7,3},{8,12},{9,13},{10,... | collective-permute-start | bytes 589832 | tf_op jit(solution)/shard_map/ppermute | solution.py:618
  6.5 16.6 %collective-permute-start.2 = (f32[192,256]{1,0:T(8,128)S(1)}, f32[192,256]{1,0:T(8,128)S(1)}, u32[]{:S(2)}, u32[]{:S(2)}) collective-permute-start(f32[192,256]{1,0:T(8,128)S(1)} %get-tuple-element.34), channel_id=1, source_target_pairs={{0,2},{1,3},{2,0},{3,1},{4,6},{5,7},{6,4},{7,5},{8,10},{9,11},{10,... | collective-permute-start | bytes 589832 | tf_op jit(solution)/shard_map/ppermute | solution.py:618
  7.2 1.1 %copy-start.1 = (f32[2,6,8,2048]{3,2,1,0:T(8,128)S(1)}, f32[2,6,8,2048]{3,2,1,0:T(8,128)}, u32[]{:S(2)}) copy-start(f32[2,6,8,2048]{3,2,1,0:T(8,128)} %param.12) | copy-start | bytes 2359300
  8.3 0.7 copy-start.11
  9.0 0.7 copy-start.12
  10.9 8.7 %collective-permute-start = (f32[96,256]{1,0:T(8,128)S(1)}, f32[96,256]{1,0:T(8,128)S(1)}, u32[]{:S(2)}, u32[]{:S(2)}) collective-permute-start(f32[96,256]{1,0:T(8,128)S(1)} %get-tuple-element.32), channel_id=1, source_target_pairs={{0,8},{16,24},{8,0},{24,16},{1,9},{17,25},{9,1},{25,17},{2,10},{18... | collective-permute-start | bytes 294920 | tf_op jit(solution)/shard_map/ppermute | solution.py:635
  12.6 7.0 %collective-permute-start.1 = (f32[96,256]{1,0:T(8,128)S(1)}, f32[96,256]{1,0:T(8,128)S(1)}, u32[]{:S(2)}, u32[]{:S(2)}) collective-permute-start(f32[96,256]{1,0:T(8,128)S(1)} %get-tuple-element.33), channel_id=1, source_target_pairs={{8,16},{16,8},{9,17},{17,9},{10,18},{18,10},{11,19},{19,11},{12,20... | collective-permute-start | bytes 294920 | tf_op jit(solution)/shard_map/ppermute | solution.py:635
  23.1 2.6 %copy-start.4 = (f32[3,128,256]{2,1,0:T(8,128)S(1)}, f32[3,128,256]{2,1,0:T(8,128)}, u32[]{:S(2)}) copy-start(f32[3,128,256]{2,1,0:T(8,128)} %refs_2_.1) | copy-start | bytes 1179652
  23.1 2.6 %copy-start.8 = (f32[128,128]{1,0:T(8,128)S(1)}, f32[128,128]{1,0:T(8,128)}, u32[]{:S(2)}) copy-start(f32[128,128]{1,0:T(8,128)} %constant.5.clone.refs_1_) | copy-start | bytes 196612
  23.1 2.6 %copy-start.9 = (f32[128,128]{1,0:T(8,128)S(1)}, f32[128,128]{1,0:T(8,128)}, u32[]{:S(2)}) copy-start(f32[128,128]{1,0:T(8,128)} %constant.4.clone.refs_0_) | copy-start | bytes 196612
  23.8 7.6 %copy-start.2 = (f32[2,6,8,2048]{3,2,1,0:T(8,128)S(1)}, f32[2,6,8,2048]{3,2,1,0:T(8,128)}, u32[]{:S(2)}) copy-start(f32[2,6,8,2048]{3,2,1,0:T(8,128)} %param.12) | copy-start | bytes 2359300
  23.8 7.6 %copy-start.6 = (f32[6,6,1024]{2,1,0:T(8,128)S(1)}, f32[6,6,1024]{2,1,0:T(8,128)}, u32[]{:S(2)}) copy-start(f32[6,6,1024]{2,1,0:T(8,128)} %stiffness.1) | copy-start | bytes 442372
  23.8 7.6 %copy-start.7 = (f32[6,6,1024]{2,1,0:T(8,128)S(1)}, f32[6,6,1024]{2,1,0:T(8,128)}, u32[]{:S(2)}) copy-start(f32[6,6,1024]{2,1,0:T(8,128)} %mass_r.1) | copy-start | bytes 442372
  23.8 1.8 %collective-permute-start.5 = (f32[384,256]{1,0:T(8,128)S(1)}, f32[384,256]{1,0:T(8,128)S(1)}, u32[]{:S(2)}, u32[]{:S(2)}) collective-permute-start(f32[384,256]{1,0:T(8,128)S(1)} %lower_halves.3), channel_id=1, source_target_pairs={{0,1},{1,0},{2,3},{3,2},{4,5},{5,4},{6,7},{7,6},{8,9},{9,8},{10,11... | collective-permute-start | bytes 1179656 | tf_op jit(solution)/shard_map/ppermute | solution.py:626
  26.7 12.5 %collective-permute-start.9 = (f32[192,256]{1,0:T(8,128)S(1)}, f32[192,256]{1,0:T(8,128)S(1)}, u32[]{:S(2)}, u32[]{:S(2)}) collective-permute-start(f32[192,256]{1,0:T(8,128)S(1)} %get-tuple-element.42), channel_id=1, source_target_pairs={{0,6},{1,7},{2,4},{3,5},{4,2},{5,3},{6,0},{7,1},{8,14},{9,15},{10,... | collective-permute-start | bytes 589832 | tf_op jit(solution)/shard_map/ppermute | solution.py:618
  29.2 16.2 %collective-permute-start.8 = (f32[192,256]{1,0:T(8,128)S(1)}, f32[192,256]{1,0:T(8,128)S(1)}, u32[]{:S(2)}, u32[]{:S(2)}) collective-permute-start(f32[192,256]{1,0:T(8,128)S(1)} %get-tuple-element.38.refs_0_), channel_id=1, source_target_pairs={{0,4},{1,5},{2,6},{3,7},{4,0},{5,1},{6,2},{7,3},{8,12},{9,13},{10,... | collective-permute-start | bytes 589832 | tf_op jit(solution)/shard_map/ppermute | solution.py:618
  29.5 16.3 %collective-permute-start.6 = (f32[192,256]{1,0:T(8,128)S(1)}, f32[192,256]{1,0:T(8,128)S(1)}, u32[]{:S(2)}, u32[]{:S(2)}) collective-permute-start(f32[192,256]{1,0:T(8,128)S(1)} %relay.1.refs_4_), channel_id=1, source_target_pairs={{0,2},{1,3},{2,0},{3,1},{4,6},{5,7},{6,4},{7,5},{8,10},{9,11},{10,... | collective-permute-start | bytes 589832 | tf_op jit(solution)/shard_map/ppermute | solution.py:618
  45.7 1.5 %collective-permute-start.10 = (f32[192,256]{1,0:T(8,128)S(1)}, f32[192,256]{1,0:T(8,128)S(1)}, u32[]{:S(2)}, u32[]{:S(2)}) collective-permute-start(f32[192,256]{1,0:T(8,128)S(1)} %lower_halves.5), channel_id=1, source_target_pairs={{0,1},{1,0},{2,3},{3,2},{4,5},{5,4},{6,7},{7,6},{8,9},{9,8},{10,11... | collective-permute-start | bytes 589832 | tf_op jit(solution)/shard_map/ppermute | solution.py:626
  46.0 1.6 %collective-permute-start.7 = (f32[192,256]{1,0:T(8,128)S(1)}, f32[192,256]{1,0:T(8,128)S(1)}, u32[]{:S(2)}, u32[]{:S(2)}) collective-permute-start(f32[192,256]{1,0:T(8,128)S(1)} %lower_halves.4), channel_id=1, source_target_pairs={{0,1},{1,0},{2,3},{3,2},{4,5},{5,4},{6,7},{7,6},{8,9},{9,8},{10,11... | collective-permute-start | bytes 589832 | tf_op jit(solution)/shard_map/ppermute | solution.py:626
  48.2 8.0 %collective-permute-start.11 = (f32[96,256]{1,0:T(8,128)S(1)}, f32[96,256]{1,0:T(8,128)S(1)}, u32[]{:S(2)}, u32[]{:S(2)}) collective-permute-start(f32[96,256]{1,0:T(8,128)S(1)} %get-tuple-element.44), channel_id=1, source_target_pairs={{0,8},{16,24},{8,0},{24,16},{1,9},{17,25},{9,1},{25,17},{2,10},{18... | collective-permute-start | bytes 294920 | tf_op jit(solution)/shard_map/ppermute | solution.py:635
  50.7 5.5 %collective-permute-start.12 = (f32[96,256]{1,0:T(8,128)S(1)}, f32[96,256]{1,0:T(8,128)S(1)}, u32[]{:S(2)}, u32[]{:S(2)}) collective-permute-start(f32[96,256]{1,0:T(8,128)S(1)} %get-tuple-element.45), channel_id=1, source_target_pairs={{8,16},{16,8},{9,17},{17,9},{10,18},{18,10},{11,19},{19,11},{12,20... | collective-permute-start | bytes 294920 | tf_op jit(solution)/shard_map/ppermute | solution.py:635
  51.6 4.6 %copy-start.5 = (f32[6,6,1024]{2,1,0:T(8,128)S(1)}, f32[6,6,1024]{2,1,0:T(8,128)}, u32[]{:S(2)}) copy-start(f32[6,6,1024]{2,1,0:T(8,128)} %coupling.1) | copy-start | bytes 442372
  60.0 9.8 %copy-start.10 = (f32[2048]{0:T(1024)S(1)}, f32[2048]{0:T(1024)}, u32[]{:S(2)}) copy-start(f32[2048]{0:T(1024)} %param.17) | copy-start | bytes 24580
  60.0 9.8 %collective-permute-start.13 = (f32[96,256]{1,0:T(8,128)S(1)}, f32[96,256]{1,0:T(8,128)S(1)}, u32[]{:S(2)}, u32[]{:S(2)}) collective-permute-start(f32[96,256]{1,0:T(8,128)S(1)} %get-tuple-element.47), channel_id=1, source_target_pairs={{0,8},{16,24},{8,0},{24,16},{1,9},{17,25},{9,1},{25,17},{2,10},{18... | collective-permute-start | bytes 294920 | tf_op jit(solution)/shard_map/ppermute | solution.py:635
  63.4 6.4 %collective-permute-start.14 = (f32[96,256]{1,0:T(8,128)S(1)}, f32[96,256]{1,0:T(8,128)S(1)}, u32[]{:S(2)}, u32[]{:S(2)}) collective-permute-start(f32[96,256]{1,0:T(8,128)S(1)} %get-tuple-element.48), channel_id=1, source_target_pairs={{8,16},{16,8},{9,17},{17,9},{10,18},{18,10},{11,19},{19,11},{12,20... | collective-permute-start | bytes 294920 | tf_op jit(solution)/shard_map/ppermute | solution.py:635
